TPU v7x, 32 devices: a whole 2x2x4 slice. The times are simulated.
32 devices in a mesh: shard: 32 (over z, y, x, core), rep: 1.
Axes of the slice: x: 2, y: 2, z: 4, core: 2. Of those that a mesh axis runs over, the one named last changes fastest.
Arguments:
- queries: bfloat16 [128, 32, 128], P(('rep', 'shard')), may hold values from -6 to 6
- passages: bfloat16 [128, 128, 128], P(('shard', 'rep')), may hold values from -0.52734375 to 0.52734375
- labels: int32 [128, 128], P('shard'), may hold values from 0 to 9
- lengths: int32 [128], P('shard'), may hold values from 16 to 128
- candidates: int32 [128, 64], P(('rep', 'shard')), may hold values from 0 to 127, all different within a row
- feedback: int32 [128, 3], P('rep'), may hold values from 0 to 127
- idf: int32 [128, 10], P('rep'), may hold values from 1 to 16
Outputs:
- first_scores: float32 [128, 64], P(('rep', 'shard'))
- final_scores: float32 [128, 64], P(('rep', 'shard'))
Inputs may be any that keep to these rules, and one draw needn't show every extreme that they name: `candidates`: each row names 64 different passages; every passage is named by some row. `feedback`: ids may repeat within a row.
All inputs are finite; a program needn't handle non-finite values.
Results may differ from a plain program's by a relative error of at most 0.0003.
Values may be sent and summed in bfloat16 or wider, within the bound.
No kernel may reach another device: no remote copies, remote signals or barrier semaphores. Data moves between devices by JAX's collectives and lax.ppermute only.
A program may use at most 64 MiB of HBM per device.

v0:
```python
import jax
import jax.numpy as jnp
from jax import lax
from jax.sharding import PartitionSpec as P


def normalize(pooled):
    factor = lax.rsqrt(jnp.mean(pooled * pooled, axis=-1, keepdims=True) + 1e-06)
    return (pooled * factor).astype(jnp.bfloat16)


def best_match(vectors, passage_bank, penalty):

    def one_passage(operand):
        document, mask_row = operand
        scores = jnp.einsum("rd,td->rt", vectors, document, preferred_element_type=jnp.float32)
        return jnp.max(scores + mask_row[None, :], axis=1)

    return lax.map(one_passage, (passage_bank, penalty))


def local(queries, passages, labels, lengths, candidates, feedback, idf):
    passage_bank = lax.all_gather(passages, "rep", axis=0, tiled=True)
    local_count = passage_bank.shape[0]
    doc_tokens = passage_bank.shape[1]
    features = queries.shape[2]
    query_tokens = queries.shape[1]
    clusters = idf.shape[1]
    positions = jnp.arange(doc_tokens, dtype=jnp.int32)
    in_length = positions[None, :] < lengths[:, None]
    penalty = jnp.where(in_length, 0.0, -1000000000.0).astype(jnp.float32)
    cluster_ids = jnp.arange(clusters, dtype=jnp.int32)
    one_hot = ((labels[:, :, None] == cluster_ids[None, None, :]) & in_length[:, :, None]).astype(
        jnp.bfloat16
    )
    cluster_totals = jnp.einsum(
        "ptc,ptd->pcd", one_hot, passage_bank, preferred_element_type=jnp.float32
    )
    piece = lax.all_gather(queries, "shard", axis=0, tiled=True)
    number = piece.shape[0]
    best_scores = best_match(piece.reshape(number * query_tokens, features), passage_bank, penalty)
    first_pass = jnp.mean(best_scores.reshape(local_count, number, query_tokens), axis=2).T
    all_totals = lax.all_gather(cluster_totals, "shard", axis=0, tiled=True)
    pooled = jnp.sum(jnp.take(all_totals, feedback, axis=0), axis=1)
    expansion = normalize(pooled)
    weights = idf.astype(jnp.float32) / (8.0 * clusters)
    group_size = expansion.shape[0]
    best_expanded = best_match(
        expansion.reshape(group_size * clusters, features), passage_bank, penalty
    )
    expanded_term = jnp.sum(
        best_expanded.reshape(local_count, group_size, clusters) * weights[None, :, :], axis=2
    ).T
    final_pass = first_pass + expanded_term
    dense_first, dense_final = (
        lax.all_to_all(first_pass, "shard", split_axis=0, concat_axis=1, tiled=True),
        lax.all_to_all(final_pass, "shard", split_axis=0, concat_axis=1, tiled=True),
    )
    first_scores = jnp.take_along_axis(dense_first, candidates, axis=1)
    final_scores = jnp.take_along_axis(dense_final, candidates, axis=1)
    return (first_scores, final_scores)


def solution(mesh):
    return jax.shard_map(
        local,
        mesh=mesh,
        in_specs=(
            P(("rep", "shard"), None, None),
            P(("shard", "rep"), None, None),
            P("shard", None),
            P("shard"),
            P(("rep", "shard"), None),
            P("rep", None),
            P("rep", None),
        ),
        out_specs=(P(("rep", "shard"), None), P(("rep", "shard"), None)),
        check_vma=False,
    )
```

profile of v0, /device:TPU:0, one launch (start us, length us, event | category | flops | bytes accessed | tf_op | source)
XLA Modules:
  0.0 107.6 jit_solution(11115818544813967703)
XLA Ops:
  7.2 0.0 all-gather.2.cloned.1.call-start
  7.2 0.7 all-gather.2.cloned.1.call-update
  7.9 0.7 compare_select_fusion.1
  8.6 0.7 compare_and_fusion.1
  9.3 0.7 iota_compare_fusion.1
  10.0 1.1 fusion.9
  11.1 46.4 %all_gather.8 = f32[128,10,128]{2,1,0:T(8,128)S(1)} all-gather(f32[4,10,128]{2,1,0:T(8,128)S(1)} %fusion.9), channel_id=1, replica_groups=mesh['shard'=32,'rep'=1] {'shard'}, dimensions={0}, use_global_device_ids=true | all-gather | bytes 675840 | tf_op jit(solution)/shard_map/all_gather | solution.py:43
  57.5 0.1 copy.19
  57.6 0.2 reshape.90
  57.8 0.1 copy.18
  58.0 2.8 %gather_fusion = f32[384,10,128]{2,1,0:T(8,128)} fusion(f32[128,10,128]{2,1,0:T(8,128)S(1)} %all_gather.8, s32[1024]{0:T(1024)S(1)} %pad_clamp_fusion), kind=kCustom, calls=%fused_computation.2 | custom fusion | bytes 3933696 | tf_op jit(solution)/shard_map/jit(_take)/gather | solution.py:44
  60.8 0.0 copy-start.3
  60.8 0.0 copy-start
  60.8 2.3 %select_reduce_fusion = f32[128,10,128]{2,1,0:T(8,128)S(1)} fusion(f32[128,3,10,128]{3,2,1,0:T(8,128)} %bitcast.51, pred[128,3]{1,0:T(8,128)(4,1)S(1)} %copy.18), kind=kLoop, calls=%fused_computation.15 | loop fusion | flops 819200 | bytes 2621824 | tf_op jit(solution)/shard_map/reduce_sum | solution.py:44
  63.1 0.0 copy-start.2
  63.1 0.1 reduce_sum.40
  63.2 0.3 multiply_reduce_fusion
  63.6 0.1 rsqrt.12
  63.7 0.0 copy-done.3
  63.7 0.1 broadcast_select_fusion.2
  63.8 0.2 multiply_convert_fusion
  64.0 0.0 copy-done
  64.0 1.7 %while.21 = (s32[]{:T(128)}, f32[4,1280]{1,0:T(4,128)S(1)}, bf16[4,128,128]{2,1,0:T(8,128)(2,1)S(1)}, bf16[1280,128]{1,0:T(8,128)(2,1)S(1)}, f32[4,128]{1,0:T(4,128)S(1)}, /*index=5*/s32[]{:T(128)}, s32[]{:T(128)}) while((s32[]{:T(128)}, f32[4,1280]{1,0:T(4,128)S(1)}, bf16[4,128,128]{2,1,0:T(8,128)(2,1)S(1)}, ...), condition=%wide.region_8.10_spmd, body=%wide.region_6.9_spmd.sunk | while | flops 42269440 | bytes 387673 | solution.py:19
  64.0 0.3 fusion.27
  64.3 0.1 dynamic_update_slice.11
  64.5 0.3 fusion.27
  64.8 0.1 dynamic_update_slice.11
  64.9 0.3 fusion.27
  65.2 0.1 dynamic_update_slice.11
  65.3 0.3 fusion.27
  65.6 0.1 dynamic_update_slice.11
  65.7 0.2 reshape.74
  65.9 0.0 copy-done.2
  65.9 0.1 copy.20
  66.1 0.1 multiply_reduce_fusion.1
  66.2 1.5 %all-gather.2.cloned.1.call-done = bf16[128,32,128]{2,1,0:T(8,128)(2,1)} async-done(((bf16[4,32,128]{2,1,0:T(8,128)(2,1)}), bf16[128,32,128]{2,1,0:T(8,128)(2,1)}) %all-gather.2.cloned.1.call-update) | async-done | bytes 1048592 | tf_op jit(solution)/shard_map/all_gather | solution.py:39
  67.7 7.8 %while.20 = (s32[]{:T(128)}, f32[4,4096]{1,0:T(4,128)S(1)}, bf16[4,128,128]{2,1,0:T(8,128)(2,1)S(1)}, bf16[4096,128]{1,0:T(8,128)(2,1)}, f32[4,128]{1,0:T(4,128)S(1)}, /*index=5*/s32[]{:T(128)}, s32[]{:T(128)}) while((s32[]{:T(128)}, f32[4,4096]{1,0:T(4,128)S(1)}, bf16[4,128,128]{2,1,0:T(8,128)(2,1)S(1)}, bf16[4096,128]{1,0:T(8,128)(2,1)}, ...), condition=%wide.region_2.3_spmd, body=%wide.region_0.2_spmd.sunk | while | flops 135262208 | bytes 1132121 | solution.py:19
  67.7 1.7 %fusion.24 = f32[4096]{0:T(1024)S(1)} fusion(bf16[4096,128]{1,0:T(8,128)(2,1)} %get-tuple-element.181, f32[128]{0:T(128)S(1)} %dynamic-slice_bitcast_fusion.4, bf16[4,128,128]{2,1,0:T(8,128)(2,1)S(1)} %get-tuple-element.180, s32[]{:T(128)} %get-tuple-element.171), kind=kOutput, calls=%fused_computation.4.clone.1 | convolution fusion | flops 135262208 | bytes 1098244 | tf_op jit(solution)/shard_map/while/body/eval_jaxpr/rd,td->rt/dot_general | solution.py:16
  69.4 0.2 dynamic_update_slice.10
  69.7 1.7 %fusion.24 = f32[4096]{0:T(1024)S(1)} fusion(bf16[4096,128]{1,0:T(8,128)(2,1)} %get-tuple-element.181, f32[128]{0:T(128)S(1)} %dynamic-slice_bitcast_fusion.4, bf16[4,128,128]{2,1,0:T(8,128)(2,1)S(1)} %get-tuple-element.180, s32[]{:T(128)} %get-tuple-element.171), kind=kOutput, calls=%fused_computation.4.clone.1 | convolution fusion | flops 135262208 | bytes 1098244 | tf_op jit(solution)/shard_map/while/body/eval_jaxpr/rd,td->rt/dot_general | solution.py:16
  71.3 0.2 dynamic_update_slice.10
  71.6 1.7 %fusion.24 = f32[4096]{0:T(1024)S(1)} fusion(bf16[4096,128]{1,0:T(8,128)(2,1)} %get-tuple-element.181, f32[128]{0:T(128)S(1)} %dynamic-slice_bitcast_fusion.4, bf16[4,128,128]{2,1,0:T(8,128)(2,1)S(1)} %get-tuple-element.180, s32[]{:T(128)} %get-tuple-element.171), kind=kOutput, calls=%fused_computation.4.clone.1 | convolution fusion | flops 135262208 | bytes 1098244 | tf_op jit(solution)/shard_map/while/body/eval_jaxpr/rd,td->rt/dot_general | solution.py:16
  73.3 0.2 dynamic_update_slice.10
  73.6 1.7 %fusion.24 = f32[4096]{0:T(1024)S(1)} fusion(bf16[4096,128]{1,0:T(8,128)(2,1)} %get-tuple-element.181, f32[128]{0:T(128)S(1)} %dynamic-slice_bitcast_fusion.4, bf16[4,128,128]{2,1,0:T(8,128)(2,1)S(1)} %get-tuple-element.180, s32[]{:T(128)} %get-tuple-element.171), kind=kOutput, calls=%fused_computation.4.clone.1 | convolution fusion | flops 135262208 | bytes 1098244 | tf_op jit(solution)/shard_map/while/body/eval_jaxpr/rd,td->rt/dot_general | solution.py:16
  75.3 0.2 dynamic_update_slice.10
  75.5 0.1 reshape.73
  75.7 0.1 reduce_sum.38
  75.8 0.1 all_to_all.32
  75.9 0.7 copy.21
  76.6 3.6 %all-to-all-start.1 = ((f32[32,4,4]{1,2,0:T(4,128)}), f32[32,4,4]{1,2,0:T(4,128)S(1)}, u32[]{:S(2)}, u32[]{:S(2)}) async-start(f32[32,4,4]{1,2,0:T(4,128)} %copy.21), calls=%async_computation.1 | async-start | bytes 131072 | tf_op jit(solution)/shard_map/all_to_all | solution.py:57
  80.2 0.1 all_to_all.28
  80.3 0.7 copy.16
  81.0 6.6 %all-to-all-done.1 = f32[32,4,4]{1,2,0:T(4,128)S(1)} async-done(((f32[32,4,4]{1,2,0:T(4,128)}), f32[32,4,4]{1,2,0:T(4,128)S(1)}, u32[]{:S(2)}, u32[]{:S(2)}) %all-to-all-start.1) | async-done | bytes 2080 | tf_op jit(solution)/shard_map/all_to_all | solution.py:57
  87.6 2.5 %all-to-all-start = ((f32[32,4,4]{1,2,0:T(4,128)}), f32[32,4,4]{1,2,0:T(4,128)S(1)}, u32[]{:S(2)}, u32[]{:S(2)}) async-start(f32[32,4,4]{1,2,0:T(4,128)} %copy.16), calls=%async_computation | async-start | bytes 131072 | tf_op jit(solution)/shard_map/all_to_all | solution.py:56
  90.1 0.0 copy-done.1
  90.2 0.1 reshape.109
  90.3 0.1 copy.24
  90.3 2.4 %gather_fusion.2 = f32[256]{0:T(256)S(1)} fusion(f32[4,128]{1,0:T(4,128)S(1)} %copy.24, s32[256]{0:T(256)S(1)} %reshape.109), kind=kCustom, calls=%fused_computation.1.clone | custom fusion | bytes 4096 | tf_op jit(solution)/shard_map/jit(take_along_axis)/gather | solution.py:60
  92.7 0.1 reshape.117
  92.8 4.7 %all-to-all-done = f32[32,4,4]{1,2,0:T(4,128)S(1)} async-done(((f32[32,4,4]{1,2,0:T(4,128)}), f32[32,4,4]{1,2,0:T(4,128)S(1)}, u32[]{:S(2)}, u32[]{:S(2)}) %all-to-all-start) | async-done | bytes 2080 | tf_op jit(solution)/shard_map/all_to_all | solution.py:56
  97.6 0.1 copy.23
  97.6 2.4 %gather_fusion.1 = f32[256]{0:T(256)S(1)} fusion(f32[4,128]{1,0:T(4,128)S(1)} %copy.23, s32[256]{0:T(256)S(1)} %reshape.109), kind=kCustom, calls=%fused_computation.clone | custom fusion | bytes 4096 | tf_op jit(solution)/shard_map/jit(take_along_axis)/gather | solution.py:59
  100.0 0.1 reshape.112
  100.1 0.6 broadcast_select_fusion
  (21 shorter events, 0.1 us)
Async XLA Ops:
  7.2 60.5 %all-gather.2.cloned.1.call-start = ((), (), s32[]{:S(2)}) async-start(), calls=%async_computation.2 | async-start | bytes 1081344 | tf_op jit(solution)/shard_map/all_gather | solution.py:39
  60.8 2.9 %copy-start.3 = (s32[4]{0:T(128)S(1)}, s32[4]{0:T(128)}, u32[]{:S(2)}) copy-start(s32[4]{0:T(128)} %param.16) | copy-start | bytes 52
  60.8 3.3 %copy-start = (bf16[4,128,128]{2,1,0:T(8,128)(2,1)S(1)}, bf16[4,128,128]{2,1,0:T(8,128)(2,1)}, u32[]{:S(2)}) copy-start(bf16[4,128,128]{2,1,0:T(8,128)(2,1)} %param.14) | copy-start | bytes 393220
  63.1 2.9 %copy-start.2 = (s32[128,10]{0,1:T(8,128)S(1)}, s32[128,10]{0,1:T(8,128)}, u32[]{:S(2)}) copy-start(s32[128,10]{0,1:T(8,128)} %param.19) | copy-start | bytes 15364
  67.7 22.5 %copy-start.1 = (s32[4,64]{1,0:T(4,128)S(1)}, s32[4,64]{1,0:T(4,128)}, u32[]{:S(2)}) copy-start(s32[4,64]{1,0:T(4,128)} %param.17) | copy-start | bytes 3076
  76.6 11.0 %all-to-all-start.1 = ((f32[32,4,4]{1,2,0:T(4,128)}), f32[32,4,4]{1,2,0:T(4,128)S(1)}, u32[]{:S(2)}, u32[]{:S(2)}) async-start(f32[32,4,4]{1,2,0:T(4,128)} %copy.21), calls=%async_computation.1 | async-start | bytes 131072 | tf_op jit(solution)/shard_map/all_to_all | solution.py:57
  87.6 10.0 %all-to-all-start = ((f32[32,4,4]{1,2,0:T(4,128)}), f32[32,4,4]{1,2,0:T(4,128)S(1)}, u32[]{:S(2)}, u32[]{:S(2)}) async-start(f32[32,4,4]{1,2,0:T(4,128)} %copy.16), calls=%async_computation | async-start | bytes 131072 | tf_op jit(solution)/shard_map/all_to_all | solution.py:56
Sparse Core Ops, SparseCore 0:
  10.9 56.7 all-gather.1
where the time goes:
time: 108 us
  blocking collectives  46.4 us (43%)
  between operations  14.2 us (13%)
  waiting for transfers between devices  13.5 us (12%)
  local copies, waits for them, and re-layouts  12.1 us (11%)
  matrix products  8.83 us (8%)
  starting transfers between devices  6.14 us (6%)
  other arithmetic  5.98 us (6%)
    all_gather x1, blocking collectives, local(): all_totals = lax.all_gather(cluster_totals, 'shard', axis=0, tiled=True)  46.4 us
    dot_general x8, matrix products, one_passage(): jnp.einsum('rd,td->rt', vectors, document, preferred_element_type=jnp.flo...  7.77 us
    all_to_all x1, waiting for transfers between devices, local(): lax.all_to_all(final_pass, 'shard', split_axis=0, concat_axis=1, tiled=True)  6.62 us
    all_to_all x1, waiting for transfers between devices, local(): lax.all_to_all(first_pass, 'shard', split_axis=0, concat_axis=1, tiled=True)  4.74 us
    all_to_all x1, starting transfers between devices, local(): lax.all_to_all(final_pass, 'shard', split_axis=0, concat_axis=1, tiled=True)  3.56 us
    gather x1, local copies, waits for them, and re-layouts, local(): pooled = jnp.sum(jnp.take(all_totals, feedback, axis=0), axis=1)  2.79 us
    gather x3, local copies, waits for them, and re-layouts, local(): first_scores = jnp.take_along_axis(dense_first, candidates, axis=1)  2.58 us
    all_to_all x1, starting transfers between devices, local(): lax.all_to_all(first_pass, 'shard', split_axis=0, concat_axis=1, tiled=True)  2.54 us
  transfers between devices with their start and end apart: 3, of which 3 were waited for; matrix products, arithmetic and copies ran while one was open for 14% of the time, Pallas kernels for 0%

commit v1 on v0

v1 whole, which is shorter than its diff:
```python
import functools

import jax
import jax.numpy as jnp
import numpy as np
from jax import lax
from jax.experimental import pallas as pl
from jax.experimental.pallas import tpu as pltpu
from jax.sharding import PartitionSpec as P

BANK_BITS = 3
HIGHEST = lax.Precision.HIGHEST
BF16, F32, I32 = jnp.bfloat16, jnp.float32, jnp.int32
VMEM_BYTES = 48 * 1024 * 1024


def iota(shape, dim):
    return lax.broadcasted_iota(I32, shape, dim)


def rows_dot(a, b, precision=None):
    return lax.dot_general(a, b, (((1,), (1,)), ((), ())), precision=precision, preferred_element_type=F32)


def prepare_kernel(clusters, lengths_ref, queries_ref, passages_ref, labels_ref, payload_ref, masked_ref):
    count, tokens, features = passages_ref.shape
    query_rows = queries_ref.shape[0]
    payload_ref[:query_rows, :] = queries_ref[...]
    totals = jnp.zeros((clusters * count, features), F32)
    for p in range(count):
        length = lengths_ref[p]
        document = passages_ref[p]
        wide = document.astype(F32)
        kept = jnp.where(iota((tokens, features), 0) < length, wide, wide[0:1, :])
        masked_ref[p * tokens : (p + 1) * tokens, :] = kept.astype(BF16)
        target = jnp.where(iota((1, tokens), 1) < length, labels_ref[p : p + 1, :] * count + p, -1)
        chosen = (iota((clusters * count, tokens), 0) == target).astype(F32).astype(BF16)
        totals = totals + jnp.dot(chosen, document, preferred_element_type=F32)
    high = totals.astype(BF16).astype(F32)
    payload_ref[query_rows:, :] = jnp.concatenate([high, totals - high], axis=0).astype(BF16)


def best_rows(document_refs, vectors, count):
    best = []
    for document_ref in document_refs:
        scores = rows_dot(document_ref[...], vectors)
        tokens = scores.shape[0] // count
        best += [jnp.max(scores[p * tokens : (p + 1) * tokens, :], axis=0, keepdims=True) for p in range(count)]
    return jnp.concatenate(best, axis=0)


def plain_kernel(count, query_tokens, query_rows, gathered_ref, *refs):
    document_refs, plain_ref = refs[:-1], refs[-1]
    slots = gathered_ref.shape[0]
    vectors = jnp.concatenate([gathered_ref[s, :query_rows, :] for s in range(slots)], axis=0)
    best = best_rows(document_refs, vectors, count)
    number = plain_ref.shape[0]
    shape = (number, vectors.shape[0])
    first = iota(shape, 0) * query_tokens
    mean = jnp.where((iota(shape, 1) >= first) & (iota(shape, 1) < first + query_tokens), 1.0 / query_tokens, 0.0)
    plain_ref[...] = rows_dot(mean.astype(F32), best, HIGHEST)


def expand_kernel(
    count, near_ref, far_ref, places_ref, feedback_ref, idf_ref, plain_ref, *refs, outputs, step
):
    document_refs, out_refs, fb_ref, weight_ref = refs[: -outputs - 2], refs[-outputs - 2 : -2], refs[-2], refs[-1]
    me = lax.axis_index("shard")
    number, clusters = weight_ref.shape
    each = number // outputs
    for s in range(outputs):
        base = (me ^ (s * step)) * each
        fb_ref[s * each : (s + 1) * each, :] = feedback_ref[pl.ds(base, each), :]
        weight_ref[s * each : (s + 1) * each, :] = idf_ref[pl.ds(base, each), :].astype(F32) / (8.0 * clusters)
    wanted = fb_ref[...] ^ (me * count)
    pooled = jnp.zeros((clusters * number, near_ref.shape[1]), F32)
    for half, totals_ref in enumerate((near_ref, far_ref)):
        place = places_ref[2 * half : 2 * half + 1, :]
        kind = places_ref[2 * half + 1 : 2 * half + 2, :]
        times = jnp.zeros((number, place.shape[1]), F32)
        for k in range(wanted.shape[1]):
            times = times + jnp.where(wanted[:, k : k + 1] == place, 1.0, 0.0)
        picks = jnp.concatenate([jnp.where(kind == c, times, 0.0) for c in range(clusters)], axis=0)
        pooled = pooled + jnp.dot(picks.astype(BF16), totals_ref[...], preferred_element_type=F32)
    factor = lax.rsqrt(jnp.mean(pooled * pooled, axis=-1, keepdims=True) + 1e-06)
    expansion = (pooled * factor).astype(BF16)
    best = best_rows(document_refs, expansion, count)
    shape = (number, clusters * number)
    spread = jnp.zeros(shape, F32)
    for c in range(clusters):
        spread = jnp.where(iota(shape, 1) == iota(shape, 0) + c * number, weight_ref[:, c : c + 1], spread)
    added = rows_dot(spread, best, HIGHEST)
    plain = plain_ref[...]
    both = jnp.concatenate([plain, plain + added], axis=1)
    for s in range(outputs):
        out_refs[s][...] = both[s * each : (s + 1) * each, :]


def select_kernel(count, candidates_ref, *refs):
    block_refs, first_ref, final_ref = refs[:-2], refs[-2], refs[-1]
    me = lax.axis_index("shard")
    given, wanted = candidates_ref.shape
    width = block_refs[0].shape[1] // 2
    place = candidates_ref[...] ^ (me * count)
    rows, lanes = -(-given // 8) * 8, -(-wanted // 128) * 128
    place = jnp.pad(place, ((0, rows - given), (0, lanes - wanted)))
    for side, out_ref in enumerate((first_ref, final_ref)):
        dense = jnp.concatenate([r[:, side * width : (side + 1) * width] for r in block_refs], axis=1)
        dense = jnp.pad(dense, ((0, rows - given), (0, 0)))
        pieces = []
        for at in range(0, place.shape[1], 128):
            here = place[:, at : at + 128]
            piece = jnp.zeros((rows, 128), F32)
            for group in range(dense.shape[1] // 128):
                found = jnp.take_along_axis(
                    dense[:, group * 128 : (group + 1) * 128], here & 127, axis=1, mode="promise_in_bounds"
                )
                piece = jnp.where((here >> 7) == group, found, piece)
            pieces.append(piece)
        out_ref[...] = jnp.concatenate(pieces, axis=1)[:given, :wanted]


def call(kernel, out_shape, *operands, scratch=(), specs=None, cost=None):
    return pl.pallas_call(
        kernel,
        out_shape=out_shape,
        in_specs=specs or [pl.BlockSpec(memory_space=pltpu.VMEM)] * len(operands),
        scratch_shapes=scratch,
        compiler_params=pltpu.CompilerParams(vmem_limit_bytes=VMEM_BYTES),
        cost_estimate=cost,
    )(*operands)


def local(devices, queries, passages, labels, lengths, candidates, feedback, idf):
    passages = lax.all_gather(passages, "rep", axis=0, tiled=True)
    count, tokens, features = passages.shape
    each, query_tokens, _ = queries.shape
    clusters = idf.shape[1]
    bank = min(1 << BANK_BITS, devices)
    columns = devices // bank
    number = columns * each
    query_rows = each * query_tokens
    total_rows = 2 * clusters * count
    sds = jax.ShapeDtypeStruct

    def swap(x, m):
        return lax.ppermute(x, "shard", [(i, i ^ m) for i in range(devices)])

    vmem, smem = pl.BlockSpec(memory_space=pltpu.VMEM), pl.BlockSpec(memory_space=pltpu.SMEM)
    payload, masked = call(
        functools.partial(prepare_kernel, clusters),
        (sds((query_rows + total_rows, features), BF16), sds((count * tokens, features), BF16)),
        lengths,
        queries.reshape(query_rows, features),
        passages,
        labels,
        specs=[smem, vmem, vmem, vmem],
    )
    gathered = payload[None]
    for bit in range(columns.bit_length() - 1):
        gathered = jnp.concatenate([gathered, swap(gathered, bank << bit)], axis=0)
    documents = {0: masked}
    for m in range(2, bank, 2):
        documents[m] = swap(masked, m)
    for m in range(0, bank, 2):
        documents[m + 1] = swap(documents[m], 1)
    documents = [documents[m] for m in range(bank)]
    own = gathered[:, query_rows:, :].reshape(columns * total_rows, features)
    near = jnp.concatenate([own] + [swap(own, m) for m in range(2, bank, 2)], axis=0)
    far = swap(near, 1)
    plain = call(
        functools.partial(plain_kernel, count, query_tokens, query_rows),
        sds((number, bank * count), F32),
        gathered,
        *documents,
    )
    row = np.arange(total_rows) % (clusters * count)
    places = []
    for half in range(2):
        m = np.arange(half, bank, 2)[:, None, None]
        s = np.arange(columns)[None, :, None] * bank
        place = (m + s) * count + (row % count)[None, None, :]
        kind = np.broadcast_to((row // count)[None, None, :], place.shape)
        places += [place.reshape(-1), kind.reshape(-1)]
    blocks = call(
        functools.partial(expand_kernel, count, outputs=columns, step=bank),
        [sds((each, 2 * bank * count), F32)] * columns,
        near,
        far,
        jnp.asarray(np.stack(places).astype(np.int32)),
        feedback,
        idf,
        plain,
        *documents,
        scratch=[pltpu.VMEM((number, feedback.shape[1]), I32), pltpu.VMEM((number, clusters), F32)],
    )
    blocks = [blocks[0]] + [swap(blocks[s], s * bank) for s in range(1, columns)]
    return call(
        functools.partial(select_kernel, count),
        (sds(candidates.shape, F32), sds(candidates.shape, F32)),
        candidates,
        *blocks,
    )


def solution(mesh):
    return jax.shard_map(
        functools.partial(local, mesh.shape["shard"]),
        mesh=mesh,
        in_specs=(
            P(("rep", "shard"), None, None),
            P(("shard", "rep"), None, None),
            P("shard", None),
            P("shard"),
            P(("rep", "shard"), None),
            P("rep", None),
            P("rep", None),
        ),
        out_specs=(P(("rep", "shard"), None), P(("rep", "shard"), None)),
        check_vma=False,
    )
```

time: 108 us -> 48.9 us (0.45)
  blocking collectives: 46.4 us -> 0 us
  between operations: 14.2 us -> 0.74 us
  starting transfers between devices: 6.14 us -> 19 us
  local copies, waits for them, and re-layouts: 12.1 us -> 3.24 us
  matrix products: 8.83 us -> 0 us
  waiting for transfers between devices: 13.5 us -> 21.3 us
  other arithmetic: 5.98 us -> 0.06 us
  Pallas kernels: 0 us -> 4.31 us
    all_gather x1 -> x0, blocking collectives: 46.4 us -> none  [local(): all_totals = lax.all_gather(cluster_totals, 'shard', axis=0, tiled=True)]
    ppermute x0 -> x16, waiting for transfers between devices: none -> 21.3 us  [swap(): return lax.ppermute(x, 'shard', [(i, i ^ m) for i in range(devices)])]
    ppermute x0 -> x16, starting transfers between devices: none -> 19 us  [swap(): return lax.ppermute(x, 'shard', [(i, i ^ m) for i in range(devices)])]
    all_to_all x2 -> x0, waiting for transfers between devices: 11.4 us -> none  [the longest x1 6.62 us: local(): lax.all_to_all(final_pass, 'shard', split_axis=0, concat_axis=1, tiled=True)]
    dot_general x9 -> x0, matrix products: 8.83 us -> none  [the longest x8 7.77 us: one_passage(): jnp.einsum('rd,td->rt', vectors, document, preferred_element_type=jnp.flo...]
    gather x6 -> x0, local copies, waits for them, and re-layouts: 7.87 us -> none  [the longest x1 2.79 us: local(): pooled = jnp.sum(jnp.take(all_totals, feedback, axis=0), axis=1)]
    all_to_all x2 -> x0, starting transfers between devices: 6.11 us -> none  [the longest x1 3.56 us: local(): lax.all_to_all(final_pass, 'shard', split_axis=0, concat_axis=1, tiled=True)]
    pallas_call x0 -> x4, Pallas kernels: none -> 4.31 us  [call(): pl.pallas_call(kernel, out_shape=out_shape, in_specs=specs or [pl.BlockSp...]
  transfers between devices with their start and end apart: 3 -> 16, of which waited for: 3 -> 12; matrix products, arithmetic and copies ran while one was open for 14% -> 0% of each run, Pallas kernels for 0% -> 3%
where the time goes in v1:
time: 48.9 us; the launch traced here: 48.7 us
  waiting for transfers between devices  21.3 us (44%)
  starting transfers between devices  19 us (39%)
  Pallas kernels  4.31 us (9%)
  local copies, waits for them, and re-layouts  3.24 us (7%)
  between operations  0.74 us (2%)
    ppermute x16, waiting for transfers between devices, swap(): return lax.ppermute(x, 'shard', [(i, i ^ m) for i in range(devices)])  21.3 us
    ppermute x16, starting transfers between devices, swap(): return lax.ppermute(x, 'shard', [(i, i ^ m) for i in range(devices)])  19 us
    pallas_call x4, Pallas kernels, call(): pl.pallas_call(kernel, out_shape=out_shape, in_specs=specs or [pl.BlockSp...  4.31 us
    unnamed x18, local copies, waits for them, and re-layouts  3.23 us
  transfers between devices with their start and end apart: 16, of which 12 were waited for; matrix products, arithmetic and copies ran while one was open for 0% of the time, Pallas kernels for 3%

profile of v1, /device:TPU:0, one launch (start us, length us, event | category | flops | bytes accessed | tf_op | source)
XLA Modules:
  0.0 48.7 jit_solution(8031858819566587374)
XLA Ops:
  0.6 0.0 copy-start.5
  0.6 0.6 %copy-done.5 = s32[4]{0:T(128)S(1)} copy-done((s32[4]{0:T(128)S(1)}, s32[4]{0:T(128)}, u32[]{:S(2)}) %copy-start.5) | copy-done | bytes 40
  1.3 0.0 copy-start
  1.3 0.9 %copy-done = bf16[4,128,128]{2,1,0:T(8,128)(2,1)S(1)} copy-done((bf16[4,128,128]{2,1,0:T(8,128)(2,1)S(1)}, bf16[4,128,128]{2,1,0:T(8,128)(2,1)}, u32[]{:S(2)}) %copy-start) | copy-done | bytes 131096
  2.2 0.0 copy-start.1
  2.2 0.8 %copy-done.1 = bf16[4,32,128]{2,1,0:T(8,128)(2,1)S(1)} copy-done((bf16[4,32,128]{2,1,0:T(8,128)(2,1)S(1)}, bf16[4,32,128]{2,1,0:T(8,128)(2,1)}, u32[]{:S(2)}) %copy-start.1) | copy-done | bytes 32792
  3.0 0.0 copy-start.4
  3.0 0.7 %copy-done.4 = s32[4,128]{1,0:T(4,128)S(1)} copy-done((s32[4,128]{1,0:T(4,128)S(1)}, s32[4,128]{1,0:T(4,128)}, u32[]{:S(2)}) %copy-start.4) | copy-done | bytes 2072
  3.6 0.7 %shard_map.95 = (bf16[208,128]{1,0:T(8,128)(2,1)S(1)}, bf16[512,128]{1,0:T(8,128)(2,1)S(1)}) custom-call(s32[4]{0:T(128)S(1)} %copy-done.5, bf16[128,128]{1,0:T(8,128)(2,1)S(1)} %bitcast.6, bf16[4,128,128]{2,1,0:T(8,128)(2,1)S(1)} %copy-done, s32[4,128]{1,0:T(4,128)S(1)} %copy-done.4), custom_call_target="tpu_custom_call" | custom-call | tf_op jit(solution)/shard_map/pallas_call | solution.py:124
  4.4 3.1 %collective-permute-start = (bf16[1,208,128]{2,1,0:T(8,128)(2,1)S(1)}, bf16[1,208,128]{2,1,0:T(8,128)(2,1)S(1)}, u32[]{:S(2)}, u32[]{:S(2)}) collective-permute-start(bf16[1,208,128]{2,1,0:T(8,128)(2,1)S(1)} %bitcast.3), channel_id=1, source_target_pairs={{0,8},{1,9},{2,10},{3,11},{4,12},{5,13},{6,14},{7,15},{8,0},{9,1},... | collective-permute-start | bytes 159752 | tf_op jit(solution)/shard_map/ppermute | solution.py:147
  7.4 2.1 %collective-permute-done = bf16[1,208,128]{2,1,0:T(8,128)(2,1)S(1)} collective-permute-done((bf16[1,208,128]{2,1,0:T(8,128)(2,1)S(1)}, bf16[1,208,128]{2,1,0:T(8,128)(2,1)S(1)}, u32[]{:S(2)}, u32[]{:S(2)}) %collective-permute-start) | collective-permute-done | bytes 53280 | tf_op jit(solution)/shard_map/ppermute | solution.py:147
  9.6 3.1 %collective-permute-start.1 = (bf16[2,208,128]{2,1,0:T(8,128)(2,1)S(1)}, bf16[2,208,128]{2,1,0:T(8,128)(2,1)S(1)}, u32[]{:S(2)}, u32[]{:S(2)}) collective-permute-start(bf16[2,208,128]{2,1,0:T(8,128)(2,1)S(1)} %pad_maximum_fusion.2), channel_id=1, source_target_pairs={{0,16},{1,17},{2,18},{3,19},{4,20},{5,21},{6,22},{7,23},{8,24},{9,... | collective-permute-start | bytes 319496 | tf_op jit(solution)/shard_map/ppermute | solution.py:147
  12.7 3.0 %collective-permute-done.1 = bf16[2,208,128]{2,1,0:T(8,128)(2,1)S(1)} collective-permute-done((bf16[2,208,128]{2,1,0:T(8,128)(2,1)S(1)}, bf16[2,208,128]{2,1,0:T(8,128)(2,1)S(1)}, u32[]{:S(2)}, u32[]{:S(2)}) %collective-permute-start.1) | collective-permute-done | bytes 106528 | tf_op jit(solution)/shard_map/ppermute | solution.py:147
  15.7 3.7 %collective-permute-start.4 = (bf16[320,128]{1,0:T(8,128)(2,1)S(1)}, bf16[320,128]{1,0:T(8,128)(2,1)S(1)}, u32[]{:S(2)}, u32[]{:S(2)}) collective-permute-start(bf16[320,128]{1,0:T(8,128)(2,1)S(1)} %bitcast.7), channel_id=1, source_target_pairs={{0,6},{1,7},{2,4},{3,5},{4,2},{5,3},{6,0},{7,1},{8,14},{9,15},{10,... | collective-permute-start | bytes 245768 | tf_op jit(solution)/shard_map/ppermute | solution.py:147
  19.4 0.5 %collective-permute-start.3 = (bf16[320,128]{1,0:T(8,128)(2,1)S(1)}, bf16[320,128]{1,0:T(8,128)(2,1)S(1)}, u32[]{:S(2)}, u32[]{:S(2)}) collective-permute-start(bf16[320,128]{1,0:T(8,128)(2,1)S(1)} %bitcast.8), channel_id=1, source_target_pairs={{0,4},{1,5},{2,6},{3,7},{4,0},{5,1},{6,2},{7,3},{8,12},{9,13},{10,... | collective-permute-start | bytes 245768 | tf_op jit(solution)/shard_map/ppermute | solution.py:147
  19.9 0.1 collective-permute-start.2
  20.0 2.1 %collective-permute-done.4 = bf16[320,128]{1,0:T(8,128)(2,1)S(1)} collective-permute-done((bf16[320,128]{1,0:T(8,128)(2,1)S(1)}, bf16[320,128]{1,0:T(8,128)(2,1)S(1)}, u32[]{:S(2)}, u32[]{:S(2)}) %collective-permute-start.4) | collective-permute-done | bytes 81952 | tf_op jit(solution)/shard_map/ppermute | solution.py:147
  22.2 1.7 %collective-permute-done.3 = bf16[320,128]{1,0:T(8,128)(2,1)S(1)} collective-permute-done((bf16[320,128]{1,0:T(8,128)(2,1)S(1)}, bf16[320,128]{1,0:T(8,128)(2,1)S(1)}, u32[]{:S(2)}, u32[]{:S(2)}) %collective-permute-start.3) | collective-permute-done | bytes 81952 | tf_op jit(solution)/shard_map/ppermute | solution.py:147
  23.8 0.5 %collective-permute-done.2 = bf16[320,128]{1,0:T(8,128)(2,1)S(1)} collective-permute-done((bf16[320,128]{1,0:T(8,128)(2,1)S(1)}, bf16[320,128]{1,0:T(8,128)(2,1)S(1)}, u32[]{:S(2)}, u32[]{:S(2)}) %collective-permute-start.2) | collective-permute-done | bytes 81952 | tf_op jit(solution)/shard_map/ppermute | solution.py:147
  24.3 0.0 copy-start.7
  24.4 0.1 collective-permute-start.5
  24.4 0.0 copy-start.6
  24.4 1.6 %collective-permute-start.11 = (bf16[512,128]{1,0:T(8,128)(2,1)S(1)}, bf16[512,128]{1,0:T(8,128)(2,1)S(1)}, u32[]{:S(2)}, u32[]{:S(2)}) collective-permute-start(bf16[512,128]{1,0:T(8,128)(2,1)S(1)} %get-tuple-element.9.refs_0_), channel_id=1, source_target_pairs={{0,6},{1,7},{2,4},{3,5},{4,2},{5,3},{6,0},{7,1},{8,14},{9,15},{10,... | collective-permute-start | bytes 393224 | tf_op jit(solution)/shard_map/ppermute | solution.py:147
  26.0 0.3 collective-permute-start.9
  26.3 1.7 %collective-permute-start.7 = (bf16[512,128]{1,0:T(8,128)(2,1)S(1)}, bf16[512,128]{1,0:T(8,128)(2,1)S(1)}, u32[]{:S(2)}, u32[]{:S(2)}) collective-permute-start(bf16[512,128]{1,0:T(8,128)(2,1)S(1)} %get-tuple-element.9.refs_0_), channel_id=1, source_target_pairs={{0,2},{1,3},{2,0},{3,1},{4,6},{5,7},{6,4},{7,5},{8,10},{9,11},{10,... | collective-permute-start | bytes 393224 | tf_op jit(solution)/shard_map/ppermute | solution.py:147
  28.0 0.0 collective-permute-start.6
  28.0 3.8 %collective-permute-done.11.refs_6_ = bf16[512,128]{1,0:T(8,128)(2,1)S(1)} collective-permute-done((bf16[512,128]{1,0:T(8,128)(2,1)S(1)}, bf16[512,128]{1,0:T(8,128)(2,1)S(1)}, u32[]{:S(2)}, u32[]{:S(2)}) %collective-permute-start.11) | collective-permute-done | bytes 131104 | tf_op jit(solution)/shard_map/ppermute | solution.py:147
  31.8 0.0 collective-permute-start.12
  31.8 2.3 %collective-permute-done.9.refs_4_ = bf16[512,128]{1,0:T(8,128)(2,1)S(1)} collective-permute-done((bf16[512,128]{1,0:T(8,128)(2,1)S(1)}, bf16[512,128]{1,0:T(8,128)(2,1)S(1)}, u32[]{:S(2)}, u32[]{:S(2)}) %collective-permute-start.9) | collective-permute-done | bytes 131104 | tf_op jit(solution)/shard_map/ppermute | solution.py:147
  34.1 0.0 collective-permute-start.10
  34.1 0.1 collective-permute-done.7.refs_2_
  34.2 0.4 collective-permute-start.8
  34.6 0.0 copy-done.7
  34.6 0.1 copy.10.feedback_ref
  34.7 0.0 copy-done.6
  34.7 0.1 copy.11.idf_ref
  34.8 0.0 copy-start.2
  34.8 0.0 collective-permute-done.6.refs_1_
  34.8 0.0 collective-permute-done.12.refs_7_
  34.8 0.6 %collective-permute-done.10.refs_5_ = bf16[512,128]{1,0:T(8,128)(2,1)S(1)} collective-permute-done((bf16[512,128]{1,0:T(8,128)(2,1)S(1)}, bf16[512,128]{1,0:T(8,128)(2,1)S(1)}, u32[]{:S(2)}, u32[]{:S(2)}) %collective-permute-start.10) | collective-permute-done | bytes 131104 | tf_op jit(solution)/shard_map/ppermute | solution.py:147
  35.4 0.2 collective-permute-done.8.refs_3_
  35.6 1.4 %shard_map.96.plain_ref = f32[16,32]{1,0:T(8,128)S(1)} custom-call(bf16[4,208,128]{2,1,0:T(8,128)(2,1)S(1)} %pad_maximum_fusion.1.gathered_ref, bf16[512,128]{1,0:T(8,128)(2,1)S(1)} %get-tuple-element.9.refs_0_, bf16[512,128]{1,0:T(8,128)(2,1)S(1)} %collective-permute-done.6.refs_1_, bf16[512,128]{1,0:T(8,128)(2,1)S(1)} %collective-permute-done.7.refs_2_, ...), custom_call_target="tpu_custom_call" | custom-call | tf_op jit(solution)/shard_map/pallas_call | solution.py:124
  37.0 0.0 collective-permute-done.5.far_ref
  37.0 0.0 copy-done.2
  37.0 1.5 %shard_map.97 = (f32[4,64]{1,0:T(4,128)S(1)}, f32[4,64]{1,0:T(4,128)S(1)}, f32[4,64]{1,0:T(4,128)S(1)}, f32[4,64]{1,0:T(4,128)S(1)}) custom-call(bf16[1280,128]{1,0:T(8,128)(2,1)S(1)} %pad_maximum_fusion.near_ref, bf16[1280,128]{1,0:T(8,128)(2,1)S(1)} %collective-permute-done.5.far_ref, s32[4,1280]{1,0:T(4,128)S(1)} %copy-done.2, ...), custom_call_target="tpu_custom_call" | custom-call | tf_op jit(solution)/shard_map/pallas_call | solution.py:124
  38.5 0.7 %collective-permute-start.13 = (f32[4,64]{1,0:T(4,128)S(1)}, f32[4,64]{1,0:T(4,128)S(1)}, u32[]{:S(2)}, u32[]{:S(2)}) collective-permute-start(f32[4,64]{1,0:T(4,128)S(1)} %get-tuple-element.11), channel_id=1, source_target_pairs={{0,8},{1,9},{2,10},{3,11},{4,12},{5,13},{6,14},{7,15},{8,0},{9,1},... | collective-permute-start | bytes 3080 | tf_op jit(solution)/shard_map/ppermute | solution.py:147
  39.2 0.0 copy-start.3
  39.2 3.4 %collective-permute-start.14 = (f32[4,64]{1,0:T(4,128)S(1)}, f32[4,64]{1,0:T(4,128)S(1)}, u32[]{:S(2)}, u32[]{:S(2)}) collective-permute-start(f32[4,64]{1,0:T(4,128)S(1)} %get-tuple-element.12), channel_id=1, source_target_pairs={{0,16},{1,17},{2,18},{3,19},{4,20},{5,21},{6,22},{7,23},{8,24},{9,... | collective-permute-start | bytes 3080 | tf_op jit(solution)/shard_map/ppermute | solution.py:147
  42.6 0.3 collective-permute-start.15
  42.9 0.0 collective-permute-done.13.refs_1_
  42.9 1.2 %collective-permute-done.14.refs_2_ = f32[4,64]{1,0:T(4,128)S(1)} collective-permute-done((f32[4,64]{1,0:T(4,128)S(1)}, f32[4,64]{1,0:T(4,128)S(1)}, u32[]{:S(2)}, u32[]{:S(2)}) %collective-permute-start.14) | collective-permute-done | bytes 1056 | tf_op jit(solution)/shard_map/ppermute | solution.py:147
  44.1 3.8 %collective-permute-done.15.refs_3_ = f32[4,64]{1,0:T(4,128)S(1)} collective-permute-done((f32[4,64]{1,0:T(4,128)S(1)}, f32[4,64]{1,0:T(4,128)S(1)}, u32[]{:S(2)}, u32[]{:S(2)}) %collective-permute-start.15) | collective-permute-done | bytes 1056 | tf_op jit(solution)/shard_map/ppermute | solution.py:147
  47.9 0.0 copy-done.3
  47.9 0.7 %shard_map.98 = (f32[4,64]{1,0:T(4,128)}, f32[4,64]{1,0:T(4,128)}) custom-call(s32[4,64]{1,0:T(4,128)S(1)} %copy-done.3, f32[4,64]{1,0:T(4,128)S(1)} %get-tuple-element.10.refs_0_, f32[4,64]{1,0:T(4,128)S(1)} %collective-permute-done.13.refs_1_, f32[4,64]{1,0:T(4,128)S(1)} %collective-permute-done.14.refs_2_, f32[4,64]{1,0:T(4,128)S(1)} %collective-permute-done.15.refs_3_), custom_call_target="tpu_custom_call" | custom-call | tf_op jit(solution)/shard_map/pallas_call | solution.py:124
  (4 shorter events, 0.1 us)
Async XLA Ops:
  0.6 0.7 %copy-start.5 = (s32[4]{0:T(128)S(1)}, s32[4]{0:T(128)}, u32[]{:S(2)}) copy-start(s32[4]{0:T(128)} %lengths_ref.1) | copy-start | bytes 52
  1.3 0.9 %copy-start = (bf16[4,128,128]{2,1,0:T(8,128)(2,1)S(1)}, bf16[4,128,128]{2,1,0:T(8,128)(2,1)}, u32[]{:S(2)}) copy-start(bf16[4,128,128]{2,1,0:T(8,128)(2,1)} %passages_ref) | copy-start | bytes 393220
  2.2 0.8 %copy-start.1 = (bf16[4,32,128]{2,1,0:T(8,128)(2,1)S(1)}, bf16[4,32,128]{2,1,0:T(8,128)(2,1)}, u32[]{:S(2)}) copy-start(bf16[4,32,128]{2,1,0:T(8,128)(2,1)} %param.8) | copy-start | bytes 98308
  3.0 0.7 %copy-start.4 = (s32[4,128]{1,0:T(4,128)S(1)}, s32[4,128]{1,0:T(4,128)}, u32[]{:S(2)}) copy-start(s32[4,128]{1,0:T(4,128)} %labels_ref.1) | copy-start | bytes 6148
  4.4 5.2 %collective-permute-start = (bf16[1,208,128]{2,1,0:T(8,128)(2,1)S(1)}, bf16[1,208,128]{2,1,0:T(8,128)(2,1)S(1)}, u32[]{:S(2)}, u32[]{:S(2)}) collective-permute-start(bf16[1,208,128]{2,1,0:T(8,128)(2,1)S(1)} %bitcast.3), channel_id=1, source_target_pairs={{0,8},{1,9},{2,10},{3,11},{4,12},{5,13},{6,14},{7,15},{8,0},{9,1},... | collective-permute-start | bytes 159752 | tf_op jit(solution)/shard_map/ppermute | solution.py:147
  9.6 6.1 %collective-permute-start.1 = (bf16[2,208,128]{2,1,0:T(8,128)(2,1)S(1)}, bf16[2,208,128]{2,1,0:T(8,128)(2,1)S(1)}, u32[]{:S(2)}, u32[]{:S(2)}) collective-permute-start(bf16[2,208,128]{2,1,0:T(8,128)(2,1)S(1)} %pad_maximum_fusion.2), channel_id=1, source_target_pairs={{0,16},{1,17},{2,18},{3,19},{4,20},{5,21},{6,22},{7,23},{8,24},{9,... | collective-permute-start | bytes 319496 | tf_op jit(solution)/shard_map/ppermute | solution.py:147
  15.7 6.5 %collective-permute-start.4 = (bf16[320,128]{1,0:T(8,128)(2,1)S(1)}, bf16[320,128]{1,0:T(8,128)(2,1)S(1)}, u32[]{:S(2)}, u32[]{:S(2)}) collective-permute-start(bf16[320,128]{1,0:T(8,128)(2,1)S(1)} %bitcast.7), channel_id=1, source_target_pairs={{0,6},{1,7},{2,4},{3,5},{4,2},{5,3},{6,0},{7,1},{8,14},{9,15},{10,... | collective-permute-start | bytes 245768 | tf_op jit(solution)/shard_map/ppermute | solution.py:147
  19.4 4.4 %collective-permute-start.3 = (bf16[320,128]{1,0:T(8,128)(2,1)S(1)}, bf16[320,128]{1,0:T(8,128)(2,1)S(1)}, u32[]{:S(2)}, u32[]{:S(2)}) collective-permute-start(bf16[320,128]{1,0:T(8,128)(2,1)S(1)} %bitcast.8), channel_id=1, source_target_pairs={{0,4},{1,5},{2,6},{3,7},{4,0},{5,1},{6,2},{7,3},{8,12},{9,13},{10,... | collective-permute-start | bytes 245768 | tf_op jit(solution)/shard_map/ppermute | solution.py:147
  19.9 4.4 %collective-permute-start.2 = (bf16[320,128]{1,0:T(8,128)(2,1)S(1)}, bf16[320,128]{1,0:T(8,128)(2,1)S(1)}, u32[]{:S(2)}, u32[]{:S(2)}) collective-permute-start(bf16[320,128]{1,0:T(8,128)(2,1)S(1)} %bitcast.9), channel_id=1, source_target_pairs={{0,2},{1,3},{2,0},{3,1},{4,6},{5,7},{6,4},{7,5},{8,10},{9,11},{10,... | collective-permute-start | bytes 245768 | tf_op jit(solution)/shard_map/ppermute | solution.py:147
  24.3 10.2 %copy-start.7 = (s32[128,3]{0,1:T(4,128)S(1)}, s32[128,3]{0,1:T(4,128)}, u32[]{:S(2)}) copy-start(s32[128,3]{0,1:T(4,128)} %param.13) | copy-start | bytes 4612
  24.4 12.7 %collective-permute-start.5 = (bf16[1280,128]{1,0:T(8,128)(2,1)S(1)}, bf16[1280,128]{1,0:T(8,128)(2,1)S(1)}, u32[]{:S(2)}, u32[]{:S(2)}) collective-permute-start(bf16[1280,128]{1,0:T(8,128)(2,1)S(1)} %pad_maximum_fusion.near_ref), channel_id=1, source_target_pairs={{0,1},{1,0},{2,3},{3,2},{4,5},{5,4},{6,7},{7,6},{8,9},{9,8},{10,11... | collective-permute-start | bytes 983048 | tf_op jit(solution)/shard_map/ppermute | solution.py:147
  24.4 10.3 %copy-start.6 = (s32[128,10]{0,1:T(8,128)S(1)}, s32[128,10]{0,1:T(8,128)}, u32[]{:S(2)}) copy-start(s32[128,10]{0,1:T(8,128)} %param.14) | copy-start | bytes 15364
  24.4 7.3 %collective-permute-start.11 = (bf16[512,128]{1,0:T(8,128)(2,1)S(1)}, bf16[512,128]{1,0:T(8,128)(2,1)S(1)}, u32[]{:S(2)}, u32[]{:S(2)}) collective-permute-start(bf16[512,128]{1,0:T(8,128)(2,1)S(1)} %get-tuple-element.9.refs_0_), channel_id=1, source_target_pairs={{0,6},{1,7},{2,4},{3,5},{4,2},{5,3},{6,0},{7,1},{8,14},{9,15},{10,... | collective-permute-start | bytes 393224 | tf_op jit(solution)/shard_map/ppermute | solution.py:147
  26.0 8.1 %collective-permute-start.9 = (bf16[512,128]{1,0:T(8,128)(2,1)S(1)}, bf16[512,128]{1,0:T(8,128)(2,1)S(1)}, u32[]{:S(2)}, u32[]{:S(2)}) collective-permute-start(bf16[512,128]{1,0:T(8,128)(2,1)S(1)} %get-tuple-element.9.refs_0_), channel_id=1, source_target_pairs={{0,4},{1,5},{2,6},{3,7},{4,0},{5,1},{6,2},{7,3},{8,12},{9,13},{10,... | collective-permute-start | bytes 393224 | tf_op jit(solution)/shard_map/ppermute | solution.py:147
  26.3 7.8 %collective-permute-start.7 = (bf16[512,128]{1,0:T(8,128)(2,1)S(1)}, bf16[512,128]{1,0:T(8,128)(2,1)S(1)}, u32[]{:S(2)}, u32[]{:S(2)}) collective-permute-start(bf16[512,128]{1,0:T(8,128)(2,1)S(1)} %get-tuple-element.9.refs_0_), channel_id=1, source_target_pairs={{0,2},{1,3},{2,0},{3,1},{4,6},{5,7},{6,4},{7,5},{8,10},{9,11},{10,... | collective-permute-start | bytes 393224 | tf_op jit(solution)/shard_map/ppermute | solution.py:147
  28.0 6.8 %collective-permute-start.6 = (bf16[512,128]{1,0:T(8,128)(2,1)S(1)}, bf16[512,128]{1,0:T(8,128)(2,1)S(1)}, u32[]{:S(2)}, u32[]{:S(2)}) collective-permute-start(bf16[512,128]{1,0:T(8,128)(2,1)S(1)} %get-tuple-element.9.refs_0_), channel_id=1, source_target_pairs={{0,1},{1,0},{2,3},{3,2},{4,5},{5,4},{6,7},{7,6},{8,9},{9,8},{10,11... | collective-permute-start | bytes 393224 | tf_op jit(solution)/shard_map/ppermute | solution.py:147
  31.8 3.1 %collective-permute-start.12 = (bf16[512,128]{1,0:T(8,128)(2,1)S(1)}, bf16[512,128]{1,0:T(8,128)(2,1)S(1)}, u32[]{:S(2)}, u32[]{:S(2)}) collective-permute-start(bf16[512,128]{1,0:T(8,128)(2,1)S(1)} %collective-permute-done.11.refs_6_), channel_id=1, source_target_pairs={{0,1},{1,0},{2,3},{3,2},{4,5},{5,4},{6,7},{7,6},{8,9},{9,8},{10,11... | collective-permute-start | bytes 393224 | tf_op jit(solution)/shard_map/ppermute | solution.py:147
  34.1 1.3 %collective-permute-start.10 = (bf16[512,128]{1,0:T(8,128)(2,1)S(1)}, bf16[512,128]{1,0:T(8,128)(2,1)S(1)}, u32[]{:S(2)}, u32[]{:S(2)}) collective-permute-start(bf16[512,128]{1,0:T(8,128)(2,1)S(1)} %collective-permute-done.9.refs_4_), channel_id=1, source_target_pairs={{0,1},{1,0},{2,3},{3,2},{4,5},{5,4},{6,7},{7,6},{8,9},{9,8},{10,11... | collective-permute-start | bytes 393224 | tf_op jit(solution)/shard_map/ppermute | solution.py:147
  34.2 1.4 %collective-permute-start.8 = (bf16[512,128]{1,0:T(8,128)(2,1)S(1)}, bf16[512,128]{1,0:T(8,128)(2,1)S(1)}, u32[]{:S(2)}, u32[]{:S(2)}) collective-permute-start(bf16[512,128]{1,0:T(8,128)(2,1)S(1)} %collective-permute-done.7.refs_2_), channel_id=1, source_target_pairs={{0,1},{1,0},{2,3},{3,2},{4,5},{5,4},{6,7},{7,6},{8,9},{9,8},{10,11... | collective-permute-start | bytes 393224 | tf_op jit(solution)/shard_map/ppermute | solution.py:147
  34.8 2.2 %copy-start.2 = (s32[4,1280]{1,0:T(4,128)S(1)}, s32[4,1280]{1,0:T(4,128)}, u32[]{:S(2)}) copy-start(s32[4,1280]{1,0:T(4,128)} %constant.2.clone.places_ref) | copy-start | bytes 61444
  38.5 4.4 %collective-permute-start.13 = (f32[4,64]{1,0:T(4,128)S(1)}, f32[4,64]{1,0:T(4,128)S(1)}, u32[]{:S(2)}, u32[]{:S(2)}) collective-permute-start(f32[4,64]{1,0:T(4,128)S(1)} %get-tuple-element.11), channel_id=1, source_target_pairs={{0,8},{1,9},{2,10},{3,11},{4,12},{5,13},{6,14},{7,15},{8,0},{9,1},... | collective-permute-start | bytes 3080 | tf_op jit(solution)/shard_map/ppermute | solution.py:147
  39.2 8.8 %copy-start.3 = (s32[4,64]{1,0:T(4,128)S(1)}, s32[4,64]{1,0:T(4,128)}, u32[]{:S(2)}) copy-start(s32[4,64]{1,0:T(4,128)} %candidates_ref.1) | copy-start | bytes 3076
  39.2 4.9 %collective-permute-start.14 = (f32[4,64]{1,0:T(4,128)S(1)}, f32[4,64]{1,0:T(4,128)S(1)}, u32[]{:S(2)}, u32[]{:S(2)}) collective-permute-start(f32[4,64]{1,0:T(4,128)S(1)} %get-tuple-element.12), channel_id=1, source_target_pairs={{0,16},{1,17},{2,18},{3,19},{4,20},{5,21},{6,22},{7,23},{8,24},{9,... | collective-permute-start | bytes 3080 | tf_op jit(solution)/shard_map/ppermute | solution.py:147
  42.6 5.4 %collective-permute-start.15 = (f32[4,64]{1,0:T(4,128)S(1)}, f32[4,64]{1,0:T(4,128)S(1)}, u32[]{:S(2)}, u32[]{:S(2)}) collective-permute-start(f32[4,64]{1,0:T(4,128)S(1)} %get-tuple-element.13), channel_id=1, source_target_pairs={{0,24},{1,25},{2,26},{3,27},{4,28},{5,29},{6,30},{7,31},{8,16},{9,... | collective-permute-start | bytes 3080 | tf_op jit(solution)/shard_map/ppermute | solution.py:147

commit v2 on v1

v2 whole, which is shorter than its diff:
```python
import functools

import jax
import jax.numpy as jnp
import numpy as np
from jax import lax
from jax.experimental import pallas as pl
from jax.experimental.pallas import tpu as pltpu
from jax.sharding import PartitionSpec as P

BANK_BITS = 3
HIGHEST = lax.Precision.HIGHEST
BF16, F32, I32 = jnp.bfloat16, jnp.float32, jnp.int32
COST = 10**9
VMEM_BYTES = 48 * 1024 * 1024


def iota(shape, dim):
    return lax.broadcasted_iota(I32, shape, dim)


def rows_dot(a, b, precision=None):
    return lax.dot_general(a, b, (((1,), (1,)), ((), ())), precision=precision, preferred_element_type=F32)


def prepare_kernel(
    clusters, lengths_hbm, queries_hbm, passages_hbm, labels_hbm, payload_ref, masked_ref, lengths_ref, passages_ref, labels_ref, arrived
):
    query_rows = queries_hbm.shape[0]
    copies = [
        pltpu.make_async_copy(passages_hbm, passages_ref, arrived.at[0]),
        pltpu.make_async_copy(lengths_hbm, lengths_ref, arrived.at[1]),
        pltpu.make_async_copy(labels_hbm, labels_ref, arrived.at[2]),
        pltpu.make_async_copy(queries_hbm, payload_ref.at[:query_rows, :], arrived.at[3]),
    ]
    for copy in copies:
        copy.start()
    count, tokens, features = passages_ref.shape
    totals = jnp.zeros((clusters * count, features), F32)
    for copy in copies[:3]:
        copy.wait()
    for p in range(count):
        length = lengths_ref[0:1, p : p + 1]
        document = passages_ref[p]
        wide = document.astype(F32)
        kept = jnp.where(iota((tokens, features), 0) < length, wide, wide[0:1, :])
        masked_ref[p * tokens : (p + 1) * tokens, :] = kept.astype(BF16)
        target = jnp.where(iota((1, tokens), 1) < length, labels_ref[p : p + 1, :] * count + p, -1)
        chosen = (iota((clusters * count, tokens), 0) == target).astype(F32).astype(BF16)
        totals = totals + jnp.dot(chosen, document, preferred_element_type=F32)
    high = totals.astype(BF16).astype(F32)
    payload_ref[query_rows:, :] = jnp.concatenate([high, totals - high], axis=0).astype(BF16)
    copies[3].wait()


def best_rows(document_refs, vectors, count, tokens):
    best, rows = [], count * tokens
    for document_ref in document_refs:
        for at in range(0, document_ref.shape[0], rows):
            scores = rows_dot(document_ref[at : at + rows, :], vectors)
            best += [jnp.max(scores[p * tokens : (p + 1) * tokens, :], axis=0, keepdims=True) for p in range(count)]
    return jnp.concatenate(best, axis=0)


def plain_kernel(count, tokens, query_tokens, query_rows, early_ref, late_ref, *refs):
    document_refs, plain_ref = refs[:-1], refs[-1]
    vectors = jnp.concatenate([slot[:query_rows, :] for slot in slots_of((early_ref, late_ref))], axis=0)
    best = best_rows(document_refs, vectors, count, tokens)
    shape = (plain_ref.shape[0], vectors.shape[0])
    first = iota(shape, 0) * query_tokens
    mean = jnp.where((iota(shape, 1) >= first) & (iota(shape, 1) < first + query_tokens), 1.0 / query_tokens, 0.0)
    plain_ref[...] = rows_dot(mean.astype(F32), best, HIGHEST)


def picks_kernel(
    count, slots, step, places_ref, feedback_ref, idf_ref, near_ref, far_ref, spread_ref, fb_ref, weight_ref
):
    number, clusters = weight_ref.shape
    me = lax.axis_index("shard")
    each = number // slots
    for s in range(slots):
        base = (me ^ (s * step)) * each
        fb_ref[s * each : (s + 1) * each, :] = feedback_ref[pl.ds(base, each), :]
        weight_ref[s * each : (s + 1) * each, :] = idf_ref[pl.ds(base, each), :].astype(F32) / (8.0 * clusters)
    wanted = fb_ref[...] ^ (me * count)
    for half, picks_ref in enumerate((near_ref, far_ref)):
        place = places_ref[2 * half : 2 * half + 1, :]
        kind = places_ref[2 * half + 1 : 2 * half + 2, :]
        times = jnp.zeros((number, place.shape[1]), F32)
        for k in range(wanted.shape[1]):
            times = times + jnp.where(wanted[:, k : k + 1] == place, 1.0, 0.0)
        for c in range(clusters):
            picks_ref[c * number : (c + 1) * number, :] = jnp.where(kind == c, times, 0.0).astype(BF16)
    shape = (number, clusters * number)
    spread = jnp.zeros(shape, F32)
    for c in range(clusters):
        spread = jnp.where(iota(shape, 1) == iota(shape, 0) + c * number, weight_ref[:, c : c + 1], spread)
    spread_ref[...] = spread


def slots_of(refs):
    return [ref.at[s] for ref in refs for s in range(ref.shape[0])]


def totals_kernel(skip, early_ref, late_ref, totals_ref):
    slots = slots_of((early_ref, late_ref))
    rows = totals_ref.shape[0] // len(slots)
    for s, slot in enumerate(slots):
        totals_ref[s * rows : (s + 1) * rows, :] = slot[skip:, :]


def pool_kernel(picks_ref, totals_ref, pooled_ref):
    pooled_ref[...] = jnp.dot(picks_ref[...], totals_ref[...], preferred_element_type=F32)


def expand_kernel(
    count, tokens, outputs, near_pooled_ref, far_ref, far_picks_ref, spread_ref, near_plain_ref, far_plain_ref, *refs
):
    document_refs, out_refs = refs[:-outputs], refs[-outputs:]
    pooled = near_pooled_ref[...] + jnp.dot(far_picks_ref[...], far_ref[...], preferred_element_type=F32)
    factor = lax.rsqrt(jnp.mean(pooled * pooled, axis=-1, keepdims=True) + 1e-06)
    expansion = (pooled * factor).astype(BF16)
    best = best_rows(document_refs, expansion, count, tokens)
    added = rows_dot(spread_ref[...], best, HIGHEST)
    plain = jnp.concatenate([near_plain_ref[...], far_plain_ref[...]], axis=1)
    both = jnp.concatenate([plain, plain + added], axis=1)
    each = both.shape[0] // outputs
    for s in range(outputs):
        out_refs[s][...] = both[s * each : (s + 1) * each, :]


def select_kernel(count, candidates_ref, *refs):
    block_refs, first_ref, final_ref = refs[:-2], refs[-2], refs[-1]
    me = lax.axis_index("shard")
    given, wanted = candidates_ref.shape
    width = block_refs[0].shape[1] // 2
    place = candidates_ref[...] ^ (me * count)
    owner, within = place // count % (width // count), place % count
    half = width // 2
    place = place // width * width + (owner & 1) * half + (owner >> 1) * count + within
    rows, lanes = -(-given // 8) * 8, -(-wanted // 128) * 128
    place = jnp.pad(place, ((0, rows - given), (0, lanes - wanted)))
    for side, out_ref in enumerate((first_ref, final_ref)):
        dense = jnp.concatenate([r[:, side * width : (side + 1) * width] for r in block_refs], axis=1)
        dense = jnp.pad(dense, ((0, rows - given), (0, 0)))
        pieces = []
        for at in range(0, place.shape[1], 128):
            here = place[:, at : at + 128]
            piece = jnp.zeros((rows, 128), F32)
            for group in range(dense.shape[1] // 128):
                found = jnp.take_along_axis(
                    dense[:, group * 128 : (group + 1) * 128], here & 127, axis=1, mode="promise_in_bounds"
                )
                piece = jnp.where((here >> 7) == group, found, piece)
            pieces.append(piece)
        out_ref[...] = jnp.concatenate(pieces, axis=1)[:given, :wanted]


def call(kernel, out_shape, *operands, scratch=(), specs=None, cost=None, vmem=VMEM_BYTES):
    return pl.pallas_call(
        kernel,
        out_shape=out_shape,
        in_specs=specs or [pl.BlockSpec(memory_space=pltpu.VMEM)] * len(operands),
        scratch_shapes=scratch,
        compiler_params=pltpu.CompilerParams(vmem_limit_bytes=vmem),
        cost_estimate=cost,
    )(*operands)


def local(devices, queries, passages, labels, lengths, candidates, feedback, idf):
    passages = lax.all_gather(passages, "rep", axis=0, tiled=True)
    count, tokens, features = passages.shape
    each, query_tokens, _ = queries.shape
    clusters = idf.shape[1]
    bank = min(1 << BANK_BITS, devices)
    columns = devices // bank
    number = columns * each
    query_rows = each * query_tokens
    total_rows = 2 * clusters * count
    sds = jax.ShapeDtypeStruct

    def swap(x, m):
        return lax.ppermute(x, "shard", [(i, i ^ m) for i in range(devices)])

    payload, masked = call(
        functools.partial(prepare_kernel, clusters),
        (sds((query_rows + total_rows, features), BF16), sds((count * tokens, features), BF16)),
        *[
            pltpu.with_memory_space_constraint(x, pltpu.HBM)
            for x in (lengths.reshape(1, count), queries.reshape(query_rows, features), passages, labels)
        ],
        specs=[pl.BlockSpec(memory_space=pltpu.HBM)] * 4,
        scratch=[
            pltpu.VMEM((1, count), I32),
            pltpu.VMEM((count, tokens, features), BF16),
            pltpu.VMEM((count, tokens), I32),
            pltpu.SemaphoreType.DMA((4,)),
        ],
    )
    received = swap(payload[None], bank)
    received, masked = lax.optimization_barrier((received, masked))
    gathered = [payload[None], received]
    row = np.arange(total_rows) % (clusters * count)
    places = []
    for half in range(2):
        m = np.arange(half, bank, 2)[:, None, None]
        s = np.arange(columns)[None, :, None] * bank
        place = (m + s) * count + (row % count)[None, None, :]
        kind = np.broadcast_to((row // count)[None, None, :], place.shape)
        places += [place.reshape(-1), kind.reshape(-1)]
    places = jnp.asarray(np.stack(places).astype(np.int32))
    picks = call(
        functools.partial(picks_kernel, count, columns, bank),
        (
            sds((clusters * number, places.shape[1]), BF16),
            sds((clusters * number, places.shape[1]), BF16),
            sds((number, clusters * number), F32),
        ),
        places,
        feedback,
        idf,
        scratch=[pltpu.VMEM((number, feedback.shape[1]), I32), pltpu.VMEM((number, clusters), F32)],
    )
    for bit in range(1, columns.bit_length() - 1):
        early = jnp.concatenate(gathered, axis=0)
        gathered = [early, swap(early, bank << bit)]
    documents = [masked] + [swap(masked, m) for m in range(2, bank, 2)]
    far_documents = swap(jnp.concatenate(documents, axis=0), 1)
    half = bank * count // 2
    plain = functools.partial(plain_kernel, count, tokens, query_tokens, query_rows)
    near_plain = call(plain, sds((number, half), F32), *gathered, *documents)
    far_plain = call(plain, sds((number, half), F32), *gathered, far_documents)
    own = call(
        functools.partial(totals_kernel, query_rows),
        sds((columns * total_rows, features), BF16),
        *gathered,
        cost=pl.CostEstimate(flops=COST, bytes_accessed=0, transcendentals=0),
    )
    near_plain, picks, *others = lax.optimization_barrier((near_plain, picks, *[swap(own, m) for m in range(2, bank, 2)]))
    near = jnp.concatenate([own, *others], axis=0)
    far = swap(near, 1)
    near_picks, far_picks, spread = picks
    near_pooled = call(pool_kernel, sds((clusters * number, features), F32), near_picks, near)
    blocks = call(
        functools.partial(expand_kernel, count, tokens, columns),
        [sds((each, 2 * bank * count), F32)] * columns,
        near_pooled,
        far,
        far_picks,
        spread,
        near_plain,
        far_plain,
        *documents,
        far_documents,
    )
    blocks = [blocks[0]] + [swap(blocks[s], s * bank) for s in range(1, columns)]
    return call(
        functools.partial(select_kernel, count),
        (sds(candidates.shape, F32), sds(candidates.shape, F32)),
        candidates,
        *blocks,
    )


def solution(mesh):
    return jax.shard_map(
        functools.partial(local, mesh.shape["shard"]),
        mesh=mesh,
        in_specs=(
            P(("rep", "shard"), None, None),
            P(("shard", "rep"), None, None),
            P("shard", None),
            P("shard"),
            P(("rep", "shard"), None),
            P("rep", None),
            P("rep", None),
        ),
        out_specs=(P(("rep", "shard"), None), P(("rep", "shard"), None)),
        check_vma=False,
    )
```

time: 48.9 us -> 35.1 us (0.72)
  waiting for transfers between devices: 21.3 us -> 9.91 us
  local copies, waits for them, and re-layouts: 3.24 us -> 0.85 us
  Pallas kernels: 4.31 us -> 5.52 us
  starting transfers between devices: 19 us -> 17.8 us
    ppermute x16 -> x13, waiting for transfers between devices: 21.3 us -> 9.91 us  [swap(): return lax.ppermute(x, 'shard', [(i, i ^ m) for i in range(devices)])]
    unnamed x18 -> x10, local copies, waits for them, and re-layouts: 3.23 us -> 0.85 us
    ppermute x16 -> x13, starting transfers between devices: 19 us -> 17.8 us  [swap(): return lax.ppermute(x, 'shard', [(i, i ^ m) for i in range(devices)])]
    pallas_call x4 -> x8, Pallas kernels: 4.31 us -> 5.52 us  [call(): pl.pallas_call(kernel, out_shape=out_shape, in_specs=specs or [pl.BlockSp...]
  transfers between devices with their start and end apart: 16 -> 13, of which waited for: 12 -> 8; matrix products, arithmetic and copies ran while one was open for 0% -> 1% of each run, Pallas kernels for 3% -> 7%
where the time goes in v2:
time: 35.1 us; the launch traced here: 34.9 us
  starting transfers between devices  17.8 us (51%)
  waiting for transfers between devices  9.91 us (28%)
  Pallas kernels  5.52 us (16%)
  local copies, waits for them, and re-layouts  0.85 us (2%)
  between operations  0.74 us (2%)
    ppermute x13, starting transfers between devices, swap(): return lax.ppermute(x, 'shard', [(i, i ^ m) for i in range(devices)])  17.8 us
    ppermute x13, waiting for transfers between devices, swap(): return lax.ppermute(x, 'shard', [(i, i ^ m) for i in range(devices)])  9.91 us
    pallas_call x8, Pallas kernels, call(): pl.pallas_call(kernel, out_shape=out_shape, in_specs=specs or [pl.BlockSp...  5.52 us
    unnamed x10, local copies, waits for them, and re-layouts  0.85 us
  transfers between devices with their start and end apart: 13, of which 8 were waited for; matrix products, arithmetic and copies ran while one was open for 1% of the time, Pallas kernels for 7%

profile of v2, /device:TPU:0, one launch (start us, length us, event | category | flops | bytes accessed | tf_op | source)
XLA Modules:
  0.0 34.9 jit_solution(917360148670157987)
XLA Ops:
  0.6 1.2 %shard_map.95 = (bf16[208,128]{1,0:T(8,128)(2,1)S(1)}, bf16[512,128]{1,0:T(8,128)(2,1)S(1)}) custom-call(s32[1,4]{1,0:T(1,128)} %bitcast.6, bf16[128,128]{1,0:T(8,128)(2,1)} %bitcast.5, bf16[4,128,128]{2,1,0:T(8,128)(2,1)} %passages_hbm, s32[4,128]{1,0:T(4,128)} %labels_hbm.1), custom_call_target="tpu_custom_call" | custom-call | tf_op jit(solution)/shard_map/pallas_call | solution.py:160
  1.8 3.1 %collective-permute-start = (bf16[1,208,128]{2,1,0:T(8,128)(2,1)S(1)}, bf16[1,208,128]{2,1,0:T(8,128)(2,1)S(1)}, u32[]{:S(2)}, u32[]{:S(2)}) collective-permute-start(bf16[1,208,128]{2,1,0:T(8,128)(2,1)S(1)} %bitcast.3), channel_id=1, source_target_pairs={{0,8},{1,9},{2,10},{3,11},{4,12},{5,13},{6,14},{7,15},{8,0},{9,1},... | collective-permute-start | bytes 159752 | tf_op jit(solution)/shard_map/ppermute | solution.py:183
  4.9 2.1 %collective-permute-done = bf16[1,208,128]{2,1,0:T(8,128)(2,1)S(1)} collective-permute-done((bf16[1,208,128]{2,1,0:T(8,128)(2,1)S(1)}, bf16[1,208,128]{2,1,0:T(8,128)(2,1)S(1)}, u32[]{:S(2)}, u32[]{:S(2)}) %collective-permute-start) | collective-permute-done | bytes 53280 | tf_op jit(solution)/shard_map/ppermute | solution.py:183
  7.0 0.0 copy-start.3
  7.0 0.0 copy-start.2
  7.0 3.1 %collective-permute-start.1 = (bf16[2,208,128]{2,1,0:T(8,128)(2,1)S(1)}, bf16[2,208,128]{2,1,0:T(8,128)(2,1)S(1)}, u32[]{:S(2)}, u32[]{:S(2)}) collective-permute-start(bf16[2,208,128]{2,1,0:T(8,128)(2,1)S(1)} %pad_maximum_fusion.2.early_ref), channel_id=1, source_target_pairs={{0,16},{1,17},{2,18},{3,19},{4,20},{5,21},{6,22},{7,23},{8,24},{9,... | collective-permute-start | bytes 319496 | tf_op jit(solution)/shard_map/ppermute | solution.py:183
  10.1 2.4 %collective-permute-start.4 = (bf16[512,128]{1,0:T(8,128)(2,1)S(1)}, bf16[512,128]{1,0:T(8,128)(2,1)S(1)}, u32[]{:S(2)}, u32[]{:S(2)}) collective-permute-start(bf16[512,128]{1,0:T(8,128)(2,1)S(1)} %get-tuple-element.23.refs_0_), channel_id=1, source_target_pairs={{0,6},{1,7},{2,4},{3,5},{4,2},{5,3},{6,0},{7,1},{8,14},{9,15},{10,... | collective-permute-start | bytes 393224 | tf_op jit(solution)/shard_map/ppermute | solution.py:183
  12.6 0.5 %collective-permute-start.3 = (bf16[512,128]{1,0:T(8,128)(2,1)S(1)}, bf16[512,128]{1,0:T(8,128)(2,1)S(1)}, u32[]{:S(2)}, u32[]{:S(2)}) collective-permute-start(bf16[512,128]{1,0:T(8,128)(2,1)S(1)} %get-tuple-element.23.refs_0_), channel_id=1, source_target_pairs={{0,4},{1,5},{2,6},{3,7},{4,0},{5,1},{6,2},{7,3},{8,12},{9,13},{10,... | collective-permute-start | bytes 393224 | tf_op jit(solution)/shard_map/ppermute | solution.py:183
  13.1 0.5 %collective-permute-start.2 = (bf16[512,128]{1,0:T(8,128)(2,1)S(1)}, bf16[512,128]{1,0:T(8,128)(2,1)S(1)}, u32[]{:S(2)}, u32[]{:S(2)}) collective-permute-start(bf16[512,128]{1,0:T(8,128)(2,1)S(1)} %get-tuple-element.23.refs_0_), channel_id=1, source_target_pairs={{0,2},{1,3},{2,0},{3,1},{4,6},{5,7},{6,4},{7,5},{8,10},{9,11},{10,... | collective-permute-start | bytes 393224 | tf_op jit(solution)/shard_map/ppermute | solution.py:183
  13.6 0.0 copy-done.3
  13.6 0.1 copy.10.feedback_ref
  13.8 0.0 copy-done.2
  13.8 0.0 copy-start
  13.8 0.1 copy.11.idf_ref
  13.9 0.6 %copy-done = s32[4,1280]{1,0:T(4,128)S(1)} copy-done((s32[4,1280]{1,0:T(4,128)S(1)}, s32[4,1280]{1,0:T(4,128)}, u32[]{:S(2)}) %copy-start) | copy-done | bytes 20504
  14.5 0.4 %shard_map.97 = (bf16[160,1280]{1,0:T(8,128)(2,1)S(1)}, bf16[160,1280]{1,0:T(8,128)(2,1)S(1)}, f32[16,160]{1,0:T(8,128)S(1)}) custom-call(s32[4,1280]{1,0:T(4,128)S(1)} %copy-done, s32[128,3]{1,0:T(8,128)S(1)} %copy.10.feedback_ref, s32[128,10]{1,0:T(8,128)S(1)} %copy.11.idf_ref), custom_call_target="tpu_custom_call" | custom-call | tf_op jit(solution)/shard_map/pallas_call | solution.py:160
  14.9 0.0 collective-permute-done.1.late_ref
  14.9 2.5 %collective-permute-start.7 = (bf16[320,128]{1,0:T(8,128)(2,1)S(1)}, bf16[320,128]{1,0:T(8,128)(2,1)S(1)}, u32[]{:S(2)}, u32[]{:S(2)}) collective-permute-start(bf16[320,128]{1,0:T(8,128)(2,1)S(1)} %shard_map.98), channel_id=1, source_target_pairs={{0,6},{1,7},{2,4},{3,5},{4,2},{5,3},{6,0},{7,1},{8,14},{9,15},{10,... | collective-permute-start | bytes 245768 | tf_op jit(solution)/shard_map/ppermute | solution.py:183
  17.4 0.5 %collective-permute-start.6 = (bf16[320,128]{1,0:T(8,128)(2,1)S(1)}, bf16[320,128]{1,0:T(8,128)(2,1)S(1)}, u32[]{:S(2)}, u32[]{:S(2)}) collective-permute-start(bf16[320,128]{1,0:T(8,128)(2,1)S(1)} %shard_map.98), channel_id=1, source_target_pairs={{0,4},{1,5},{2,6},{3,7},{4,0},{5,1},{6,2},{7,3},{8,12},{9,13},{10,... | collective-permute-start | bytes 245768 | tf_op jit(solution)/shard_map/ppermute | solution.py:183
  17.9 0.0 collective-permute-done.4.refs_3_
  17.9 0.5 %collective-permute-start.5 = (bf16[320,128]{1,0:T(8,128)(2,1)S(1)}, bf16[320,128]{1,0:T(8,128)(2,1)S(1)}, u32[]{:S(2)}, u32[]{:S(2)}) collective-permute-start(bf16[320,128]{1,0:T(8,128)(2,1)S(1)} %shard_map.98), channel_id=1, source_target_pairs={{0,2},{1,3},{2,0},{3,1},{4,6},{5,7},{6,4},{7,5},{8,10},{9,11},{10,... | collective-permute-start | bytes 245768 | tf_op jit(solution)/shard_map/ppermute | solution.py:183
  18.4 1.4 %collective-permute-done.3.refs_2_ = bf16[512,128]{1,0:T(8,128)(2,1)S(1)} collective-permute-done((bf16[512,128]{1,0:T(8,128)(2,1)S(1)}, bf16[512,128]{1,0:T(8,128)(2,1)S(1)}, u32[]{:S(2)}, u32[]{:S(2)}) %collective-permute-start.3) | collective-permute-done | bytes 131104 | tf_op jit(solution)/shard_map/ppermute | solution.py:183
  19.9 0.0 collective-permute-done.2.refs_1_
  19.9 0.1 collective-permute-start.9
  20.0 0.9 %shard_map.96.near_plain_ref = f32[16,16]{1,0:T(8,128)S(1)} custom-call(bf16[2,208,128]{2,1,0:T(8,128)(2,1)S(1)} %pad_maximum_fusion.2.early_ref, bf16[2,208,128]{2,1,0:T(8,128)(2,1)S(1)} %collective-permute-done.1.late_ref, bf16[512,128]{1,0:T(8,128)(2,1)S(1)} %get-tuple-element.23.refs_0_, bf16[512,128]{1,0:T(8,128)(2,1)S(1)} %collective-permute-done.2.refs_1_, ...), custom_call_target="tpu_custom_call" | custom-call | tf_op jit(solution)/shard_map/pallas_call | solution.py:160
  20.9 0.5 %collective-permute-done.7 = bf16[320,128]{1,0:T(8,128)(2,1)S(1)} collective-permute-done((bf16[320,128]{1,0:T(8,128)(2,1)S(1)}, bf16[320,128]{1,0:T(8,128)(2,1)S(1)}, u32[]{:S(2)}, u32[]{:S(2)}) %collective-permute-start.7) | collective-permute-done | bytes 81952 | tf_op jit(solution)/shard_map/ppermute | solution.py:183
  21.4 0.8 %collective-permute-done.6 = bf16[320,128]{1,0:T(8,128)(2,1)S(1)} collective-permute-done((bf16[320,128]{1,0:T(8,128)(2,1)S(1)}, bf16[320,128]{1,0:T(8,128)(2,1)S(1)}, u32[]{:S(2)}, u32[]{:S(2)}) %collective-permute-start.6) | collective-permute-done | bytes 81952 | tf_op jit(solution)/shard_map/ppermute | solution.py:183
  22.2 0.1 collective-permute-done.5
  22.4 0.1 collective-permute-start.8
  22.4 0.3 shard_map.99.near_pooled_ref
  22.7 0.0 collective-permute-done.9.refs_0_.refs_4_
  22.7 0.9 %shard_map.100.far_plain_ref = f32[16,16]{1,0:T(8,128)S(1)} custom-call(bf16[2,208,128]{2,1,0:T(8,128)(2,1)S(1)} %pad_maximum_fusion.2.early_ref, bf16[2,208,128]{2,1,0:T(8,128)(2,1)S(1)} %collective-permute-done.1.late_ref, bf16[2048,128]{1,0:T(8,128)(2,1)S(1)} %collective-permute-done.9.refs_0_.refs_4_), custom_call_target="tpu_custom_call" | custom-call | tf_op jit(solution)/shard_map/pallas_call | solution.py:160
  23.6 0.5 %collective-permute-done.8.far_ref = bf16[1280,128]{1,0:T(8,128)(2,1)S(1)} collective-permute-done((bf16[1280,128]{1,0:T(8,128)(2,1)S(1)}, bf16[1280,128]{1,0:T(8,128)(2,1)S(1)}, u32[]{:S(2)}, u32[]{:S(2)}) %collective-permute-start.8) | collective-permute-done | bytes 327712 | tf_op jit(solution)/shard_map/ppermute | solution.py:183
  24.1 1.3 %shard_map.101 = (f32[4,64]{1,0:T(4,128)S(1)}, f32[4,64]{1,0:T(4,128)S(1)}, f32[4,64]{1,0:T(4,128)S(1)}, f32[4,64]{1,0:T(4,128)S(1)}) custom-call(f32[160,128]{1,0:T(8,128)S(1)} %shard_map.99.near_pooled_ref, bf16[1280,128]{1,0:T(8,128)(2,1)S(1)} %collective-permute-done.8.far_ref, bf16[160,1280]{1,0:T(8,128)(2,1)S(1)} %get-tuple-element.31.far_picks_ref, ...), custom_call_target="tpu_custom_call" | custom-call | tf_op jit(solution)/shard_map/pallas_call | solution.py:160
  25.3 1.6 %collective-permute-start.10 = (f32[4,64]{1,0:T(4,128)S(1)}, f32[4,64]{1,0:T(4,128)S(1)}, u32[]{:S(2)}, u32[]{:S(2)}) collective-permute-start(f32[4,64]{1,0:T(4,128)S(1)} %get-tuple-element.35), channel_id=1, source_target_pairs={{0,8},{1,9},{2,10},{3,11},{4,12},{5,13},{6,14},{7,15},{8,0},{9,1},... | collective-permute-start | bytes 3080 | tf_op jit(solution)/shard_map/ppermute | solution.py:183
  26.9 0.0 copy-start.1
  26.9 1.8 %collective-permute-start.11 = (f32[4,64]{1,0:T(4,128)S(1)}, f32[4,64]{1,0:T(4,128)S(1)}, u32[]{:S(2)}, u32[]{:S(2)}) collective-permute-start(f32[4,64]{1,0:T(4,128)S(1)} %get-tuple-element.36), channel_id=1, source_target_pairs={{0,16},{1,17},{2,18},{3,19},{4,20},{5,21},{6,22},{7,23},{8,24},{9,... | collective-permute-start | bytes 3080 | tf_op jit(solution)/shard_map/ppermute | solution.py:183
  28.8 1.0 %collective-permute-start.12 = (f32[4,64]{1,0:T(4,128)S(1)}, f32[4,64]{1,0:T(4,128)S(1)}, u32[]{:S(2)}, u32[]{:S(2)}) collective-permute-start(f32[4,64]{1,0:T(4,128)S(1)} %get-tuple-element.37), channel_id=1, source_target_pairs={{0,24},{1,25},{2,26},{3,27},{4,28},{5,29},{6,30},{7,31},{8,16},{9,... | collective-permute-start | bytes 3080 | tf_op jit(solution)/shard_map/ppermute | solution.py:183
  29.7 0.0 collective-permute-done.10.refs_1_
  29.7 1.7 %collective-permute-done.11.refs_2_ = f32[4,64]{1,0:T(4,128)S(1)} collective-permute-done((f32[4,64]{1,0:T(4,128)S(1)}, f32[4,64]{1,0:T(4,128)S(1)}, u32[]{:S(2)}, u32[]{:S(2)}) %collective-permute-start.11) | collective-permute-done | bytes 1056 | tf_op jit(solution)/shard_map/ppermute | solution.py:183
  31.4 2.7 %collective-permute-done.12.refs_3_ = f32[4,64]{1,0:T(4,128)S(1)} collective-permute-done((f32[4,64]{1,0:T(4,128)S(1)}, f32[4,64]{1,0:T(4,128)S(1)}, u32[]{:S(2)}, u32[]{:S(2)}) %collective-permute-start.12) | collective-permute-done | bytes 1056 | tf_op jit(solution)/shard_map/ppermute | solution.py:183
  34.1 0.0 copy-done.1
  34.2 0.7 %shard_map.102 = (f32[4,64]{1,0:T(4,128)}, f32[4,64]{1,0:T(4,128)}) custom-call(s32[4,64]{1,0:T(4,128)S(1)} %copy-done.1, f32[4,64]{1,0:T(4,128)S(1)} %get-tuple-element.34.refs_0_, f32[4,64]{1,0:T(4,128)S(1)} %collective-permute-done.10.refs_1_, f32[4,64]{1,0:T(4,128)S(1)} %collective-permute-done.11.refs_2_, f32[4,64]{1,0:T(4,128)S(1)} %collective-permute-done.12.refs_3_), custom_call_target="tpu_custom_call" | custom-call | tf_op jit(solution)/shard_map/pallas_call | solution.py:160
  (4 shorter events, 0.1 us)
Async XLA Ops:
  1.8 5.2 %collective-permute-start = (bf16[1,208,128]{2,1,0:T(8,128)(2,1)S(1)}, bf16[1,208,128]{2,1,0:T(8,128)(2,1)S(1)}, u32[]{:S(2)}, u32[]{:S(2)}) collective-permute-start(bf16[1,208,128]{2,1,0:T(8,128)(2,1)S(1)} %bitcast.3), channel_id=1, source_target_pairs={{0,8},{1,9},{2,10},{3,11},{4,12},{5,13},{6,14},{7,15},{8,0},{9,1},... | collective-permute-start | bytes 159752 | tf_op jit(solution)/shard_map/ppermute | solution.py:183
  7.0 6.6 %copy-start.3 = (s32[128,3]{0,1:T(4,128)S(1)}, s32[128,3]{0,1:T(4,128)}, u32[]{:S(2)}) copy-start(s32[128,3]{0,1:T(4,128)} %param.13) | copy-start | bytes 4612
  7.0 6.7 %copy-start.2 = (s32[128,10]{0,1:T(8,128)S(1)}, s32[128,10]{0,1:T(8,128)}, u32[]{:S(2)}) copy-start(s32[128,10]{0,1:T(8,128)} %param.14) | copy-start | bytes 15364
  7.0 7.8 %collective-permute-start.1 = (bf16[2,208,128]{2,1,0:T(8,128)(2,1)S(1)}, bf16[2,208,128]{2,1,0:T(8,128)(2,1)S(1)}, u32[]{:S(2)}, u32[]{:S(2)}) collective-permute-start(bf16[2,208,128]{2,1,0:T(8,128)(2,1)S(1)} %pad_maximum_fusion.2.early_ref), channel_id=1, source_target_pairs={{0,16},{1,17},{2,18},{3,19},{4,20},{5,21},{6,22},{7,23},{8,24},{9,... | collective-permute-start | bytes 319496 | tf_op jit(solution)/shard_map/ppermute | solution.py:183
  10.1 7.8 %collective-permute-start.4 = (bf16[512,128]{1,0:T(8,128)(2,1)S(1)}, bf16[512,128]{1,0:T(8,128)(2,1)S(1)}, u32[]{:S(2)}, u32[]{:S(2)}) collective-permute-start(bf16[512,128]{1,0:T(8,128)(2,1)S(1)} %get-tuple-element.23.refs_0_), channel_id=1, source_target_pairs={{0,6},{1,7},{2,4},{3,5},{4,2},{5,3},{6,0},{7,1},{8,14},{9,15},{10,... | collective-permute-start | bytes 393224 | tf_op jit(solution)/shard_map/ppermute | solution.py:183
  12.6 7.3 %collective-permute-start.3 = (bf16[512,128]{1,0:T(8,128)(2,1)S(1)}, bf16[512,128]{1,0:T(8,128)(2,1)S(1)}, u32[]{:S(2)}, u32[]{:S(2)}) collective-permute-start(bf16[512,128]{1,0:T(8,128)(2,1)S(1)} %get-tuple-element.23.refs_0_), channel_id=1, source_target_pairs={{0,4},{1,5},{2,6},{3,7},{4,0},{5,1},{6,2},{7,3},{8,12},{9,13},{10,... | collective-permute-start | bytes 393224 | tf_op jit(solution)/shard_map/ppermute | solution.py:183
  13.1 6.8 %collective-permute-start.2 = (bf16[512,128]{1,0:T(8,128)(2,1)S(1)}, bf16[512,128]{1,0:T(8,128)(2,1)S(1)}, u32[]{:S(2)}, u32[]{:S(2)}) collective-permute-start(bf16[512,128]{1,0:T(8,128)(2,1)S(1)} %get-tuple-element.23.refs_0_), channel_id=1, source_target_pairs={{0,2},{1,3},{2,0},{3,1},{4,6},{5,7},{6,4},{7,5},{8,10},{9,11},{10,... | collective-permute-start | bytes 393224 | tf_op jit(solution)/shard_map/ppermute | solution.py:183
  13.8 0.7 %copy-start = (s32[4,1280]{1,0:T(4,128)S(1)}, s32[4,1280]{1,0:T(4,128)}, u32[]{:S(2)}) copy-start(s32[4,1280]{1,0:T(4,128)} %constant.2.clone.places_ref) | copy-start | bytes 61444
  14.9 6.5 %collective-permute-start.7 = (bf16[320,128]{1,0:T(8,128)(2,1)S(1)}, bf16[320,128]{1,0:T(8,128)(2,1)S(1)}, u32[]{:S(2)}, u32[]{:S(2)}) collective-permute-start(bf16[320,128]{1,0:T(8,128)(2,1)S(1)} %shard_map.98), channel_id=1, source_target_pairs={{0,6},{1,7},{2,4},{3,5},{4,2},{5,3},{6,0},{7,1},{8,14},{9,15},{10,... | collective-permute-start | bytes 245768 | tf_op jit(solution)/shard_map/ppermute | solution.py:183
  17.4 4.8 %collective-permute-start.6 = (bf16[320,128]{1,0:T(8,128)(2,1)S(1)}, bf16[320,128]{1,0:T(8,128)(2,1)S(1)}, u32[]{:S(2)}, u32[]{:S(2)}) collective-permute-start(bf16[320,128]{1,0:T(8,128)(2,1)S(1)} %shard_map.98), channel_id=1, source_target_pairs={{0,4},{1,5},{2,6},{3,7},{4,0},{5,1},{6,2},{7,3},{8,12},{9,13},{10,... | collective-permute-start | bytes 245768 | tf_op jit(solution)/shard_map/ppermute | solution.py:183
  17.9 4.4 %collective-permute-start.5 = (bf16[320,128]{1,0:T(8,128)(2,1)S(1)}, bf16[320,128]{1,0:T(8,128)(2,1)S(1)}, u32[]{:S(2)}, u32[]{:S(2)}) collective-permute-start(bf16[320,128]{1,0:T(8,128)(2,1)S(1)} %shard_map.98), channel_id=1, source_target_pairs={{0,2},{1,3},{2,0},{3,1},{4,6},{5,7},{6,4},{7,5},{8,10},{9,11},{10,... | collective-permute-start | bytes 245768 | tf_op jit(solution)/shard_map/ppermute | solution.py:183
  19.9 2.8 %collective-permute-start.9 = (bf16[2048,128]{1,0:T(8,128)(2,1)S(1)}, bf16[2048,128]{1,0:T(8,128)(2,1)S(1)}, u32[]{:S(2)}, u32[]{:S(2)}) collective-permute-start(bf16[2048,128]{1,0:T(8,128)(2,1)S(1)} %pad_maximum_fusion), channel_id=1, source_target_pairs={{0,1},{1,0},{2,3},{3,2},{4,5},{5,4},{6,7},{7,6},{8,9},{9,8},{10,11... | collective-permute-start | bytes 1572872 | tf_op jit(solution)/shard_map/ppermute | solution.py:183
  22.4 1.7 %collective-permute-start.8 = (bf16[1280,128]{1,0:T(8,128)(2,1)S(1)}, bf16[1280,128]{1,0:T(8,128)(2,1)S(1)}, u32[]{:S(2)}, u32[]{:S(2)}) collective-permute-start(bf16[1280,128]{1,0:T(8,128)(2,1)S(1)} %pad_maximum_fusion.1.totals_ref), channel_id=1, source_target_pairs={{0,1},{1,0},{2,3},{3,2},{4,5},{5,4},{6,7},{7,6},{8,9},{9,8},{10,11... | collective-permute-start | bytes 983048 | tf_op jit(solution)/shard_map/ppermute | solution.py:183
  25.3 4.4 %collective-permute-start.10 = (f32[4,64]{1,0:T(4,128)S(1)}, f32[4,64]{1,0:T(4,128)S(1)}, u32[]{:S(2)}, u32[]{:S(2)}) collective-permute-start(f32[4,64]{1,0:T(4,128)S(1)} %get-tuple-element.35), channel_id=1, source_target_pairs={{0,8},{1,9},{2,10},{3,11},{4,12},{5,13},{6,14},{7,15},{8,0},{9,1},... | collective-permute-start | bytes 3080 | tf_op jit(solution)/shard_map/ppermute | solution.py:183
  26.9 7.2 %copy-start.1 = (s32[4,64]{1,0:T(4,128)S(1)}, s32[4,64]{1,0:T(4,128)}, u32[]{:S(2)}) copy-start(s32[4,64]{1,0:T(4,128)} %candidates_ref.1) | copy-start | bytes 3076
  26.9 4.5 %collective-permute-start.11 = (f32[4,64]{1,0:T(4,128)S(1)}, f32[4,64]{1,0:T(4,128)S(1)}, u32[]{:S(2)}, u32[]{:S(2)}) collective-permute-start(f32[4,64]{1,0:T(4,128)S(1)} %get-tuple-element.36), channel_id=1, source_target_pairs={{0,16},{1,17},{2,18},{3,19},{4,20},{5,21},{6,22},{7,23},{8,24},{9,... | collective-permute-start | bytes 3080 | tf_op jit(solution)/shard_map/ppermute | solution.py:183
  28.8 5.4 %collective-permute-start.12 = (f32[4,64]{1,0:T(4,128)S(1)}, f32[4,64]{1,0:T(4,128)S(1)}, u32[]{:S(2)}, u32[]{:S(2)}) collective-permute-start(f32[4,64]{1,0:T(4,128)S(1)} %get-tuple-element.37), channel_id=1, source_target_pairs={{0,24},{1,25},{2,26},{3,27},{4,28},{5,29},{6,30},{7,31},{8,16},{9,... | collective-permute-start | bytes 3080 | tf_op jit(solution)/shard_map/ppermute | solution.py:183

commit v3 on v2

--- a/solution.py
+++ b/solution.py
@@ -2,7 +2,6 @@
 
 import jax
 import jax.numpy as jnp
-import numpy as np
 from jax import lax
 from jax.experimental import pallas as pl
 from jax.experimental.pallas import tpu as pltpu
@@ -62,9 +61,9 @@
     return jnp.concatenate(best, axis=0)
 
 
-def plain_kernel(count, tokens, query_tokens, query_rows, early_ref, late_ref, *refs):
-    document_refs, plain_ref = refs[:-1], refs[-1]
-    vectors = jnp.concatenate([slot[:query_rows, :] for slot in slots_of((early_ref, late_ref))], axis=0)
+def plain_kernel(count, tokens, query_tokens, query_rows, slots, *refs):
+    gathered_refs, document_refs, plain_ref = refs[:slots], refs[slots:-1], refs[-1]
+    vectors = jnp.concatenate([slot[:query_rows, :] for slot in gathered_refs], axis=0)
     best = best_rows(document_refs, vectors, count, tokens)
     shape = (plain_ref.shape[0], vectors.shape[0])
     first = iota(shape, 0) * query_tokens
@@ -72,20 +71,36 @@
     plain_ref[...] = rows_dot(mean.astype(F32), best, HIGHEST)
 
 
-def picks_kernel(
-    count, slots, step, places_ref, feedback_ref, idf_ref, near_ref, far_ref, spread_ref, fb_ref, weight_ref
-):
+def parts(index, size):
+    whole = jnp.floor((index.astype(F32) + 0.5) * (1.0 / size)).astype(I32)
+    return whole, index - whole * size
+
+
+def relative(passage, me, count, bank, columns):
+    owner, within = passage // count, passage % count
+    column = (owner // bank + columns - me // bank) % columns
+    return (column * bank + (owner % bank ^ me % bank)) * count + within
+
+
+def near_kernel(count, tokens, query_tokens, query_rows, bank, slots, feedback_ref, idf_ref, *refs):
+    refs, (plain_ref, near_ref, far_ref, spread_ref, fb_ref, weight_ref) = refs[:-6], refs[-6:]
+    plain_kernel(count, tokens, query_tokens, query_rows, len(slots), *refs, plain_ref)
+    me = lax.axis_index("shard")
     number, clusters = weight_ref.shape
-    me = lax.axis_index("shard")
-    each = number // slots
-    for s in range(slots):
-        base = (me ^ (s * step)) * each
+    each = number // len(slots)
+    for s, slot in enumerate(slots):
+        base = (me % bank + (me // bank + slot) % len(slots) * bank) * each
         fb_ref[s * each : (s + 1) * each, :] = feedback_ref[pl.ds(base, each), :]
         weight_ref[s * each : (s + 1) * each, :] = idf_ref[pl.ds(base, each), :].astype(F32) / (8.0 * clusters)
-    wanted = fb_ref[...] ^ (me * count)
+    wanted = relative(fb_ref[...], me, count, bank, len(slots))
+    block, row = parts(iota((1, near_ref.shape[1]), 1), 2 * clusters * count)
+    block, column = parts(block, len(slots))
+    kind, within = parts(jnp.where(row < clusters * count, row, row - clusters * count), count)
+    owner = 2 * block
+    for s, slot in enumerate(slots):
+        owner = jnp.where(column == s, owner + slot * bank, owner)
     for half, picks_ref in enumerate((near_ref, far_ref)):
-        place = places_ref[2 * half : 2 * half + 1, :]
-        kind = places_ref[2 * half + 1 : 2 * half + 2, :]
+        place = (owner ^ half) * count + within
         times = jnp.zeros((number, place.shape[1]), F32)
         for k in range(wanted.shape[1]):
             times = times + jnp.where(wanted[:, k : k + 1] == place, 1.0, 0.0)
@@ -98,12 +113,8 @@
     spread_ref[...] = spread
 
 
-def slots_of(refs):
-    return [ref.at[s] for ref in refs for s in range(ref.shape[0])]
-
-
-def totals_kernel(skip, early_ref, late_ref, totals_ref):
-    slots = slots_of((early_ref, late_ref))
+def totals_kernel(skip, *refs):
+    slots, totals_ref = refs[:-1], refs[-1]
     rows = totals_ref.shape[0] // len(slots)
     for s, slot in enumerate(slots):
         totals_ref[s * rows : (s + 1) * rows, :] = slot[skip:, :]
@@ -114,8 +125,9 @@
 
 
 def expand_kernel(
-    count, tokens, outputs, near_pooled_ref, far_ref, far_picks_ref, spread_ref, near_plain_ref, far_plain_ref, *refs
+    count, tokens, places, near_pooled_ref, far_ref, far_picks_ref, spread_ref, near_plain_ref, far_plain_ref, *refs
 ):
+    outputs = len(places)
     document_refs, out_refs = refs[:-outputs], refs[-outputs:]
     pooled = near_pooled_ref[...] + jnp.dot(far_picks_ref[...], far_ref[...], preferred_element_type=F32)
     factor = lax.rsqrt(jnp.mean(pooled * pooled, axis=-1, keepdims=True) + 1e-06)
@@ -125,16 +137,16 @@
     plain = jnp.concatenate([near_plain_ref[...], far_plain_ref[...]], axis=1)
     both = jnp.concatenate([plain, plain + added], axis=1)
     each = both.shape[0] // outputs
-    for s in range(outputs):
-        out_refs[s][...] = both[s * each : (s + 1) * each, :]
-
-
-def select_kernel(count, candidates_ref, *refs):
-    block_refs, first_ref, final_ref = refs[:-2], refs[-2], refs[-1]
+    for place, out_ref in zip(places, out_refs):
+        out_ref[...] = both[place * each : (place + 1) * each, :]
+
+
+def select_kernel(count, bank, places, candidates_ref, *refs):
+    block_refs, first_ref, final_ref = [refs[i] for i in places], refs[-2], refs[-1]
     me = lax.axis_index("shard")
     given, wanted = candidates_ref.shape
     width = block_refs[0].shape[1] // 2
-    place = candidates_ref[...] ^ (me * count)
+    place = relative(candidates_ref[...], me, count, bank, len(places))
     owner, within = place // count % (width // count), place % count
     half = width // 2
     place = place // width * width + (owner & 1) * half + (owner >> 1) * count + within
@@ -179,6 +191,9 @@
     total_rows = 2 * clusters * count
     sds = jax.ShapeDtypeStruct
 
+    def shift(x, s):
+        return lax.ppermute(x, "shard", [(i, (i + s * bank) % devices) for i in range(devices)])
+
     def swap(x, m):
         return lax.ppermute(x, "shard", [(i, i ^ m) for i in range(devices)])
 
@@ -197,38 +212,22 @@
             pltpu.SemaphoreType.DMA((4,)),
         ],
     )
-    received = swap(payload[None], bank)
-    received, masked = lax.optimization_barrier((received, masked))
-    gathered = [payload[None], received]
-    row = np.arange(total_rows) % (clusters * count)
-    places = []
-    for half in range(2):
-        m = np.arange(half, bank, 2)[:, None, None]
-        s = np.arange(columns)[None, :, None] * bank
-        place = (m + s) * count + (row % count)[None, None, :]
-        kind = np.broadcast_to((row // count)[None, None, :], place.shape)
-        places += [place.reshape(-1), kind.reshape(-1)]
-    places = jnp.asarray(np.stack(places).astype(np.int32))
-    picks = call(
-        functools.partial(picks_kernel, count, columns, bank),
-        (
-            sds((clusters * number, places.shape[1]), BF16),
-            sds((clusters * number, places.shape[1]), BF16),
-            sds((number, clusters * number), F32),
-        ),
-        places,
-        feedback,
-        idf,
-        scratch=[pltpu.VMEM((number, feedback.shape[1]), I32), pltpu.VMEM((number, clusters), F32)],
-    )
-    for bit in range(1, columns.bit_length() - 1):
-        early = jnp.concatenate(gathered, axis=0)
-        gathered = [early, swap(early, bank << bit)]
+    slots = list(range(columns))
+    gathered = [payload] + [shift(payload, -s) for s in slots[1:]]
     documents = [masked] + [swap(masked, m) for m in range(2, bank, 2)]
     far_documents = swap(jnp.concatenate(documents, axis=0), 1)
     half = bank * count // 2
-    plain = functools.partial(plain_kernel, count, tokens, query_tokens, query_rows)
-    near_plain = call(plain, sds((number, half), F32), *gathered, *documents)
+    plain = functools.partial(plain_kernel, count, tokens, query_tokens, query_rows, columns)
+    picks_shape = sds((clusters * number, bank // 2 * columns * total_rows), BF16)
+    ready = call(
+        functools.partial(near_kernel, count, tokens, query_tokens, query_rows, bank, slots),
+        (sds((number, half), F32), picks_shape, picks_shape, sds((number, clusters * number), F32)),
+        feedback,
+        idf,
+        *gathered,
+        *documents,
+        scratch=[pltpu.VMEM((number, feedback.shape[1]), I32), pltpu.VMEM((number, clusters), F32)],
+    )
     far_plain = call(plain, sds((number, half), F32), *gathered, far_documents)
     own = call(
         functools.partial(totals_kernel, query_rows),
@@ -236,13 +235,14 @@
         *gathered,
         cost=pl.CostEstimate(flops=COST, bytes_accessed=0, transcendentals=0),
     )
-    near_plain, picks, *others = lax.optimization_barrier((near_plain, picks, *[swap(own, m) for m in range(2, bank, 2)]))
+    ready, *others = lax.optimization_barrier((ready, *[swap(own, m) for m in range(2, bank, 2)]))
+    near_plain, near_picks, far_picks, spread = ready
     near = jnp.concatenate([own, *others], axis=0)
     far = swap(near, 1)
-    near_picks, far_picks, spread = picks
     near_pooled = call(pool_kernel, sds((clusters * number, features), F32), near_picks, near)
+    returns = slots[1:] + slots[:1]
     blocks = call(
-        functools.partial(expand_kernel, count, tokens, columns),
+        functools.partial(expand_kernel, count, tokens, [slots.index(m) for m in returns]),
         [sds((each, 2 * bank * count), F32)] * columns,
         near_pooled,
         far,
@@ -253,9 +253,9 @@
         *documents,
         far_documents,
     )
-    blocks = [blocks[0]] + [swap(blocks[s], s * bank) for s in range(1, columns)]
+    blocks = [shift(block, s) if s else block for s, block in zip(returns, blocks)]
     return call(
-        functools.partial(select_kernel, count),
+        functools.partial(select_kernel, count, bank, [returns.index(-s % columns) for s in range(columns)]),
         (sds(candidates.shape, F32), sds(candidates.shape, F32)),
         candidates,
         *blocks,

time: 35.1 us -> 30.4 us (0.87)
  waiting for transfers between devices: 9.91 us -> 4.55 us
  starting transfers between devices: 17.8 us -> 19.4 us
  local copies, waits for them, and re-layouts: 0.85 us -> 0.24 us
    ppermute x0 -> x6, starting transfers between devices: none -> 10.9 us  [shift(): lax.ppermute(x, 'shard', [(i, (i + s * bank) % devices) for i in range(de...]
    ppermute x13 -> x8, starting transfers between devices: 17.8 us -> 8.51 us  [swap(): return lax.ppermute(x, 'shard', [(i, i ^ m) for i in range(devices)])]
    ppermute x13 -> x8, waiting for transfers between devices: 9.91 us -> 2.42 us  [swap(): return lax.ppermute(x, 'shard', [(i, i ^ m) for i in range(devices)])]
    ppermute x0 -> x6, waiting for transfers between devices: none -> 2.13 us  [shift(): lax.ppermute(x, 'shard', [(i, (i + s * bank) % devices) for i in range(de...]
    unnamed x10 -> x8, local copies, waits for them, and re-layouts: 0.85 us -> 0.24 us
    pallas_call x8 -> x7, Pallas kernels: 5.52 us -> 5.29 us  [call(): pl.pallas_call(kernel, out_shape=out_shape, in_specs=specs or [pl.BlockSp...]
  transfers between devices with their start and end apart: 13 -> 14, of which waited for: 8 -> 9; matrix products, arithmetic and copies ran while one was open for 1% -> 1% of each run, Pallas kernels for 7% -> 7%
where the time goes in v3:
time: 30.4 us; the launch traced here: 30.2 us
  starting transfers between devices  19.4 us (64%)
  Pallas kernels  5.29 us (17%)
  waiting for transfers between devices  4.55 us (15%)
  between operations  0.73 us (2%)
    ppermute x6, starting transfers between devices, shift(): lax.ppermute(x, 'shard', [(i, (i + s * bank) % devices) for i in range(de...  10.9 us
    ppermute x8, starting transfers between devices, swap(): return lax.ppermute(x, 'shard', [(i, i ^ m) for i in range(devices)])  8.51 us
    pallas_call x7, Pallas kernels, call(): pl.pallas_call(kernel, out_shape=out_shape, in_specs=specs or [pl.BlockSp...  5.29 us
    ppermute x8, waiting for transfers between devices, swap(): return lax.ppermute(x, 'shard', [(i, i ^ m) for i in range(devices)])  2.42 us
    ppermute x6, waiting for transfers between devices, shift(): lax.ppermute(x, 'shard', [(i, (i + s * bank) % devices) for i in range(de...  2.13 us
  transfers between devices with their start and end apart: 14, of which 9 were waited for; matrix products, arithmetic and copies ran while one was open for 1% of the time, Pallas kernels for 7%

profile of v3, /device:TPU:0, one launch (start us, length us, event | category | flops | bytes accessed | tf_op | source)
XLA Modules:
  0.0 30.2 jit_solution(15196024684410373855)
XLA Ops:
  0.6 1.2 %shard_map.86 = (bf16[208,128]{1,0:T(8,128)(2,1)S(1)}, bf16[512,128]{1,0:T(8,128)(2,1)S(1)}) custom-call(s32[1,4]{1,0:T(1,128)} %bitcast.3, bf16[128,128]{1,0:T(8,128)(2,1)} %bitcast.2, bf16[4,128,128]{2,1,0:T(8,128)(2,1)} %passages_hbm, s32[4,128]{1,0:T(4,128)} %labels_hbm.1), custom_call_target="tpu_custom_call" | custom-call | tf_op jit(solution)/shard_map/pallas_call | solution.py:172
  1.8 0.0 copy-start.2
  1.8 3.1 %collective-permute-start.2 = (bf16[208,128]{1,0:T(8,128)(2,1)S(1)}, bf16[208,128]{1,0:T(8,128)(2,1)S(1)}, u32[]{:S(2)}, u32[]{:S(2)}) collective-permute-start(bf16[208,128]{1,0:T(8,128)(2,1)S(1)} %get-tuple-element.19.refs_0_), channel_id=1, source_target_pairs={{0,8},{1,9},{2,10},{3,11},{4,12},{5,13},{6,14},{7,15},{8,16},{9,17... | collective-permute-start | bytes 159752 | tf_op jit(solution)/shard_map/ppermute | solution.py:195
  4.9 2.6 %collective-permute-start.1 = (bf16[208,128]{1,0:T(8,128)(2,1)S(1)}, bf16[208,128]{1,0:T(8,128)(2,1)S(1)}, u32[]{:S(2)}, u32[]{:S(2)}) collective-permute-start(bf16[208,128]{1,0:T(8,128)(2,1)S(1)} %get-tuple-element.19.refs_0_), channel_id=1, source_target_pairs={{0,16},{1,17},{2,18},{3,19},{4,20},{5,21},{6,22},{7,23},{8,24},{9,... | collective-permute-start | bytes 159752 | tf_op jit(solution)/shard_map/ppermute | solution.py:195
  7.5 1.3 %collective-permute-start = (bf16[208,128]{1,0:T(8,128)(2,1)S(1)}, bf16[208,128]{1,0:T(8,128)(2,1)S(1)}, u32[]{:S(2)}, u32[]{:S(2)}) collective-permute-start(bf16[208,128]{1,0:T(8,128)(2,1)S(1)} %get-tuple-element.19.refs_0_), channel_id=1, source_target_pairs={{0,24},{1,25},{2,26},{3,27},{4,28},{5,29},{6,30},{7,31},{8,0},{9,1... | collective-permute-start | bytes 159752 | tf_op jit(solution)/shard_map/ppermute | solution.py:195
  8.8 0.0 copy-start.1
  8.8 2.4 %collective-permute-start.5 = (bf16[512,128]{1,0:T(8,128)(2,1)S(1)}, bf16[512,128]{1,0:T(8,128)(2,1)S(1)}, u32[]{:S(2)}, u32[]{:S(2)}) collective-permute-start(bf16[512,128]{1,0:T(8,128)(2,1)S(1)} %get-tuple-element.20.refs_4_.refs_0_), channel_id=1, source_target_pairs={{0,6},{1,7},{2,4},{3,5},{4,2},{5,3},{6,0},{7,1},{8,14},{9,15},{10,... | collective-permute-start | bytes 393224 | tf_op jit(solution)/shard_map/ppermute | solution.py:198
  11.3 0.5 %collective-permute-start.4 = (bf16[512,128]{1,0:T(8,128)(2,1)S(1)}, bf16[512,128]{1,0:T(8,128)(2,1)S(1)}, u32[]{:S(2)}, u32[]{:S(2)}) collective-permute-start(bf16[512,128]{1,0:T(8,128)(2,1)S(1)} %get-tuple-element.20.refs_4_.refs_0_), channel_id=1, source_target_pairs={{0,4},{1,5},{2,6},{3,7},{4,0},{5,1},{6,2},{7,3},{8,12},{9,13},{10,... | collective-permute-start | bytes 393224 | tf_op jit(solution)/shard_map/ppermute | solution.py:198
  11.8 0.0 collective-permute-done.2.refs_3_
  11.8 0.5 %collective-permute-start.3 = (bf16[512,128]{1,0:T(8,128)(2,1)S(1)}, bf16[512,128]{1,0:T(8,128)(2,1)S(1)}, u32[]{:S(2)}, u32[]{:S(2)}) collective-permute-start(bf16[512,128]{1,0:T(8,128)(2,1)S(1)} %get-tuple-element.20.refs_4_.refs_0_), channel_id=1, source_target_pairs={{0,2},{1,3},{2,0},{3,1},{4,6},{5,7},{6,4},{7,5},{8,10},{9,11},{10,... | collective-permute-start | bytes 393224 | tf_op jit(solution)/shard_map/ppermute | solution.py:198
  12.3 0.0 copy-done.2
  12.3 0.1 copy.9.feedback_ref
  12.5 0.0 copy-done.1
  12.5 0.1 copy.10.idf_ref
  12.6 0.0 collective-permute-done.1.refs_2_
  12.6 0.0 collective-permute-done.refs_1_
  12.6 2.5 %collective-permute-start.8 = (bf16[320,128]{1,0:T(8,128)(2,1)S(1)}, bf16[320,128]{1,0:T(8,128)(2,1)S(1)}, u32[]{:S(2)}, u32[]{:S(2)}) collective-permute-start(bf16[320,128]{1,0:T(8,128)(2,1)S(1)} %shard_map.88), channel_id=1, source_target_pairs={{0,6},{1,7},{2,4},{3,5},{4,2},{5,3},{6,0},{7,1},{8,14},{9,15},{10,... | collective-permute-start | bytes 245768 | tf_op jit(solution)/shard_map/ppermute | solution.py:198
  15.1 0.5 %collective-permute-start.7 = (bf16[320,128]{1,0:T(8,128)(2,1)S(1)}, bf16[320,128]{1,0:T(8,128)(2,1)S(1)}, u32[]{:S(2)}, u32[]{:S(2)}) collective-permute-start(bf16[320,128]{1,0:T(8,128)(2,1)S(1)} %shard_map.88), channel_id=1, source_target_pairs={{0,4},{1,5},{2,6},{3,7},{4,0},{5,1},{6,2},{7,3},{8,12},{9,13},{10,... | collective-permute-start | bytes 245768 | tf_op jit(solution)/shard_map/ppermute | solution.py:198
  15.6 0.1 collective-permute-done.5.refs_7_.refs_3_
  15.7 1.9 %collective-permute-start.6 = (bf16[320,128]{1,0:T(8,128)(2,1)S(1)}, bf16[320,128]{1,0:T(8,128)(2,1)S(1)}, u32[]{:S(2)}, u32[]{:S(2)}) collective-permute-start(bf16[320,128]{1,0:T(8,128)(2,1)S(1)} %shard_map.88), channel_id=1, source_target_pairs={{0,2},{1,3},{2,0},{3,1},{4,6},{5,7},{6,4},{7,5},{8,10},{9,11},{10,... | collective-permute-start | bytes 245768 | tf_op jit(solution)/shard_map/ppermute | solution.py:198
  17.6 1.1 %collective-permute-done.4.refs_6_.refs_2_ = bf16[512,128]{1,0:T(8,128)(2,1)S(1)} collective-permute-done((bf16[512,128]{1,0:T(8,128)(2,1)S(1)}, bf16[512,128]{1,0:T(8,128)(2,1)S(1)}, u32[]{:S(2)}, u32[]{:S(2)}) %collective-permute-start.4) | collective-permute-done | bytes 131104 | tf_op jit(solution)/shard_map/ppermute | solution.py:198
  18.7 0.1 collective-permute-done.3.refs_5_.refs_1_
  18.8 0.1 collective-permute-start.10
  18.9 1.0 %shard_map.87 = (f32[16,16]{1,0:T(8,128)S(1)}, bf16[160,1280]{1,0:T(8,128)(2,1)S(1)}, bf16[160,1280]{1,0:T(8,128)(2,1)S(1)}, f32[16,160]{1,0:T(8,128)S(1)}) custom-call(s32[128,3]{1,0:T(8,128)S(1)} %copy.9.feedback_ref, s32[128,10]{1,0:T(8,128)S(1)} %copy.10.idf_ref, bf16[208,128]{1,0:T(8,128)(2,1)S(1)} %get-tuple-element.19.refs_0_, ...), custom_call_target="tpu_custom_call" | custom-call | tf_op jit(solution)/shard_map/pallas_call | solution.py:172
  19.9 0.3 %collective-permute-done.8 = bf16[320,128]{1,0:T(8,128)(2,1)S(1)} collective-permute-done((bf16[320,128]{1,0:T(8,128)(2,1)S(1)}, bf16[320,128]{1,0:T(8,128)(2,1)S(1)}, u32[]{:S(2)}, u32[]{:S(2)}) %collective-permute-start.8) | collective-permute-done | bytes 81952 | tf_op jit(solution)/shard_map/ppermute | solution.py:198
  20.3 0.2 collective-permute-done.7
  20.5 0.1 collective-permute-done.6
  20.6 0.1 collective-permute-start.9
  20.7 0.3 shard_map.89.near_pooled_ref
  20.9 0.0 collective-permute-done.10.refs_4_
  20.9 0.9 %shard_map.90.far_plain_ref = f32[16,16]{1,0:T(8,128)S(1)} custom-call(bf16[208,128]{1,0:T(8,128)(2,1)S(1)} %get-tuple-element.19.refs_0_, bf16[208,128]{1,0:T(8,128)(2,1)S(1)} %collective-permute-done.refs_1_, bf16[208,128]{1,0:T(8,128)(2,1)S(1)} %collective-permute-done.1.refs_2_, bf16[208,128]{1,0:T(8,128)(2,1)S(1)} %collective-permute-done.2.refs_3_, ...), custom_call_target="tpu_custom_call" | custom-call | tf_op jit(solution)/shard_map/pallas_call | solution.py:172
  21.8 0.5 %collective-permute-done.9.far_ref = bf16[1280,128]{1,0:T(8,128)(2,1)S(1)} collective-permute-done((bf16[1280,128]{1,0:T(8,128)(2,1)S(1)}, bf16[1280,128]{1,0:T(8,128)(2,1)S(1)}, u32[]{:S(2)}, u32[]{:S(2)}) %collective-permute-start.9) | collective-permute-done | bytes 327712 | tf_op jit(solution)/shard_map/ppermute | solution.py:198
  22.3 1.3 %shard_map.91 = (f32[4,64]{1,0:T(4,128)S(1)}, f32[4,64]{1,0:T(4,128)S(1)}, f32[4,64]{1,0:T(4,128)S(1)}, f32[4,64]{1,0:T(4,128)S(1)}) custom-call(f32[160,128]{1,0:T(8,128)S(1)} %shard_map.89.near_pooled_ref, bf16[1280,128]{1,0:T(8,128)(2,1)S(1)} %collective-permute-done.9.far_ref, bf16[160,1280]{1,0:T(8,128)(2,1)S(1)} %get-tuple-element.29.far_picks_ref, ...), custom_call_target="tpu_custom_call" | custom-call | tf_op jit(solution)/shard_map/pallas_call | solution.py:172
  23.5 0.7 %collective-permute-start.11 = (f32[4,64]{1,0:T(4,128)S(1)}, f32[4,64]{1,0:T(4,128)S(1)}, u32[]{:S(2)}, u32[]{:S(2)}) collective-permute-start(f32[4,64]{1,0:T(4,128)S(1)} %get-tuple-element.32), channel_id=1, source_target_pairs={{0,8},{1,9},{2,10},{3,11},{4,12},{5,13},{6,14},{7,15},{8,16},{9,17... | collective-permute-start | bytes 3080 | tf_op jit(solution)/shard_map/ppermute | solution.py:195
  24.2 0.0 copy-start
  24.2 1.5 %collective-permute-start.12 = (f32[4,64]{1,0:T(4,128)S(1)}, f32[4,64]{1,0:T(4,128)S(1)}, u32[]{:S(2)}, u32[]{:S(2)}) collective-permute-start(f32[4,64]{1,0:T(4,128)S(1)} %get-tuple-element.33), channel_id=1, source_target_pairs={{0,16},{1,17},{2,18},{3,19},{4,20},{5,21},{6,22},{7,23},{8,24},{9,... | collective-permute-start | bytes 3080 | tf_op jit(solution)/shard_map/ppermute | solution.py:195
  25.8 1.6 %collective-permute-start.13 = (f32[4,64]{1,0:T(4,128)S(1)}, f32[4,64]{1,0:T(4,128)S(1)}, u32[]{:S(2)}, u32[]{:S(2)}) collective-permute-start(f32[4,64]{1,0:T(4,128)S(1)} %get-tuple-element.34), channel_id=1, source_target_pairs={{0,24},{1,25},{2,26},{3,27},{4,28},{5,29},{6,30},{7,31},{8,0},{9,1... | collective-permute-start | bytes 3080 | tf_op jit(solution)/shard_map/ppermute | solution.py:195
  27.4 1.6 %collective-permute-done.11.refs_0_ = f32[4,64]{1,0:T(4,128)S(1)} collective-permute-done((f32[4,64]{1,0:T(4,128)S(1)}, f32[4,64]{1,0:T(4,128)S(1)}, u32[]{:S(2)}, u32[]{:S(2)}) %collective-permute-start.11) | collective-permute-done | bytes 1056 | tf_op jit(solution)/shard_map/ppermute | solution.py:195
  28.9 0.0 collective-permute-done.12.refs_1_
  28.9 0.6 %collective-permute-done.13.refs_2_ = f32[4,64]{1,0:T(4,128)S(1)} collective-permute-done((f32[4,64]{1,0:T(4,128)S(1)}, f32[4,64]{1,0:T(4,128)S(1)}, u32[]{:S(2)}, u32[]{:S(2)}) %collective-permute-start.13) | collective-permute-done | bytes 1056 | tf_op jit(solution)/shard_map/ppermute | solution.py:195
  29.5 0.0 copy-done
  29.5 0.7 %shard_map.92 = (f32[4,64]{1,0:T(4,128)}, f32[4,64]{1,0:T(4,128)}) custom-call(s32[4,64]{1,0:T(4,128)S(1)} %copy-done, f32[4,64]{1,0:T(4,128)S(1)} %collective-permute-done.11.refs_0_, f32[4,64]{1,0:T(4,128)S(1)} %collective-permute-done.12.refs_1_, f32[4,64]{1,0:T(4,128)S(1)} %collective-permute-done.13.refs_2_, f32[4,64]{1,0:T(4,128)S(1)} %get-tuple-element.35.refs_3_), custom_call_target="tpu_custom_call" | custom-call | tf_op jit(solution)/shard_map/pallas_call | solution.py:172
  (3 shorter events, 0.1 us)
Async XLA Ops:
  1.8 10.5 %copy-start.2 = (s32[128,3]{0,1:T(4,128)S(1)}, s32[128,3]{0,1:T(4,128)}, u32[]{:S(2)}) copy-start(s32[128,3]{0,1:T(4,128)} %param.12) | copy-start | bytes 4612
  1.8 10.0 %collective-permute-start.2 = (bf16[208,128]{1,0:T(8,128)(2,1)S(1)}, bf16[208,128]{1,0:T(8,128)(2,1)S(1)}, u32[]{:S(2)}, u32[]{:S(2)}) collective-permute-start(bf16[208,128]{1,0:T(8,128)(2,1)S(1)} %get-tuple-element.19.refs_0_), channel_id=1, source_target_pairs={{0,8},{1,9},{2,10},{3,11},{4,12},{5,13},{6,14},{7,15},{8,16},{9,17... | collective-permute-start | bytes 159752 | tf_op jit(solution)/shard_map/ppermute | solution.py:195
  4.9 7.7 %collective-permute-start.1 = (bf16[208,128]{1,0:T(8,128)(2,1)S(1)}, bf16[208,128]{1,0:T(8,128)(2,1)S(1)}, u32[]{:S(2)}, u32[]{:S(2)}) collective-permute-start(bf16[208,128]{1,0:T(8,128)(2,1)S(1)} %get-tuple-element.19.refs_0_), channel_id=1, source_target_pairs={{0,16},{1,17},{2,18},{3,19},{4,20},{5,21},{6,22},{7,23},{8,24},{9,... | collective-permute-start | bytes 159752 | tf_op jit(solution)/shard_map/ppermute | solution.py:195
  7.5 5.1 %collective-permute-start = (bf16[208,128]{1,0:T(8,128)(2,1)S(1)}, bf16[208,128]{1,0:T(8,128)(2,1)S(1)}, u32[]{:S(2)}, u32[]{:S(2)}) collective-permute-start(bf16[208,128]{1,0:T(8,128)(2,1)S(1)} %get-tuple-element.19.refs_0_), channel_id=1, source_target_pairs={{0,24},{1,25},{2,26},{3,27},{4,28},{5,29},{6,30},{7,31},{8,0},{9,1... | collective-permute-start | bytes 159752 | tf_op jit(solution)/shard_map/ppermute | solution.py:195
  8.8 3.6 %copy-start.1 = (s32[128,10]{0,1:T(8,128)S(1)}, s32[128,10]{0,1:T(8,128)}, u32[]{:S(2)}) copy-start(s32[128,10]{0,1:T(8,128)} %param.13) | copy-start | bytes 15364
  8.8 6.9 %collective-permute-start.5 = (bf16[512,128]{1,0:T(8,128)(2,1)S(1)}, bf16[512,128]{1,0:T(8,128)(2,1)S(1)}, u32[]{:S(2)}, u32[]{:S(2)}) collective-permute-start(bf16[512,128]{1,0:T(8,128)(2,1)S(1)} %get-tuple-element.20.refs_4_.refs_0_), channel_id=1, source_target_pairs={{0,6},{1,7},{2,4},{3,5},{4,2},{5,3},{6,0},{7,1},{8,14},{9,15},{10,... | collective-permute-start | bytes 393224 | tf_op jit(solution)/shard_map/ppermute | solution.py:198
  11.3 7.4 %collective-permute-start.4 = (bf16[512,128]{1,0:T(8,128)(2,1)S(1)}, bf16[512,128]{1,0:T(8,128)(2,1)S(1)}, u32[]{:S(2)}, u32[]{:S(2)}) collective-permute-start(bf16[512,128]{1,0:T(8,128)(2,1)S(1)} %get-tuple-element.20.refs_4_.refs_0_), channel_id=1, source_target_pairs={{0,4},{1,5},{2,6},{3,7},{4,0},{5,1},{6,2},{7,3},{8,12},{9,13},{10,... | collective-permute-start | bytes 393224 | tf_op jit(solution)/shard_map/ppermute | solution.py:198
  11.8 7.0 %collective-permute-start.3 = (bf16[512,128]{1,0:T(8,128)(2,1)S(1)}, bf16[512,128]{1,0:T(8,128)(2,1)S(1)}, u32[]{:S(2)}, u32[]{:S(2)}) collective-permute-start(bf16[512,128]{1,0:T(8,128)(2,1)S(1)} %get-tuple-element.20.refs_4_.refs_0_), channel_id=1, source_target_pairs={{0,2},{1,3},{2,0},{3,1},{4,6},{5,7},{6,4},{7,5},{8,10},{9,11},{10,... | collective-permute-start | bytes 393224 | tf_op jit(solution)/shard_map/ppermute | solution.py:198
  12.6 7.7 %collective-permute-start.8 = (bf16[320,128]{1,0:T(8,128)(2,1)S(1)}, bf16[320,128]{1,0:T(8,128)(2,1)S(1)}, u32[]{:S(2)}, u32[]{:S(2)}) collective-permute-start(bf16[320,128]{1,0:T(8,128)(2,1)S(1)} %shard_map.88), channel_id=1, source_target_pairs={{0,6},{1,7},{2,4},{3,5},{4,2},{5,3},{6,0},{7,1},{8,14},{9,15},{10,... | collective-permute-start | bytes 245768 | tf_op jit(solution)/shard_map/ppermute | solution.py:198
  15.1 5.3 %collective-permute-start.7 = (bf16[320,128]{1,0:T(8,128)(2,1)S(1)}, bf16[320,128]{1,0:T(8,128)(2,1)S(1)}, u32[]{:S(2)}, u32[]{:S(2)}) collective-permute-start(bf16[320,128]{1,0:T(8,128)(2,1)S(1)} %shard_map.88), channel_id=1, source_target_pairs={{0,4},{1,5},{2,6},{3,7},{4,0},{5,1},{6,2},{7,3},{8,12},{9,13},{10,... | collective-permute-start | bytes 245768 | tf_op jit(solution)/shard_map/ppermute | solution.py:198
  15.7 4.8 %collective-permute-start.6 = (bf16[320,128]{1,0:T(8,128)(2,1)S(1)}, bf16[320,128]{1,0:T(8,128)(2,1)S(1)}, u32[]{:S(2)}, u32[]{:S(2)}) collective-permute-start(bf16[320,128]{1,0:T(8,128)(2,1)S(1)} %shard_map.88), channel_id=1, source_target_pairs={{0,2},{1,3},{2,0},{3,1},{4,6},{5,7},{6,4},{7,5},{8,10},{9,11},{10,... | collective-permute-start | bytes 245768 | tf_op jit(solution)/shard_map/ppermute | solution.py:198
  18.8 2.1 %collective-permute-start.10 = (bf16[2048,128]{1,0:T(8,128)(2,1)S(1)}, bf16[2048,128]{1,0:T(8,128)(2,1)S(1)}, u32[]{:S(2)}, u32[]{:S(2)}) collective-permute-start(bf16[2048,128]{1,0:T(8,128)(2,1)S(1)} %pad_maximum_fusion), channel_id=1, source_target_pairs={{0,1},{1,0},{2,3},{3,2},{4,5},{5,4},{6,7},{7,6},{8,9},{9,8},{10,11... | collective-permute-start | bytes 1572872 | tf_op jit(solution)/shard_map/ppermute | solution.py:198
  20.6 1.7 %collective-permute-start.9 = (bf16[1280,128]{1,0:T(8,128)(2,1)S(1)}, bf16[1280,128]{1,0:T(8,128)(2,1)S(1)}, u32[]{:S(2)}, u32[]{:S(2)}) collective-permute-start(bf16[1280,128]{1,0:T(8,128)(2,1)S(1)} %pad_maximum_fusion.1.totals_ref), channel_id=1, source_target_pairs={{0,1},{1,0},{2,3},{3,2},{4,5},{5,4},{6,7},{7,6},{8,9},{9,8},{10,11... | collective-permute-start | bytes 983048 | tf_op jit(solution)/shard_map/ppermute | solution.py:198
  23.5 5.4 %collective-permute-start.11 = (f32[4,64]{1,0:T(4,128)S(1)}, f32[4,64]{1,0:T(4,128)S(1)}, u32[]{:S(2)}, u32[]{:S(2)}) collective-permute-start(f32[4,64]{1,0:T(4,128)S(1)} %get-tuple-element.32), channel_id=1, source_target_pairs={{0,8},{1,9},{2,10},{3,11},{4,12},{5,13},{6,14},{7,15},{8,16},{9,17... | collective-permute-start | bytes 3080 | tf_op jit(solution)/shard_map/ppermute | solution.py:195
  24.2 5.3 %copy-start = (s32[4,64]{1,0:T(4,128)S(1)}, s32[4,64]{1,0:T(4,128)}, u32[]{:S(2)}) copy-start(s32[4,64]{1,0:T(4,128)} %candidates_ref.1) | copy-start | bytes 3076
  24.2 4.7 %collective-permute-start.12 = (f32[4,64]{1,0:T(4,128)S(1)}, f32[4,64]{1,0:T(4,128)S(1)}, u32[]{:S(2)}, u32[]{:S(2)}) collective-permute-start(f32[4,64]{1,0:T(4,128)S(1)} %get-tuple-element.33), channel_id=1, source_target_pairs={{0,16},{1,17},{2,18},{3,19},{4,20},{5,21},{6,22},{7,23},{8,24},{9,... | collective-permute-start | bytes 3080 | tf_op jit(solution)/shard_map/ppermute | solution.py:195
  25.8 3.8 %collective-permute-start.13 = (f32[4,64]{1,0:T(4,128)S(1)}, f32[4,64]{1,0:T(4,128)S(1)}, u32[]{:S(2)}, u32[]{:S(2)}) collective-permute-start(f32[4,64]{1,0:T(4,128)S(1)} %get-tuple-element.34), channel_id=1, source_target_pairs={{0,24},{1,25},{2,26},{3,27},{4,28},{5,29},{6,30},{7,31},{8,0},{9,1... | collective-permute-start | bytes 3080 | tf_op jit(solution)/shard_map/ppermute | solution.py:195

commit v4 on v3

--- a/solution.py
+++ b/solution.py
@@ -10,7 +10,6 @@
 BANK_BITS = 3
 HIGHEST = lax.Precision.HIGHEST
 BF16, F32, I32 = jnp.bfloat16, jnp.float32, jnp.int32
-COST = 10**9
 VMEM_BYTES = 48 * 1024 * 1024
 
 
@@ -88,19 +87,20 @@
     me = lax.axis_index("shard")
     number, clusters = weight_ref.shape
     each = number // len(slots)
-    for s, slot in enumerate(slots):
-        base = (me % bank + (me // bank + slot) % len(slots) * bank) * each
-        fb_ref[s * each : (s + 1) * each, :] = feedback_ref[pl.ds(base, each), :]
-        weight_ref[s * each : (s + 1) * each, :] = idf_ref[pl.ds(base, each), :].astype(F32) / (8.0 * clusters)
-    wanted = relative(fb_ref[...], me, count, bank, len(slots))
     block, row = parts(iota((1, near_ref.shape[1]), 1), 2 * clusters * count)
     block, column = parts(block, len(slots))
     kind, within = parts(jnp.where(row < clusters * count, row, row - clusters * count), count)
-    owner = 2 * block
+    owner = (bank - 2 * block) % bank
     for s, slot in enumerate(slots):
         owner = jnp.where(column == s, owner + slot * bank, owner)
-    for half, picks_ref in enumerate((near_ref, far_ref)):
-        place = (owner ^ half) * count + within
+    place = owner * count + within
+    for core, picks_ref in enumerate((near_ref, far_ref)):
+        for s, slot in enumerate(slots):
+            base = ((me ^ core) % bank + (me // bank + slot) % len(slots) * bank) * each
+            fb_ref[s * each : (s + 1) * each, :] = feedback_ref[pl.ds(base, each), :]
+            if core == 0:
+                weight_ref[s * each : (s + 1) * each, :] = idf_ref[pl.ds(base, each), :].astype(F32) / (8.0 * clusters)
+        wanted = relative(fb_ref[...], me, count, bank, len(slots))
         times = jnp.zeros((number, place.shape[1]), F32)
         for k in range(wanted.shape[1]):
             times = times + jnp.where(wanted[:, k : k + 1] == place, 1.0, 0.0)
@@ -125,11 +125,11 @@
 
 
 def expand_kernel(
-    count, tokens, places, near_pooled_ref, far_ref, far_picks_ref, spread_ref, near_plain_ref, far_plain_ref, *refs
+    count, tokens, places, near_pooled_ref, far_pooled_ref, spread_ref, near_plain_ref, far_plain_ref, *refs
 ):
     outputs = len(places)
     document_refs, out_refs = refs[:-outputs], refs[-outputs:]
-    pooled = near_pooled_ref[...] + jnp.dot(far_picks_ref[...], far_ref[...], preferred_element_type=F32)
+    pooled = near_pooled_ref[...] + far_pooled_ref[...]
     factor = lax.rsqrt(jnp.mean(pooled * pooled, axis=-1, keepdims=True) + 1e-06)
     expansion = (pooled * factor).astype(BF16)
     best = best_rows(document_refs, expansion, count, tokens)
@@ -149,7 +149,8 @@
     place = relative(candidates_ref[...], me, count, bank, len(places))
     owner, within = place // count % (width // count), place % count
     half = width // 2
-    place = place // width * width + (owner & 1) * half + (owner >> 1) * count + within
+    block = (bank - owner // 2 * 2) % bank // 2
+    place = place // width * width + owner % 2 * half + block * count + within
     rows, lanes = -(-given // 8) * 8, -(-wanted // 128) * 128
     place = jnp.pad(place, ((0, rows - given), (0, lanes - wanted)))
     for side, out_ref in enumerate((first_ref, final_ref)):
@@ -212,9 +213,10 @@
             pltpu.SemaphoreType.DMA((4,)),
         ],
     )
-    slots = list(range(columns))
+    slots = [0, columns - 1] + list(range(1, columns - 1))
     gathered = [payload] + [shift(payload, -s) for s in slots[1:]]
-    documents = [masked] + [swap(masked, m) for m in range(2, bank, 2)]
+    near = [(bank - 2 * b) % bank for b in range(bank // 2)]
+    documents = [masked] + [swap(masked, m) for m in near[1:]]
     far_documents = swap(jnp.concatenate(documents, axis=0), 1)
     half = bank * count // 2
     plain = functools.partial(plain_kernel, count, tokens, query_tokens, query_rows, columns)
@@ -233,20 +235,20 @@
         functools.partial(totals_kernel, query_rows),
         sds((columns * total_rows, features), BF16),
         *gathered,
-        cost=pl.CostEstimate(flops=COST, bytes_accessed=0, transcendentals=0),
-    )
-    ready, *others = lax.optimization_barrier((ready, *[swap(own, m) for m in range(2, bank, 2)]))
+        cost=pl.CostEstimate(flops=10**9, bytes_accessed=0, transcendentals=0),
+    )
+    ready, *others = lax.optimization_barrier((ready, *[swap(own, m) for m in near[1:]]))
     near_plain, near_picks, far_picks, spread = ready
-    near = jnp.concatenate([own, *others], axis=0)
-    far = swap(near, 1)
-    near_pooled = call(pool_kernel, sds((clusters * number, features), F32), near_picks, near)
-    returns = slots[1:] + slots[:1]
+    totals = jnp.concatenate([own, *others], axis=0)
+    pooled_shape = sds((clusters * number, features), F32)
+    far_pooled = swap(call(pool_kernel, pooled_shape, far_picks, totals, cost=pl.CostEstimate(flops=3 * 10**9, bytes_accessed=0, transcendentals=0)), 1)
+    near_pooled = call(pool_kernel, pooled_shape, near_picks, totals)
+    returns = list(range(1, columns)) + [0]
     blocks = call(
         functools.partial(expand_kernel, count, tokens, [slots.index(m) for m in returns]),
         [sds((each, 2 * bank * count), F32)] * columns,
         near_pooled,
-        far,
-        far_picks,
+        far_pooled,
         spread,
         near_plain,
         far_plain,

time: 30.4 us -> 29.8 us (0.980)
  starting transfers between devices: 19.4 us -> 18.8 us
    ppermute x8, starting transfers between devices: 8.51 us -> 7.57 us  [swap(): return lax.ppermute(x, 'shard', [(i, i ^ m) for i in range(devices)])]
    ppermute x6, starting transfers between devices: 10.9 us -> 11.2 us  [shift(): lax.ppermute(x, 'shard', [(i, (i + s * bank) % devices) for i in range(de...]
    pallas_call x7 -> x8, Pallas kernels: 5.29 us -> 5.35 us  [call(): pl.pallas_call(kernel, out_shape=out_shape, in_specs=specs or [pl.BlockSp...]
  transfers between devices with their start and end apart: 14 -> 14, of which waited for: 9 -> 9; matrix products, arithmetic and copies ran while one was open for 1% -> 1% of each run, Pallas kernels for 7% -> 8%
where the time goes in v4:
time: 29.8 us; the launch traced here: 29.6 us
  starting transfers between devices  18.8 us (63%)
  Pallas kernels  5.35 us (18%)
  waiting for transfers between devices  4.49 us (15%)
  between operations  0.72 us (2%)
    ppermute x6, starting transfers between devices, shift(): lax.ppermute(x, 'shard', [(i, (i + s * bank) % devices) for i in range(de...  11.2 us
    ppermute x8, starting transfers between devices, swap(): return lax.ppermute(x, 'shard', [(i, i ^ m) for i in range(devices)])  7.57 us
    pallas_call x8, Pallas kernels, call(): pl.pallas_call(kernel, out_shape=out_shape, in_specs=specs or [pl.BlockSp...  5.35 us
    ppermute x8, waiting for transfers between devices, swap(): return lax.ppermute(x, 'shard', [(i, i ^ m) for i in range(devices)])  2.45 us
    ppermute x6, waiting for transfers between devices, shift(): lax.ppermute(x, 'shard', [(i, (i + s * bank) % devices) for i in range(de...  2.03 us
  transfers between devices with their start and end apart: 14, of which 9 were waited for; matrix products, arithmetic and copies ran while one was open for 1% of the time, Pallas kernels for 8%

profile of v4, /device:TPU:0, one launch (start us, length us, event | category | flops | bytes accessed | tf_op | source)
XLA Modules:
  0.0 29.6 jit_solution(5557927392720508769)
XLA Ops:
  0.6 0.0 copy-start.1
  0.6 1.2 %shard_map.86 = (bf16[208,128]{1,0:T(8,128)(2,1)S(1)}, bf16[512,128]{1,0:T(8,128)(2,1)S(1)}) custom-call(s32[1,4]{1,0:T(1,128)} %bitcast.3, bf16[128,128]{1,0:T(8,128)(2,1)} %bitcast.2, bf16[4,128,128]{2,1,0:T(8,128)(2,1)} %passages_hbm, s32[4,128]{1,0:T(4,128)} %labels_hbm.1), custom_call_target="tpu_custom_call" | custom-call | tf_op jit(solution)/shard_map/pallas_call | solution.py:173
  1.8 3.1 %collective-permute-start = (bf16[208,128]{1,0:T(8,128)(2,1)S(1)}, bf16[208,128]{1,0:T(8,128)(2,1)S(1)}, u32[]{:S(2)}, u32[]{:S(2)}) collective-permute-start(bf16[208,128]{1,0:T(8,128)(2,1)S(1)} %get-tuple-element.19.refs_0_), channel_id=1, source_target_pairs={{0,8},{1,9},{2,10},{3,11},{4,12},{5,13},{6,14},{7,15},{8,16},{9,17... | collective-permute-start | bytes 159752 | tf_op jit(solution)/shard_map/ppermute | solution.py:196
  4.9 2.1 %collective-permute-start.1 = (bf16[208,128]{1,0:T(8,128)(2,1)S(1)}, bf16[208,128]{1,0:T(8,128)(2,1)S(1)}, u32[]{:S(2)}, u32[]{:S(2)}) collective-permute-start(bf16[208,128]{1,0:T(8,128)(2,1)S(1)} %get-tuple-element.19.refs_0_), channel_id=1, source_target_pairs={{0,24},{1,25},{2,26},{3,27},{4,28},{5,29},{6,30},{7,31},{8,0},{9,1... | collective-permute-start | bytes 159752 | tf_op jit(solution)/shard_map/ppermute | solution.py:196
  7.0 0.9 %collective-permute-start.2 = (bf16[208,128]{1,0:T(8,128)(2,1)S(1)}, bf16[208,128]{1,0:T(8,128)(2,1)S(1)}, u32[]{:S(2)}, u32[]{:S(2)}) collective-permute-start(bf16[208,128]{1,0:T(8,128)(2,1)S(1)} %get-tuple-element.19.refs_0_), channel_id=1, source_target_pairs={{0,16},{1,17},{2,18},{3,19},{4,20},{5,21},{6,22},{7,23},{8,24},{9,... | collective-permute-start | bytes 159752 | tf_op jit(solution)/shard_map/ppermute | solution.py:196
  7.9 0.0 copy-start.2
  7.9 2.4 %collective-permute-start.3 = (bf16[512,128]{1,0:T(8,128)(2,1)S(1)}, bf16[512,128]{1,0:T(8,128)(2,1)S(1)}, u32[]{:S(2)}, u32[]{:S(2)}) collective-permute-start(bf16[512,128]{1,0:T(8,128)(2,1)S(1)} %get-tuple-element.20.refs_4_.refs_0_), channel_id=1, source_target_pairs={{0,6},{1,7},{2,4},{3,5},{4,2},{5,3},{6,0},{7,1},{8,14},{9,15},{10,... | collective-permute-start | bytes 393224 | tf_op jit(solution)/shard_map/ppermute | solution.py:199
  10.4 0.5 %collective-permute-start.4 = (bf16[512,128]{1,0:T(8,128)(2,1)S(1)}, bf16[512,128]{1,0:T(8,128)(2,1)S(1)}, u32[]{:S(2)}, u32[]{:S(2)}) collective-permute-start(bf16[512,128]{1,0:T(8,128)(2,1)S(1)} %get-tuple-element.20.refs_4_.refs_0_), channel_id=1, source_target_pairs={{0,4},{1,5},{2,6},{3,7},{4,0},{5,1},{6,2},{7,3},{8,12},{9,13},{10,... | collective-permute-start | bytes 393224 | tf_op jit(solution)/shard_map/ppermute | solution.py:199
  10.9 0.0 collective-permute-done.refs_1_
  10.9 0.5 %collective-permute-start.5 = (bf16[512,128]{1,0:T(8,128)(2,1)S(1)}, bf16[512,128]{1,0:T(8,128)(2,1)S(1)}, u32[]{:S(2)}, u32[]{:S(2)}) collective-permute-start(bf16[512,128]{1,0:T(8,128)(2,1)S(1)} %get-tuple-element.20.refs_4_.refs_0_), channel_id=1, source_target_pairs={{0,2},{1,3},{2,0},{3,1},{4,6},{5,7},{6,4},{7,5},{8,10},{9,11},{10,... | collective-permute-start | bytes 393224 | tf_op jit(solution)/shard_map/ppermute | solution.py:199
  11.4 0.0 copy-done.1
  11.4 0.1 copy.10.idf_ref
  11.6 0.0 copy-done.2
  11.6 0.1 copy.9.feedback_ref
  11.7 0.0 collective-permute-done.1.refs_2_
  11.7 0.7 %collective-permute-done.2.refs_3_ = bf16[208,128]{1,0:T(8,128)(2,1)S(1)} collective-permute-done((bf16[208,128]{1,0:T(8,128)(2,1)S(1)}, bf16[208,128]{1,0:T(8,128)(2,1)S(1)}, u32[]{:S(2)}, u32[]{:S(2)}) %collective-permute-start.2) | collective-permute-done | bytes 53280 | tf_op jit(solution)/shard_map/ppermute | solution.py:196
  12.3 2.5 %collective-permute-start.6 = (bf16[320,128]{1,0:T(8,128)(2,1)S(1)}, bf16[320,128]{1,0:T(8,128)(2,1)S(1)}, u32[]{:S(2)}, u32[]{:S(2)}) collective-permute-start(bf16[320,128]{1,0:T(8,128)(2,1)S(1)} %shard_map.88), channel_id=1, source_target_pairs={{0,6},{1,7},{2,4},{3,5},{4,2},{5,3},{6,0},{7,1},{8,14},{9,15},{10,... | collective-permute-start | bytes 245768 | tf_op jit(solution)/shard_map/ppermute | solution.py:199
  14.8 0.5 %collective-permute-start.7 = (bf16[320,128]{1,0:T(8,128)(2,1)S(1)}, bf16[320,128]{1,0:T(8,128)(2,1)S(1)}, u32[]{:S(2)}, u32[]{:S(2)}) collective-permute-start(bf16[320,128]{1,0:T(8,128)(2,1)S(1)} %shard_map.88), channel_id=1, source_target_pairs={{0,4},{1,5},{2,6},{3,7},{4,0},{5,1},{6,2},{7,3},{8,12},{9,13},{10,... | collective-permute-start | bytes 245768 | tf_op jit(solution)/shard_map/ppermute | solution.py:199
  15.3 0.0 collective-permute-done.3.refs_5_.refs_1_
  15.3 1.0 %collective-permute-start.8 = (bf16[320,128]{1,0:T(8,128)(2,1)S(1)}, bf16[320,128]{1,0:T(8,128)(2,1)S(1)}, u32[]{:S(2)}, u32[]{:S(2)}) collective-permute-start(bf16[320,128]{1,0:T(8,128)(2,1)S(1)} %shard_map.88), channel_id=1, source_target_pairs={{0,2},{1,3},{2,0},{3,1},{4,6},{5,7},{6,4},{7,5},{8,10},{9,11},{10,... | collective-permute-start | bytes 245768 | tf_op jit(solution)/shard_map/ppermute | solution.py:199
  16.3 1.0 %collective-permute-done.4.refs_6_.refs_2_ = bf16[512,128]{1,0:T(8,128)(2,1)S(1)} collective-permute-done((bf16[512,128]{1,0:T(8,128)(2,1)S(1)}, bf16[512,128]{1,0:T(8,128)(2,1)S(1)}, u32[]{:S(2)}, u32[]{:S(2)}) %collective-permute-start.4) | collective-permute-done | bytes 131104 | tf_op jit(solution)/shard_map/ppermute | solution.py:199
  17.2 0.0 collective-permute-done.5.refs_7_.refs_3_
  17.3 0.1 collective-permute-start.10
  17.4 1.0 %shard_map.87 = (f32[16,16]{1,0:T(8,128)S(1)}, bf16[160,1280]{1,0:T(8,128)(2,1)S(1)}, bf16[160,1280]{1,0:T(8,128)(2,1)S(1)}, f32[16,160]{1,0:T(8,128)S(1)}) custom-call(s32[128,3]{1,0:T(8,128)S(1)} %copy.9.feedback_ref, s32[128,10]{1,0:T(8,128)S(1)} %copy.10.idf_ref, bf16[208,128]{1,0:T(8,128)(2,1)S(1)} %get-tuple-element.19.refs_0_, ...), custom_call_target="tpu_custom_call" | custom-call | tf_op jit(solution)/shard_map/pallas_call | solution.py:173
  18.4 0.7 %collective-permute-done.6 = bf16[320,128]{1,0:T(8,128)(2,1)S(1)} collective-permute-done((bf16[320,128]{1,0:T(8,128)(2,1)S(1)}, bf16[320,128]{1,0:T(8,128)(2,1)S(1)}, u32[]{:S(2)}, u32[]{:S(2)}) %collective-permute-start.6) | collective-permute-done | bytes 81952 | tf_op jit(solution)/shard_map/ppermute | solution.py:199
  19.1 0.5 %collective-permute-done.7 = bf16[320,128]{1,0:T(8,128)(2,1)S(1)} collective-permute-done((bf16[320,128]{1,0:T(8,128)(2,1)S(1)}, bf16[320,128]{1,0:T(8,128)(2,1)S(1)}, u32[]{:S(2)}, u32[]{:S(2)}) %collective-permute-start.7) | collective-permute-done | bytes 81952 | tf_op jit(solution)/shard_map/ppermute | solution.py:199
  19.6 0.1 collective-permute-done.8
  19.8 0.3 shard_map.90
  20.1 0.1 collective-permute-start.9
  20.1 0.3 shard_map.89.near_pooled_ref
  20.4 0.0 collective-permute-done.10.refs_4_
  20.4 0.9 %shard_map.91.far_plain_ref = f32[16,16]{1,0:T(8,128)S(1)} custom-call(bf16[208,128]{1,0:T(8,128)(2,1)S(1)} %get-tuple-element.19.refs_0_, bf16[208,128]{1,0:T(8,128)(2,1)S(1)} %collective-permute-done.refs_1_, bf16[208,128]{1,0:T(8,128)(2,1)S(1)} %collective-permute-done.1.refs_2_, bf16[208,128]{1,0:T(8,128)(2,1)S(1)} %collective-permute-done.2.refs_3_, ...), custom_call_target="tpu_custom_call" | custom-call | tf_op jit(solution)/shard_map/pallas_call | solution.py:173
  21.3 0.1 collective-permute-done.9.far_pooled_ref
  21.4 1.0 %shard_map.92 = (f32[4,64]{1,0:T(4,128)S(1)}, f32[4,64]{1,0:T(4,128)S(1)}, f32[4,64]{1,0:T(4,128)S(1)}, f32[4,64]{1,0:T(4,128)S(1)}) custom-call(f32[160,128]{1,0:T(8,128)S(1)} %shard_map.89.near_pooled_ref, f32[160,128]{1,0:T(8,128)S(1)} %collective-permute-done.9.far_pooled_ref, f32[16,160]{1,0:T(8,128)S(1)} %get-tuple-element.30.spread_ref, ...), custom_call_target="tpu_custom_call" | custom-call | tf_op jit(solution)/shard_map/pallas_call | solution.py:173
  22.4 1.5 %collective-permute-start.11 = (f32[4,64]{1,0:T(4,128)S(1)}, f32[4,64]{1,0:T(4,128)S(1)}, u32[]{:S(2)}, u32[]{:S(2)}) collective-permute-start(f32[4,64]{1,0:T(4,128)S(1)} %get-tuple-element.32), channel_id=1, source_target_pairs={{0,8},{1,9},{2,10},{3,11},{4,12},{5,13},{6,14},{7,15},{8,16},{9,17... | collective-permute-start | bytes 3080 | tf_op jit(solution)/shard_map/ppermute | solution.py:196
  23.9 0.0 copy-start
  23.9 1.4 %collective-permute-start.12 = (f32[4,64]{1,0:T(4,128)S(1)}, f32[4,64]{1,0:T(4,128)S(1)}, u32[]{:S(2)}, u32[]{:S(2)}) collective-permute-start(f32[4,64]{1,0:T(4,128)S(1)} %get-tuple-element.33), channel_id=1, source_target_pairs={{0,16},{1,17},{2,18},{3,19},{4,20},{5,21},{6,22},{7,23},{8,24},{9,... | collective-permute-start | bytes 3080 | tf_op jit(solution)/shard_map/ppermute | solution.py:196
  25.3 2.2 %collective-permute-start.13 = (f32[4,64]{1,0:T(4,128)S(1)}, f32[4,64]{1,0:T(4,128)S(1)}, u32[]{:S(2)}, u32[]{:S(2)}) collective-permute-start(f32[4,64]{1,0:T(4,128)S(1)} %get-tuple-element.34), channel_id=1, source_target_pairs={{0,24},{1,25},{2,26},{3,27},{4,28},{5,29},{6,30},{7,31},{8,0},{9,1... | collective-permute-start | bytes 3080 | tf_op jit(solution)/shard_map/ppermute | solution.py:196
  27.5 0.3 %collective-permute-done.11.refs_0_ = f32[4,64]{1,0:T(4,128)S(1)} collective-permute-done((f32[4,64]{1,0:T(4,128)S(1)}, f32[4,64]{1,0:T(4,128)S(1)}, u32[]{:S(2)}, u32[]{:S(2)}) %collective-permute-start.11) | collective-permute-done | bytes 1056 | tf_op jit(solution)/shard_map/ppermute | solution.py:196
  27.8 0.6 %collective-permute-done.12.refs_1_ = f32[4,64]{1,0:T(4,128)S(1)} collective-permute-done((f32[4,64]{1,0:T(4,128)S(1)}, f32[4,64]{1,0:T(4,128)S(1)}, u32[]{:S(2)}, u32[]{:S(2)}) %collective-permute-start.12) | collective-permute-done | bytes 1056 | tf_op jit(solution)/shard_map/ppermute | solution.py:196
  28.4 0.5 %collective-permute-done.13.refs_2_ = f32[4,64]{1,0:T(4,128)S(1)} collective-permute-done((f32[4,64]{1,0:T(4,128)S(1)}, f32[4,64]{1,0:T(4,128)S(1)}, u32[]{:S(2)}, u32[]{:S(2)}) %collective-permute-start.13) | collective-permute-done | bytes 1056 | tf_op jit(solution)/shard_map/ppermute | solution.py:196
  28.9 0.0 copy-done
  28.9 0.7 %shard_map.93 = (f32[4,64]{1,0:T(4,128)}, f32[4,64]{1,0:T(4,128)}) custom-call(s32[4,64]{1,0:T(4,128)S(1)} %copy-done, f32[4,64]{1,0:T(4,128)S(1)} %collective-permute-done.11.refs_0_, f32[4,64]{1,0:T(4,128)S(1)} %collective-permute-done.12.refs_1_, f32[4,64]{1,0:T(4,128)S(1)} %collective-permute-done.13.refs_2_, f32[4,64]{1,0:T(4,128)S(1)} %get-tuple-element.35.refs_3_), custom_call_target="tpu_custom_call" | custom-call | tf_op jit(solution)/shard_map/pallas_call | solution.py:173
  (3 shorter events, 0.1 us)
Async XLA Ops:
  0.6 10.8 %copy-start.1 = (s32[128,10]{0,1:T(8,128)S(1)}, s32[128,10]{0,1:T(8,128)}, u32[]{:S(2)}) copy-start(s32[128,10]{0,1:T(8,128)} %param.13) | copy-start | bytes 15364
  1.8 9.1 %collective-permute-start = (bf16[208,128]{1,0:T(8,128)(2,1)S(1)}, bf16[208,128]{1,0:T(8,128)(2,1)S(1)}, u32[]{:S(2)}, u32[]{:S(2)}) collective-permute-start(bf16[208,128]{1,0:T(8,128)(2,1)S(1)} %get-tuple-element.19.refs_0_), channel_id=1, source_target_pairs={{0,8},{1,9},{2,10},{3,11},{4,12},{5,13},{6,14},{7,15},{8,16},{9,17... | collective-permute-start | bytes 159752 | tf_op jit(solution)/shard_map/ppermute | solution.py:196
  4.9 6.8 %collective-permute-start.1 = (bf16[208,128]{1,0:T(8,128)(2,1)S(1)}, bf16[208,128]{1,0:T(8,128)(2,1)S(1)}, u32[]{:S(2)}, u32[]{:S(2)}) collective-permute-start(bf16[208,128]{1,0:T(8,128)(2,1)S(1)} %get-tuple-element.19.refs_0_), channel_id=1, source_target_pairs={{0,24},{1,25},{2,26},{3,27},{4,28},{5,29},{6,30},{7,31},{8,0},{9,1... | collective-permute-start | bytes 159752 | tf_op jit(solution)/shard_map/ppermute | solution.py:196
  7.0 5.3 %collective-permute-start.2 = (bf16[208,128]{1,0:T(8,128)(2,1)S(1)}, bf16[208,128]{1,0:T(8,128)(2,1)S(1)}, u32[]{:S(2)}, u32[]{:S(2)}) collective-permute-start(bf16[208,128]{1,0:T(8,128)(2,1)S(1)} %get-tuple-element.19.refs_0_), channel_id=1, source_target_pairs={{0,16},{1,17},{2,18},{3,19},{4,20},{5,21},{6,22},{7,23},{8,24},{9,... | collective-permute-start | bytes 159752 | tf_op jit(solution)/shard_map/ppermute | solution.py:196
  7.9 3.6 %copy-start.2 = (s32[128,3]{0,1:T(4,128)S(1)}, s32[128,3]{0,1:T(4,128)}, u32[]{:S(2)}) copy-start(s32[128,3]{0,1:T(4,128)} %param.12) | copy-start | bytes 4612
  7.9 7.4 %collective-permute-start.3 = (bf16[512,128]{1,0:T(8,128)(2,1)S(1)}, bf16[512,128]{1,0:T(8,128)(2,1)S(1)}, u32[]{:S(2)}, u32[]{:S(2)}) collective-permute-start(bf16[512,128]{1,0:T(8,128)(2,1)S(1)} %get-tuple-element.20.refs_4_.refs_0_), channel_id=1, source_target_pairs={{0,6},{1,7},{2,4},{3,5},{4,2},{5,3},{6,0},{7,1},{8,14},{9,15},{10,... | collective-permute-start | bytes 393224 | tf_op jit(solution)/shard_map/ppermute | solution.py:199
  10.4 6.9 %collective-permute-start.4 = (bf16[512,128]{1,0:T(8,128)(2,1)S(1)}, bf16[512,128]{1,0:T(8,128)(2,1)S(1)}, u32[]{:S(2)}, u32[]{:S(2)}) collective-permute-start(bf16[512,128]{1,0:T(8,128)(2,1)S(1)} %get-tuple-element.20.refs_4_.refs_0_), channel_id=1, source_target_pairs={{0,4},{1,5},{2,6},{3,7},{4,0},{5,1},{6,2},{7,3},{8,12},{9,13},{10,... | collective-permute-start | bytes 393224 | tf_op jit(solution)/shard_map/ppermute | solution.py:199
  10.9 6.3 %collective-permute-start.5 = (bf16[512,128]{1,0:T(8,128)(2,1)S(1)}, bf16[512,128]{1,0:T(8,128)(2,1)S(1)}, u32[]{:S(2)}, u32[]{:S(2)}) collective-permute-start(bf16[512,128]{1,0:T(8,128)(2,1)S(1)} %get-tuple-element.20.refs_4_.refs_0_), channel_id=1, source_target_pairs={{0,2},{1,3},{2,0},{3,1},{4,6},{5,7},{6,4},{7,5},{8,10},{9,11},{10,... | collective-permute-start | bytes 393224 | tf_op jit(solution)/shard_map/ppermute | solution.py:199
  12.3 6.8 %collective-permute-start.6 = (bf16[320,128]{1,0:T(8,128)(2,1)S(1)}, bf16[320,128]{1,0:T(8,128)(2,1)S(1)}, u32[]{:S(2)}, u32[]{:S(2)}) collective-permute-start(bf16[320,128]{1,0:T(8,128)(2,1)S(1)} %shard_map.88), channel_id=1, source_target_pairs={{0,6},{1,7},{2,4},{3,5},{4,2},{5,3},{6,0},{7,1},{8,14},{9,15},{10,... | collective-permute-start | bytes 245768 | tf_op jit(solution)/shard_map/ppermute | solution.py:199
  14.8 4.8 %collective-permute-start.7 = (bf16[320,128]{1,0:T(8,128)(2,1)S(1)}, bf16[320,128]{1,0:T(8,128)(2,1)S(1)}, u32[]{:S(2)}, u32[]{:S(2)}) collective-permute-start(bf16[320,128]{1,0:T(8,128)(2,1)S(1)} %shard_map.88), channel_id=1, source_target_pairs={{0,4},{1,5},{2,6},{3,7},{4,0},{5,1},{6,2},{7,3},{8,12},{9,13},{10,... | collective-permute-start | bytes 245768 | tf_op jit(solution)/shard_map/ppermute | solution.py:199
  15.3 4.4 %collective-permute-start.8 = (bf16[320,128]{1,0:T(8,128)(2,1)S(1)}, bf16[320,128]{1,0:T(8,128)(2,1)S(1)}, u32[]{:S(2)}, u32[]{:S(2)}) collective-permute-start(bf16[320,128]{1,0:T(8,128)(2,1)S(1)} %shard_map.88), channel_id=1, source_target_pairs={{0,2},{1,3},{2,0},{3,1},{4,6},{5,7},{6,4},{7,5},{8,10},{9,11},{10,... | collective-permute-start | bytes 245768 | tf_op jit(solution)/shard_map/ppermute | solution.py:199
  17.3 3.1 %collective-permute-start.10 = (bf16[2048,128]{1,0:T(8,128)(2,1)S(1)}, bf16[2048,128]{1,0:T(8,128)(2,1)S(1)}, u32[]{:S(2)}, u32[]{:S(2)}) collective-permute-start(bf16[2048,128]{1,0:T(8,128)(2,1)S(1)} %pad_maximum_fusion), channel_id=1, source_target_pairs={{0,1},{1,0},{2,3},{3,2},{4,5},{5,4},{6,7},{7,6},{8,9},{9,8},{10,11... | collective-permute-start | bytes 1572872 | tf_op jit(solution)/shard_map/ppermute | solution.py:199
  20.1 1.3 %collective-permute-start.9 = (f32[160,128]{1,0:T(8,128)S(1)}, f32[160,128]{1,0:T(8,128)S(1)}, u32[]{:S(2)}, u32[]{:S(2)}) collective-permute-start(f32[160,128]{1,0:T(8,128)S(1)} %shard_map.90), channel_id=1, source_target_pairs={{0,1},{1,0},{2,3},{3,2},{4,5},{5,4},{6,7},{7,6},{8,9},{9,8},{10,11... | collective-permute-start | bytes 245768 | tf_op jit(solution)/shard_map/ppermute | solution.py:199
  22.4 5.4 %collective-permute-start.11 = (f32[4,64]{1,0:T(4,128)S(1)}, f32[4,64]{1,0:T(4,128)S(1)}, u32[]{:S(2)}, u32[]{:S(2)}) collective-permute-start(f32[4,64]{1,0:T(4,128)S(1)} %get-tuple-element.32), channel_id=1, source_target_pairs={{0,8},{1,9},{2,10},{3,11},{4,12},{5,13},{6,14},{7,15},{8,16},{9,17... | collective-permute-start | bytes 3080 | tf_op jit(solution)/shard_map/ppermute | solution.py:196
  23.9 5.0 %copy-start = (s32[4,64]{1,0:T(4,128)S(1)}, s32[4,64]{1,0:T(4,128)}, u32[]{:S(2)}) copy-start(s32[4,64]{1,0:T(4,128)} %candidates_ref.1) | copy-start | bytes 3076
  23.9 4.5 %collective-permute-start.12 = (f32[4,64]{1,0:T(4,128)S(1)}, f32[4,64]{1,0:T(4,128)S(1)}, u32[]{:S(2)}, u32[]{:S(2)}) collective-permute-start(f32[4,64]{1,0:T(4,128)S(1)} %get-tuple-element.33), channel_id=1, source_target_pairs={{0,16},{1,17},{2,18},{3,19},{4,20},{5,21},{6,22},{7,23},{8,24},{9,... | collective-permute-start | bytes 3080 | tf_op jit(solution)/shard_map/ppermute | solution.py:196
  25.3 3.6 %collective-permute-start.13 = (f32[4,64]{1,0:T(4,128)S(1)}, f32[4,64]{1,0:T(4,128)S(1)}, u32[]{:S(2)}, u32[]{:S(2)}) collective-permute-start(f32[4,64]{1,0:T(4,128)S(1)} %get-tuple-element.34), channel_id=1, source_target_pairs={{0,24},{1,25},{2,26},{3,27},{4,28},{5,29},{6,30},{7,31},{8,0},{9,1... | collective-permute-start | bytes 3080 | tf_op jit(solution)/shard_map/ppermute | solution.py:196

commit v5 on v4

--- a/solution.py
+++ b/solution.py
@@ -22,7 +22,7 @@
 
 
 def prepare_kernel(
-    clusters, lengths_hbm, queries_hbm, passages_hbm, labels_hbm, payload_ref, masked_ref, lengths_ref, passages_ref, labels_ref, arrived
+    clusters, lengths_hbm, queries_hbm, passages_hbm, labels_hbm, payload_ref, passages_ref, lengths_ref, labels_ref, arrived
 ):
     query_rows = queries_hbm.shape[0]
     copies = [
@@ -34,21 +34,27 @@
     for copy in copies:
         copy.start()
     count, tokens, features = passages_ref.shape
+    for copy in copies[1:3]:
+        copy.wait()
+    chosen = []
+    for p in range(count):
+        target = jnp.where(iota((1, tokens), 1) < lengths_ref[0:1, p : p + 1], labels_ref[p : p + 1, :] * count + p, -1)
+        chosen.append((iota((clusters * count, tokens), 0) == target).astype(F32).astype(BF16))
+    copies[0].wait()
     totals = jnp.zeros((clusters * count, features), F32)
-    for copy in copies[:3]:
-        copy.wait()
     for p in range(count):
-        length = lengths_ref[0:1, p : p + 1]
-        document = passages_ref[p]
-        wide = document.astype(F32)
-        kept = jnp.where(iota((tokens, features), 0) < length, wide, wide[0:1, :])
-        masked_ref[p * tokens : (p + 1) * tokens, :] = kept.astype(BF16)
-        target = jnp.where(iota((1, tokens), 1) < length, labels_ref[p : p + 1, :] * count + p, -1)
-        chosen = (iota((clusters * count, tokens), 0) == target).astype(F32).astype(BF16)
-        totals = totals + jnp.dot(chosen, document, preferred_element_type=F32)
+        totals = totals + jnp.dot(chosen[p], passages_ref[p], preferred_element_type=F32)
     high = totals.astype(BF16).astype(F32)
     payload_ref[query_rows:, :] = jnp.concatenate([high, totals - high], axis=0).astype(BF16)
     copies[3].wait()
+
+
+def mask_kernel(passages_ref, lengths_ref, masked_ref):
+    count, tokens, features = passages_ref.shape
+    for p in range(count):
+        wide = passages_ref[p].astype(F32)
+        kept = jnp.where(iota((tokens, features), 0) < lengths_ref[0:1, p : p + 1], wide, wide[0:1, :])
+        masked_ref[p * tokens : (p + 1) * tokens, :] = kept.astype(BF16)
 
 
 def best_rows(document_refs, vectors, count, tokens):
@@ -198,21 +204,21 @@
     def swap(x, m):
         return lax.ppermute(x, "shard", [(i, i ^ m) for i in range(devices)])
 
-    payload, masked = call(
+    payload, loaded, ends = call(
         functools.partial(prepare_kernel, clusters),
-        (sds((query_rows + total_rows, features), BF16), sds((count * tokens, features), BF16)),
+        (
+            sds((query_rows + total_rows, features), BF16),
+            sds((count, tokens, features), BF16),
+            sds((1, count), I32),
+        ),
         *[
             pltpu.with_memory_space_constraint(x, pltpu.HBM)
             for x in (lengths.reshape(1, count), queries.reshape(query_rows, features), passages, labels)
         ],
         specs=[pl.BlockSpec(memory_space=pltpu.HBM)] * 4,
-        scratch=[
-            pltpu.VMEM((1, count), I32),
-            pltpu.VMEM((count, tokens, features), BF16),
-            pltpu.VMEM((count, tokens), I32),
-            pltpu.SemaphoreType.DMA((4,)),
-        ],
-    )
+        scratch=[pltpu.VMEM((count, tokens), I32), pltpu.SemaphoreType.DMA((4,))],
+    )
+    masked = call(mask_kernel, sds((count * tokens, features), BF16), loaded, ends)
     slots = [0, columns - 1] + list(range(1, columns - 1))
     gathered = [payload] + [shift(payload, -s) for s in slots[1:]]
     near = [(bank - 2 * b) % bank for b in range(bank // 2)]

time: 29.8 us -> 29.8 us (level)
  waiting for transfers between devices: 4.49 us -> 4.13 us
  starting transfers between devices: 18.8 us -> 19.1 us
    pallas_call x8 -> x9, Pallas kernels: 5.35 us -> 5.39 us  [call(): pl.pallas_call(kernel, out_shape=out_shape, in_specs=specs or [pl.BlockSp...]
  transfers between devices with their start and end apart: 14 -> 14, of which waited for: 9 -> 8; matrix products, arithmetic and copies ran while one was open for 1% -> 1% of each run, Pallas kernels for 8% -> 9%
where the time goes in v5:
time: 29.8 us; the launch traced here: 29.7 us
  starting transfers between devices  19.1 us (64%)
  Pallas kernels  5.39 us (18%)
  waiting for transfers between devices  4.13 us (14%)
  between operations  0.72 us (2%)
    ppermute x6, starting transfers between devices, shift(): lax.ppermute(x, 'shard', [(i, (i + s * bank) % devices) for i in range(de...  11.3 us
    ppermute x8, starting transfers between devices, swap(): return lax.ppermute(x, 'shard', [(i, i ^ m) for i in range(devices)])  7.82 us
    pallas_call x9, Pallas kernels, call(): pl.pallas_call(kernel, out_shape=out_shape, in_specs=specs or [pl.BlockSp...  5.39 us
    ppermute x8, waiting for transfers between devices, swap(): return lax.ppermute(x, 'shard', [(i, i ^ m) for i in range(devices)])  2.35 us
    ppermute x6, waiting for transfers between devices, shift(): lax.ppermute(x, 'shard', [(i, (i + s * bank) % devices) for i in range(de...  1.78 us
  transfers between devices with their start and end apart: 14, of which 8 were waited for; matrix products, arithmetic and copies ran while one was open for 1% of the time, Pallas kernels for 9%

profile of v5, /device:TPU:0, one launch (start us, length us, event | category | flops | bytes accessed | tf_op | source)
XLA Modules:
  0.0 29.7 jit_solution(14728433586454042706)
XLA Ops:
  0.6 1.1 %shard_map.86 = (bf16[208,128]{1,0:T(8,128)(2,1)S(1)}, bf16[4,128,128]{2,1,0:T(8,128)(2,1)S(1)}, s32[1,4]{1,0:T(1,128)S(1)}) custom-call(s32[1,4]{1,0:T(1,128)} %bitcast.3, bf16[128,128]{1,0:T(8,128)(2,1)} %bitcast.2, bf16[4,128,128]{2,1,0:T(8,128)(2,1)} %passages_hbm, s32[4,128]{1,0:T(4,128)} %labels_hbm.1), custom_call_target="tpu_custom_call" | custom-call | tf_op jit(solution)/shard_map/pallas_call | solution.py:179
  1.8 3.1 %collective-permute-start = (bf16[208,128]{1,0:T(8,128)(2,1)S(1)}, bf16[208,128]{1,0:T(8,128)(2,1)S(1)}, u32[]{:S(2)}, u32[]{:S(2)}) collective-permute-start(bf16[208,128]{1,0:T(8,128)(2,1)S(1)} %get-tuple-element.20.refs_0_), channel_id=1, source_target_pairs={{0,8},{1,9},{2,10},{3,11},{4,12},{5,13},{6,14},{7,15},{8,16},{9,17... | collective-permute-start | bytes 159752 | tf_op jit(solution)/shard_map/ppermute | solution.py:202
  4.8 2.1 %collective-permute-start.1 = (bf16[208,128]{1,0:T(8,128)(2,1)S(1)}, bf16[208,128]{1,0:T(8,128)(2,1)S(1)}, u32[]{:S(2)}, u32[]{:S(2)}) collective-permute-start(bf16[208,128]{1,0:T(8,128)(2,1)S(1)} %get-tuple-element.20.refs_0_), channel_id=1, source_target_pairs={{0,24},{1,25},{2,26},{3,27},{4,28},{5,29},{6,30},{7,31},{8,0},{9,1... | collective-permute-start | bytes 159752 | tf_op jit(solution)/shard_map/ppermute | solution.py:202
  6.9 0.9 %collective-permute-start.2 = (bf16[208,128]{1,0:T(8,128)(2,1)S(1)}, bf16[208,128]{1,0:T(8,128)(2,1)S(1)}, u32[]{:S(2)}, u32[]{:S(2)}) collective-permute-start(bf16[208,128]{1,0:T(8,128)(2,1)S(1)} %get-tuple-element.20.refs_0_), channel_id=1, source_target_pairs={{0,16},{1,17},{2,18},{3,19},{4,20},{5,21},{6,22},{7,23},{8,24},{9,... | collective-permute-start | bytes 159752 | tf_op jit(solution)/shard_map/ppermute | solution.py:202
  7.9 0.0 copy-start.2
  7.9 0.1 shard_map.87.refs_4_.refs_0_
  8.0 0.0 copy-start.1
  8.0 2.5 %collective-permute-start.3 = (bf16[512,128]{1,0:T(8,128)(2,1)S(1)}, bf16[512,128]{1,0:T(8,128)(2,1)S(1)}, u32[]{:S(2)}, u32[]{:S(2)}) collective-permute-start(bf16[512,128]{1,0:T(8,128)(2,1)S(1)} %shard_map.87.refs_4_.refs_0_), channel_id=1, source_target_pairs={{0,6},{1,7},{2,4},{3,5},{4,2},{5,3},{6,0},{7,1},{8,14},{9,15},{10,... | collective-permute-start | bytes 393224 | tf_op jit(solution)/shard_map/ppermute | solution.py:205
  10.5 0.5 %collective-permute-start.4 = (bf16[512,128]{1,0:T(8,128)(2,1)S(1)}, bf16[512,128]{1,0:T(8,128)(2,1)S(1)}, u32[]{:S(2)}, u32[]{:S(2)}) collective-permute-start(bf16[512,128]{1,0:T(8,128)(2,1)S(1)} %shard_map.87.refs_4_.refs_0_), channel_id=1, source_target_pairs={{0,4},{1,5},{2,6},{3,7},{4,0},{5,1},{6,2},{7,3},{8,12},{9,13},{10,... | collective-permute-start | bytes 393224 | tf_op jit(solution)/shard_map/ppermute | solution.py:205
  11.0 0.0 collective-permute-done.refs_1_
  11.0 0.5 %collective-permute-start.5 = (bf16[512,128]{1,0:T(8,128)(2,1)S(1)}, bf16[512,128]{1,0:T(8,128)(2,1)S(1)}, u32[]{:S(2)}, u32[]{:S(2)}) collective-permute-start(bf16[512,128]{1,0:T(8,128)(2,1)S(1)} %shard_map.87.refs_4_.refs_0_), channel_id=1, source_target_pairs={{0,2},{1,3},{2,0},{3,1},{4,6},{5,7},{6,4},{7,5},{8,10},{9,11},{10,... | collective-permute-start | bytes 393224 | tf_op jit(solution)/shard_map/ppermute | solution.py:205
  11.6 0.0 copy-done.2
  11.6 0.1 copy.9.feedback_ref
  11.7 0.0 copy-done.1
  11.7 0.1 copy.10.idf_ref
  11.8 0.0 collective-permute-done.1.refs_2_
  11.8 0.5 %collective-permute-done.2.refs_3_ = bf16[208,128]{1,0:T(8,128)(2,1)S(1)} collective-permute-done((bf16[208,128]{1,0:T(8,128)(2,1)S(1)}, bf16[208,128]{1,0:T(8,128)(2,1)S(1)}, u32[]{:S(2)}, u32[]{:S(2)}) %collective-permute-start.2) | collective-permute-done | bytes 53280 | tf_op jit(solution)/shard_map/ppermute | solution.py:202
  12.3 2.5 %collective-permute-start.6 = (bf16[320,128]{1,0:T(8,128)(2,1)S(1)}, bf16[320,128]{1,0:T(8,128)(2,1)S(1)}, u32[]{:S(2)}, u32[]{:S(2)}) collective-permute-start(bf16[320,128]{1,0:T(8,128)(2,1)S(1)} %shard_map.89), channel_id=1, source_target_pairs={{0,6},{1,7},{2,4},{3,5},{4,2},{5,3},{6,0},{7,1},{8,14},{9,15},{10,... | collective-permute-start | bytes 245768 | tf_op jit(solution)/shard_map/ppermute | solution.py:205
  14.7 0.5 %collective-permute-start.7 = (bf16[320,128]{1,0:T(8,128)(2,1)S(1)}, bf16[320,128]{1,0:T(8,128)(2,1)S(1)}, u32[]{:S(2)}, u32[]{:S(2)}) collective-permute-start(bf16[320,128]{1,0:T(8,128)(2,1)S(1)} %shard_map.89), channel_id=1, source_target_pairs={{0,4},{1,5},{2,6},{3,7},{4,0},{5,1},{6,2},{7,3},{8,12},{9,13},{10,... | collective-permute-start | bytes 245768 | tf_op jit(solution)/shard_map/ppermute | solution.py:205
  15.2 0.0 collective-permute-done.3.refs_5_.refs_1_
  15.2 1.1 %collective-permute-start.8 = (bf16[320,128]{1,0:T(8,128)(2,1)S(1)}, bf16[320,128]{1,0:T(8,128)(2,1)S(1)}, u32[]{:S(2)}, u32[]{:S(2)}) collective-permute-start(bf16[320,128]{1,0:T(8,128)(2,1)S(1)} %shard_map.89), channel_id=1, source_target_pairs={{0,2},{1,3},{2,0},{3,1},{4,6},{5,7},{6,4},{7,5},{8,10},{9,11},{10,... | collective-permute-start | bytes 245768 | tf_op jit(solution)/shard_map/ppermute | solution.py:205
  16.4 1.1 %collective-permute-done.4.refs_6_.refs_2_ = bf16[512,128]{1,0:T(8,128)(2,1)S(1)} collective-permute-done((bf16[512,128]{1,0:T(8,128)(2,1)S(1)}, bf16[512,128]{1,0:T(8,128)(2,1)S(1)}, u32[]{:S(2)}, u32[]{:S(2)}) %collective-permute-start.4) | collective-permute-done | bytes 131104 | tf_op jit(solution)/shard_map/ppermute | solution.py:205
  17.5 0.0 collective-permute-done.5.refs_7_.refs_3_
  17.5 0.1 collective-permute-start.10
  17.6 1.0 %shard_map.88 = (f32[16,16]{1,0:T(8,128)S(1)}, bf16[160,1280]{1,0:T(8,128)(2,1)S(1)}, bf16[160,1280]{1,0:T(8,128)(2,1)S(1)}, f32[16,160]{1,0:T(8,128)S(1)}) custom-call(s32[128,3]{1,0:T(8,128)S(1)} %copy.9.feedback_ref, s32[128,10]{1,0:T(8,128)S(1)} %copy.10.idf_ref, bf16[208,128]{1,0:T(8,128)(2,1)S(1)} %get-tuple-element.20.refs_0_, ...), custom_call_target="tpu_custom_call" | custom-call | tf_op jit(solution)/shard_map/pallas_call | solution.py:179
  18.6 0.9 %collective-permute-done.6 = bf16[320,128]{1,0:T(8,128)(2,1)S(1)} collective-permute-done((bf16[320,128]{1,0:T(8,128)(2,1)S(1)}, bf16[320,128]{1,0:T(8,128)(2,1)S(1)}, u32[]{:S(2)}, u32[]{:S(2)}) %collective-permute-start.6) | collective-permute-done | bytes 81952 | tf_op jit(solution)/shard_map/ppermute | solution.py:205
  19.5 0.3 collective-permute-done.7
  19.7 0.0 collective-permute-done.8
  19.8 0.3 shard_map.91
  20.1 0.1 collective-permute-start.9
  20.2 0.3 shard_map.90.near_pooled_ref
  20.4 0.0 collective-permute-done.10.refs_4_
  20.4 0.9 %shard_map.92.far_plain_ref = f32[16,16]{1,0:T(8,128)S(1)} custom-call(bf16[208,128]{1,0:T(8,128)(2,1)S(1)} %get-tuple-element.20.refs_0_, bf16[208,128]{1,0:T(8,128)(2,1)S(1)} %collective-permute-done.refs_1_, bf16[208,128]{1,0:T(8,128)(2,1)S(1)} %collective-permute-done.1.refs_2_, bf16[208,128]{1,0:T(8,128)(2,1)S(1)} %collective-permute-done.2.refs_3_, ...), custom_call_target="tpu_custom_call" | custom-call | tf_op jit(solution)/shard_map/pallas_call | solution.py:179
  21.3 0.1 collective-permute-done.9.far_pooled_ref
  21.4 1.0 %shard_map.93 = (f32[4,64]{1,0:T(4,128)S(1)}, f32[4,64]{1,0:T(4,128)S(1)}, f32[4,64]{1,0:T(4,128)S(1)}, f32[4,64]{1,0:T(4,128)S(1)}) custom-call(f32[160,128]{1,0:T(8,128)S(1)} %shard_map.90.near_pooled_ref, f32[160,128]{1,0:T(8,128)S(1)} %collective-permute-done.9.far_pooled_ref, f32[16,160]{1,0:T(8,128)S(1)} %get-tuple-element.32.spread_ref, ...), custom_call_target="tpu_custom_call" | custom-call | tf_op jit(solution)/shard_map/pallas_call | solution.py:179
  22.4 1.6 %collective-permute-start.11 = (f32[4,64]{1,0:T(4,128)S(1)}, f32[4,64]{1,0:T(4,128)S(1)}, u32[]{:S(2)}, u32[]{:S(2)}) collective-permute-start(f32[4,64]{1,0:T(4,128)S(1)} %get-tuple-element.34), channel_id=1, source_target_pairs={{0,8},{1,9},{2,10},{3,11},{4,12},{5,13},{6,14},{7,15},{8,16},{9,17... | collective-permute-start | bytes 3080 | tf_op jit(solution)/shard_map/ppermute | solution.py:202
  24.0 0.0 copy-start
  24.0 1.2 %collective-permute-start.12 = (f32[4,64]{1,0:T(4,128)S(1)}, f32[4,64]{1,0:T(4,128)S(1)}, u32[]{:S(2)}, u32[]{:S(2)}) collective-permute-start(f32[4,64]{1,0:T(4,128)S(1)} %get-tuple-element.35), channel_id=1, source_target_pairs={{0,16},{1,17},{2,18},{3,19},{4,20},{5,21},{6,22},{7,23},{8,24},{9,... | collective-permute-start | bytes 3080 | tf_op jit(solution)/shard_map/ppermute | solution.py:202
  25.2 2.4 %collective-permute-start.13 = (f32[4,64]{1,0:T(4,128)S(1)}, f32[4,64]{1,0:T(4,128)S(1)}, u32[]{:S(2)}, u32[]{:S(2)}) collective-permute-start(f32[4,64]{1,0:T(4,128)S(1)} %get-tuple-element.36), channel_id=1, source_target_pairs={{0,24},{1,25},{2,26},{3,27},{4,28},{5,29},{6,30},{7,31},{8,0},{9,1... | collective-permute-start | bytes 3080 | tf_op jit(solution)/shard_map/ppermute | solution.py:202
  27.6 0.2 collective-permute-done.11.refs_0_
  27.8 0.7 %collective-permute-done.12.refs_1_ = f32[4,64]{1,0:T(4,128)S(1)} collective-permute-done((f32[4,64]{1,0:T(4,128)S(1)}, f32[4,64]{1,0:T(4,128)S(1)}, u32[]{:S(2)}, u32[]{:S(2)}) %collective-permute-start.12) | collective-permute-done | bytes 1056 | tf_op jit(solution)/shard_map/ppermute | solution.py:202
  28.5 0.4 %collective-permute-done.13.refs_2_ = f32[4,64]{1,0:T(4,128)S(1)} collective-permute-done((f32[4,64]{1,0:T(4,128)S(1)}, f32[4,64]{1,0:T(4,128)S(1)}, u32[]{:S(2)}, u32[]{:S(2)}) %collective-permute-start.13) | collective-permute-done | bytes 1056 | tf_op jit(solution)/shard_map/ppermute | solution.py:202
  28.9 0.0 copy-done
  28.9 0.7 %shard_map.94 = (f32[4,64]{1,0:T(4,128)}, f32[4,64]{1,0:T(4,128)}) custom-call(s32[4,64]{1,0:T(4,128)S(1)} %copy-done, f32[4,64]{1,0:T(4,128)S(1)} %collective-permute-done.11.refs_0_, f32[4,64]{1,0:T(4,128)S(1)} %collective-permute-done.12.refs_1_, f32[4,64]{1,0:T(4,128)S(1)} %collective-permute-done.13.refs_2_, f32[4,64]{1,0:T(4,128)S(1)} %get-tuple-element.37.refs_3_), custom_call_target="tpu_custom_call" | custom-call | tf_op jit(solution)/shard_map/pallas_call | solution.py:179
  (3 shorter events, 0.1 us)
Async XLA Ops:
  1.8 9.3 %collective-permute-start = (bf16[208,128]{1,0:T(8,128)(2,1)S(1)}, bf16[208,128]{1,0:T(8,128)(2,1)S(1)}, u32[]{:S(2)}, u32[]{:S(2)}) collective-permute-start(bf16[208,128]{1,0:T(8,128)(2,1)S(1)} %get-tuple-element.20.refs_0_), channel_id=1, source_target_pairs={{0,8},{1,9},{2,10},{3,11},{4,12},{5,13},{6,14},{7,15},{8,16},{9,17... | collective-permute-start | bytes 159752 | tf_op jit(solution)/shard_map/ppermute | solution.py:202
  4.8 7.0 %collective-permute-start.1 = (bf16[208,128]{1,0:T(8,128)(2,1)S(1)}, bf16[208,128]{1,0:T(8,128)(2,1)S(1)}, u32[]{:S(2)}, u32[]{:S(2)}) collective-permute-start(bf16[208,128]{1,0:T(8,128)(2,1)S(1)} %get-tuple-element.20.refs_0_), channel_id=1, source_target_pairs={{0,24},{1,25},{2,26},{3,27},{4,28},{5,29},{6,30},{7,31},{8,0},{9,1... | collective-permute-start | bytes 159752 | tf_op jit(solution)/shard_map/ppermute | solution.py:202
  6.9 5.3 %collective-permute-start.2 = (bf16[208,128]{1,0:T(8,128)(2,1)S(1)}, bf16[208,128]{1,0:T(8,128)(2,1)S(1)}, u32[]{:S(2)}, u32[]{:S(2)}) collective-permute-start(bf16[208,128]{1,0:T(8,128)(2,1)S(1)} %get-tuple-element.20.refs_0_), channel_id=1, source_target_pairs={{0,16},{1,17},{2,18},{3,19},{4,20},{5,21},{6,22},{7,23},{8,24},{9,... | collective-permute-start | bytes 159752 | tf_op jit(solution)/shard_map/ppermute | solution.py:202
  7.9 3.7 %copy-start.2 = (s32[128,3]{0,1:T(4,128)S(1)}, s32[128,3]{0,1:T(4,128)}, u32[]{:S(2)}) copy-start(s32[128,3]{0,1:T(4,128)} %param.12) | copy-start | bytes 4612
  8.0 3.7 %copy-start.1 = (s32[128,10]{0,1:T(8,128)S(1)}, s32[128,10]{0,1:T(8,128)}, u32[]{:S(2)}) copy-start(s32[128,10]{0,1:T(8,128)} %param.13) | copy-start | bytes 15364
  8.0 7.3 %collective-permute-start.3 = (bf16[512,128]{1,0:T(8,128)(2,1)S(1)}, bf16[512,128]{1,0:T(8,128)(2,1)S(1)}, u32[]{:S(2)}, u32[]{:S(2)}) collective-permute-start(bf16[512,128]{1,0:T(8,128)(2,1)S(1)} %shard_map.87.refs_4_.refs_0_), channel_id=1, source_target_pairs={{0,6},{1,7},{2,4},{3,5},{4,2},{5,3},{6,0},{7,1},{8,14},{9,15},{10,... | collective-permute-start | bytes 393224 | tf_op jit(solution)/shard_map/ppermute | solution.py:205
  10.5 7.0 %collective-permute-start.4 = (bf16[512,128]{1,0:T(8,128)(2,1)S(1)}, bf16[512,128]{1,0:T(8,128)(2,1)S(1)}, u32[]{:S(2)}, u32[]{:S(2)}) collective-permute-start(bf16[512,128]{1,0:T(8,128)(2,1)S(1)} %shard_map.87.refs_4_.refs_0_), channel_id=1, source_target_pairs={{0,4},{1,5},{2,6},{3,7},{4,0},{5,1},{6,2},{7,3},{8,12},{9,13},{10,... | collective-permute-start | bytes 393224 | tf_op jit(solution)/shard_map/ppermute | solution.py:205
  11.0 6.4 %collective-permute-start.5 = (bf16[512,128]{1,0:T(8,128)(2,1)S(1)}, bf16[512,128]{1,0:T(8,128)(2,1)S(1)}, u32[]{:S(2)}, u32[]{:S(2)}) collective-permute-start(bf16[512,128]{1,0:T(8,128)(2,1)S(1)} %shard_map.87.refs_4_.refs_0_), channel_id=1, source_target_pairs={{0,2},{1,3},{2,0},{3,1},{4,6},{5,7},{6,4},{7,5},{8,10},{9,11},{10,... | collective-permute-start | bytes 393224 | tf_op jit(solution)/shard_map/ppermute | solution.py:205
  12.3 7.2 %collective-permute-start.6 = (bf16[320,128]{1,0:T(8,128)(2,1)S(1)}, bf16[320,128]{1,0:T(8,128)(2,1)S(1)}, u32[]{:S(2)}, u32[]{:S(2)}) collective-permute-start(bf16[320,128]{1,0:T(8,128)(2,1)S(1)} %shard_map.89), channel_id=1, source_target_pairs={{0,6},{1,7},{2,4},{3,5},{4,2},{5,3},{6,0},{7,1},{8,14},{9,15},{10,... | collective-permute-start | bytes 245768 | tf_op jit(solution)/shard_map/ppermute | solution.py:205
  14.7 5.0 %collective-permute-start.7 = (bf16[320,128]{1,0:T(8,128)(2,1)S(1)}, bf16[320,128]{1,0:T(8,128)(2,1)S(1)}, u32[]{:S(2)}, u32[]{:S(2)}) collective-permute-start(bf16[320,128]{1,0:T(8,128)(2,1)S(1)} %shard_map.89), channel_id=1, source_target_pairs={{0,4},{1,5},{2,6},{3,7},{4,0},{5,1},{6,2},{7,3},{8,12},{9,13},{10,... | collective-permute-start | bytes 245768 | tf_op jit(solution)/shard_map/ppermute | solution.py:205
  15.2 4.5 %collective-permute-start.8 = (bf16[320,128]{1,0:T(8,128)(2,1)S(1)}, bf16[320,128]{1,0:T(8,128)(2,1)S(1)}, u32[]{:S(2)}, u32[]{:S(2)}) collective-permute-start(bf16[320,128]{1,0:T(8,128)(2,1)S(1)} %shard_map.89), channel_id=1, source_target_pairs={{0,2},{1,3},{2,0},{3,1},{4,6},{5,7},{6,4},{7,5},{8,10},{9,11},{10,... | collective-permute-start | bytes 245768 | tf_op jit(solution)/shard_map/ppermute | solution.py:205
  17.5 2.9 %collective-permute-start.10 = (bf16[2048,128]{1,0:T(8,128)(2,1)S(1)}, bf16[2048,128]{1,0:T(8,128)(2,1)S(1)}, u32[]{:S(2)}, u32[]{:S(2)}) collective-permute-start(bf16[2048,128]{1,0:T(8,128)(2,1)S(1)} %pad_maximum_fusion), channel_id=1, source_target_pairs={{0,1},{1,0},{2,3},{3,2},{4,5},{5,4},{6,7},{7,6},{8,9},{9,8},{10,11... | collective-permute-start | bytes 1572872 | tf_op jit(solution)/shard_map/ppermute | solution.py:205
  20.1 1.3 %collective-permute-start.9 = (f32[160,128]{1,0:T(8,128)S(1)}, f32[160,128]{1,0:T(8,128)S(1)}, u32[]{:S(2)}, u32[]{:S(2)}) collective-permute-start(f32[160,128]{1,0:T(8,128)S(1)} %shard_map.91), channel_id=1, source_target_pairs={{0,1},{1,0},{2,3},{3,2},{4,5},{5,4},{6,7},{7,6},{8,9},{9,8},{10,11... | collective-permute-start | bytes 245768 | tf_op jit(solution)/shard_map/ppermute | solution.py:205
  22.4 5.4 %collective-permute-start.11 = (f32[4,64]{1,0:T(4,128)S(1)}, f32[4,64]{1,0:T(4,128)S(1)}, u32[]{:S(2)}, u32[]{:S(2)}) collective-permute-start(f32[4,64]{1,0:T(4,128)S(1)} %get-tuple-element.34), channel_id=1, source_target_pairs={{0,8},{1,9},{2,10},{3,11},{4,12},{5,13},{6,14},{7,15},{8,16},{9,17... | collective-permute-start | bytes 3080 | tf_op jit(solution)/shard_map/ppermute | solution.py:202
  24.0 4.9 %copy-start = (s32[4,64]{1,0:T(4,128)S(1)}, s32[4,64]{1,0:T(4,128)}, u32[]{:S(2)}) copy-start(s32[4,64]{1,0:T(4,128)} %candidates_ref.1) | copy-start | bytes 3076
  24.0 4.5 %collective-permute-start.12 = (f32[4,64]{1,0:T(4,128)S(1)}, f32[4,64]{1,0:T(4,128)S(1)}, u32[]{:S(2)}, u32[]{:S(2)}) collective-permute-start(f32[4,64]{1,0:T(4,128)S(1)} %get-tuple-element.35), channel_id=1, source_target_pairs={{0,16},{1,17},{2,18},{3,19},{4,20},{5,21},{6,22},{7,23},{8,24},{9,... | collective-permute-start | bytes 3080 | tf_op jit(solution)/shard_map/ppermute | solution.py:202
  25.2 3.7 %collective-permute-start.13 = (f32[4,64]{1,0:T(4,128)S(1)}, f32[4,64]{1,0:T(4,128)S(1)}, u32[]{:S(2)}, u32[]{:S(2)}) collective-permute-start(f32[4,64]{1,0:T(4,128)S(1)} %get-tuple-element.36), channel_id=1, source_target_pairs={{0,24},{1,25},{2,26},{3,27},{4,28},{5,29},{6,30},{7,31},{8,0},{9,1... | collective-permute-start | bytes 3080 | tf_op jit(solution)/shard_map/ppermute | solution.py:202

commit v6 on v4

--- a/solution.py
+++ b/solution.py
@@ -141,18 +141,24 @@
         out_ref[...] = both[place * each : (place + 1) * each, :]
 
 
-def select_kernel(count, bank, places, candidates_ref, *refs):
-    block_refs, first_ref, final_ref = [refs[i] for i in places], refs[-2], refs[-1]
+def place_kernel(count, bank, columns, candidates_ref, place_ref):
     me = lax.axis_index("shard")
     given, wanted = candidates_ref.shape
+    width = bank * count
+    place = relative(candidates_ref[...], me, count, bank, columns)
+    owner, within = place // count % bank, place % count
+    block = (bank - owner // 2 * 2) % bank // 2
+    place = place // width * width + owner % 2 * (width // 2) + block * count + within
+    rows, lanes = place_ref.shape
+    place_ref[...] = jnp.pad(place, ((0, rows - given), (0, lanes - wanted)))
+
+
+def select_kernel(places, place_ref, *refs):
+    block_refs, first_ref, final_ref = [refs[i] for i in places], refs[-2], refs[-1]
+    given, wanted = first_ref.shape
     width = block_refs[0].shape[1] // 2
-    place = relative(candidates_ref[...], me, count, bank, len(places))
-    owner, within = place // count % (width // count), place % count
-    half = width // 2
-    block = (bank - owner // 2 * 2) % bank // 2
-    place = place // width * width + owner % 2 * half + block * count + within
-    rows, lanes = -(-given // 8) * 8, -(-wanted // 128) * 128
-    place = jnp.pad(place, ((0, rows - given), (0, lanes - wanted)))
+    place = place_ref[...]
+    rows = place.shape[0]
     for side, out_ref in enumerate((first_ref, final_ref)):
         dense = jnp.concatenate([r[:, side * width : (side + 1) * width] for r in block_refs], axis=1)
         dense = jnp.pad(dense, ((0, rows - given), (0, 0)))
@@ -256,10 +262,12 @@
         far_documents,
     )
     blocks = [shift(block, s) if s else block for s, block in zip(returns, blocks)]
+    rows, lanes = -(-each // 8) * 8, -(-candidates.shape[1] // 128) * 128
+    place = call(functools.partial(place_kernel, count, bank, columns), sds((rows, lanes), I32), candidates)
     return call(
-        functools.partial(select_kernel, count, bank, [returns.index(-s % columns) for s in range(columns)]),
+        functools.partial(select_kernel, [returns.index(-s % columns) for s in range(columns)]),
         (sds(candidates.shape, F32), sds(candidates.shape, F32)),
-        candidates,
+        place,
         *blocks,
     )
 

time: 29.8 us -> 29.8 us (level)
    pallas_call x8 -> x9, Pallas kernels: 5.35 us -> 5.42 us  [call(): pl.pallas_call(kernel, out_shape=out_shape, in_specs=specs or [pl.BlockSp...]
where the time goes in v6:
time: 29.8 us; the launch traced here: 29.6 us
  starting transfers between devices  18.8 us (63%)
  Pallas kernels  5.42 us (18%)
  waiting for transfers between devices  4.41 us (15%)
  between operations  0.72 us (2%)
    ppermute x6, starting transfers between devices, shift(): lax.ppermute(x, 'shard', [(i, (i + s * bank) % devices) for i in range(de...  11.2 us
    ppermute x8, starting transfers between devices, swap(): return lax.ppermute(x, 'shard', [(i, i ^ m) for i in range(devices)])  7.57 us
    pallas_call x9, Pallas kernels, call(): pl.pallas_call(kernel, out_shape=out_shape, in_specs=specs or [pl.BlockSp...  5.42 us
    ppermute x8, waiting for transfers between devices, swap(): return lax.ppermute(x, 'shard', [(i, i ^ m) for i in range(devices)])  2.45 us
    ppermute x6, waiting for transfers between devices, shift(): lax.ppermute(x, 'shard', [(i, (i + s * bank) % devices) for i in range(de...  1.96 us
  transfers between devices with their start and end apart: 14, of which 9 were waited for; matrix products, arithmetic and copies ran while one was open for 1% of the time, Pallas kernels for 8%

profile of v6, /device:TPU:0, one launch (start us, length us, event | category | flops | bytes accessed | tf_op | source)
XLA Modules:
  0.0 29.6 jit_solution(6221584174893273688)
XLA Ops:
  0.6 0.0 copy-start.1
  0.6 1.2 %shard_map.87 = (bf16[208,128]{1,0:T(8,128)(2,1)S(1)}, bf16[512,128]{1,0:T(8,128)(2,1)S(1)}) custom-call(s32[1,4]{1,0:T(1,128)} %bitcast.3, bf16[128,128]{1,0:T(8,128)(2,1)} %bitcast.2, bf16[4,128,128]{2,1,0:T(8,128)(2,1)} %passages_hbm, s32[4,128]{1,0:T(4,128)} %labels_hbm.1), custom_call_target="tpu_custom_call" | custom-call | tf_op jit(solution)/shard_map/pallas_call | solution.py:179
  1.8 3.1 %collective-permute-start = (bf16[208,128]{1,0:T(8,128)(2,1)S(1)}, bf16[208,128]{1,0:T(8,128)(2,1)S(1)}, u32[]{:S(2)}, u32[]{:S(2)}) collective-permute-start(bf16[208,128]{1,0:T(8,128)(2,1)S(1)} %get-tuple-element.19.refs_0_), channel_id=1, source_target_pairs={{0,8},{1,9},{2,10},{3,11},{4,12},{5,13},{6,14},{7,15},{8,16},{9,17... | collective-permute-start | bytes 159752 | tf_op jit(solution)/shard_map/ppermute | solution.py:202
  4.9 2.1 %collective-permute-start.1 = (bf16[208,128]{1,0:T(8,128)(2,1)S(1)}, bf16[208,128]{1,0:T(8,128)(2,1)S(1)}, u32[]{:S(2)}, u32[]{:S(2)}) collective-permute-start(bf16[208,128]{1,0:T(8,128)(2,1)S(1)} %get-tuple-element.19.refs_0_), channel_id=1, source_target_pairs={{0,24},{1,25},{2,26},{3,27},{4,28},{5,29},{6,30},{7,31},{8,0},{9,1... | collective-permute-start | bytes 159752 | tf_op jit(solution)/shard_map/ppermute | solution.py:202
  7.0 0.9 %collective-permute-start.2 = (bf16[208,128]{1,0:T(8,128)(2,1)S(1)}, bf16[208,128]{1,0:T(8,128)(2,1)S(1)}, u32[]{:S(2)}, u32[]{:S(2)}) collective-permute-start(bf16[208,128]{1,0:T(8,128)(2,1)S(1)} %get-tuple-element.19.refs_0_), channel_id=1, source_target_pairs={{0,16},{1,17},{2,18},{3,19},{4,20},{5,21},{6,22},{7,23},{8,24},{9,... | collective-permute-start | bytes 159752 | tf_op jit(solution)/shard_map/ppermute | solution.py:202
  7.9 0.0 copy-start.2
  7.9 2.4 %collective-permute-start.3 = (bf16[512,128]{1,0:T(8,128)(2,1)S(1)}, bf16[512,128]{1,0:T(8,128)(2,1)S(1)}, u32[]{:S(2)}, u32[]{:S(2)}) collective-permute-start(bf16[512,128]{1,0:T(8,128)(2,1)S(1)} %get-tuple-element.20.refs_4_.refs_0_), channel_id=1, source_target_pairs={{0,6},{1,7},{2,4},{3,5},{4,2},{5,3},{6,0},{7,1},{8,14},{9,15},{10,... | collective-permute-start | bytes 393224 | tf_op jit(solution)/shard_map/ppermute | solution.py:205
  10.4 0.5 %collective-permute-start.4 = (bf16[512,128]{1,0:T(8,128)(2,1)S(1)}, bf16[512,128]{1,0:T(8,128)(2,1)S(1)}, u32[]{:S(2)}, u32[]{:S(2)}) collective-permute-start(bf16[512,128]{1,0:T(8,128)(2,1)S(1)} %get-tuple-element.20.refs_4_.refs_0_), channel_id=1, source_target_pairs={{0,4},{1,5},{2,6},{3,7},{4,0},{5,1},{6,2},{7,3},{8,12},{9,13},{10,... | collective-permute-start | bytes 393224 | tf_op jit(solution)/shard_map/ppermute | solution.py:205
  10.9 0.0 collective-permute-done.refs_1_
  10.9 0.5 %collective-permute-start.5 = (bf16[512,128]{1,0:T(8,128)(2,1)S(1)}, bf16[512,128]{1,0:T(8,128)(2,1)S(1)}, u32[]{:S(2)}, u32[]{:S(2)}) collective-permute-start(bf16[512,128]{1,0:T(8,128)(2,1)S(1)} %get-tuple-element.20.refs_4_.refs_0_), channel_id=1, source_target_pairs={{0,2},{1,3},{2,0},{3,1},{4,6},{5,7},{6,4},{7,5},{8,10},{9,11},{10,... | collective-permute-start | bytes 393224 | tf_op jit(solution)/shard_map/ppermute | solution.py:205
  11.4 0.0 copy-done.1
  11.4 0.1 copy.10.idf_ref
  11.6 0.0 copy-done.2
  11.6 0.1 copy.9.feedback_ref
  11.7 0.0 collective-permute-done.1.refs_2_
  11.7 0.7 %collective-permute-done.2.refs_3_ = bf16[208,128]{1,0:T(8,128)(2,1)S(1)} collective-permute-done((bf16[208,128]{1,0:T(8,128)(2,1)S(1)}, bf16[208,128]{1,0:T(8,128)(2,1)S(1)}, u32[]{:S(2)}, u32[]{:S(2)}) %collective-permute-start.2) | collective-permute-done | bytes 53280 | tf_op jit(solution)/shard_map/ppermute | solution.py:202
  12.3 2.5 %collective-permute-start.6 = (bf16[320,128]{1,0:T(8,128)(2,1)S(1)}, bf16[320,128]{1,0:T(8,128)(2,1)S(1)}, u32[]{:S(2)}, u32[]{:S(2)}) collective-permute-start(bf16[320,128]{1,0:T(8,128)(2,1)S(1)} %shard_map.89), channel_id=1, source_target_pairs={{0,6},{1,7},{2,4},{3,5},{4,2},{5,3},{6,0},{7,1},{8,14},{9,15},{10,... | collective-permute-start | bytes 245768 | tf_op jit(solution)/shard_map/ppermute | solution.py:205
  14.8 0.5 %collective-permute-start.7 = (bf16[320,128]{1,0:T(8,128)(2,1)S(1)}, bf16[320,128]{1,0:T(8,128)(2,1)S(1)}, u32[]{:S(2)}, u32[]{:S(2)}) collective-permute-start(bf16[320,128]{1,0:T(8,128)(2,1)S(1)} %shard_map.89), channel_id=1, source_target_pairs={{0,4},{1,5},{2,6},{3,7},{4,0},{5,1},{6,2},{7,3},{8,12},{9,13},{10,... | collective-permute-start | bytes 245768 | tf_op jit(solution)/shard_map/ppermute | solution.py:205
  15.3 0.0 collective-permute-done.3.refs_5_.refs_1_
  15.3 1.0 %collective-permute-start.8 = (bf16[320,128]{1,0:T(8,128)(2,1)S(1)}, bf16[320,128]{1,0:T(8,128)(2,1)S(1)}, u32[]{:S(2)}, u32[]{:S(2)}) collective-permute-start(bf16[320,128]{1,0:T(8,128)(2,1)S(1)} %shard_map.89), channel_id=1, source_target_pairs={{0,2},{1,3},{2,0},{3,1},{4,6},{5,7},{6,4},{7,5},{8,10},{9,11},{10,... | collective-permute-start | bytes 245768 | tf_op jit(solution)/shard_map/ppermute | solution.py:205
  16.3 1.0 %collective-permute-done.4.refs_6_.refs_2_ = bf16[512,128]{1,0:T(8,128)(2,1)S(1)} collective-permute-done((bf16[512,128]{1,0:T(8,128)(2,1)S(1)}, bf16[512,128]{1,0:T(8,128)(2,1)S(1)}, u32[]{:S(2)}, u32[]{:S(2)}) %collective-permute-start.4) | collective-permute-done | bytes 131104 | tf_op jit(solution)/shard_map/ppermute | solution.py:205
  17.2 0.0 collective-permute-done.5.refs_7_.refs_3_
  17.3 0.1 collective-permute-start.10
  17.4 1.0 %shard_map.88 = (f32[16,16]{1,0:T(8,128)S(1)}, bf16[160,1280]{1,0:T(8,128)(2,1)S(1)}, bf16[160,1280]{1,0:T(8,128)(2,1)S(1)}, f32[16,160]{1,0:T(8,128)S(1)}) custom-call(s32[128,3]{1,0:T(8,128)S(1)} %copy.9.feedback_ref, s32[128,10]{1,0:T(8,128)S(1)} %copy.10.idf_ref, bf16[208,128]{1,0:T(8,128)(2,1)S(1)} %get-tuple-element.19.refs_0_, ...), custom_call_target="tpu_custom_call" | custom-call | tf_op jit(solution)/shard_map/pallas_call | solution.py:179
  18.4 0.7 %collective-permute-done.6 = bf16[320,128]{1,0:T(8,128)(2,1)S(1)} collective-permute-done((bf16[320,128]{1,0:T(8,128)(2,1)S(1)}, bf16[320,128]{1,0:T(8,128)(2,1)S(1)}, u32[]{:S(2)}, u32[]{:S(2)}) %collective-permute-start.6) | collective-permute-done | bytes 81952 | tf_op jit(solution)/shard_map/ppermute | solution.py:205
  19.1 0.5 %collective-permute-done.7 = bf16[320,128]{1,0:T(8,128)(2,1)S(1)} collective-permute-done((bf16[320,128]{1,0:T(8,128)(2,1)S(1)}, bf16[320,128]{1,0:T(8,128)(2,1)S(1)}, u32[]{:S(2)}, u32[]{:S(2)}) %collective-permute-start.7) | collective-permute-done | bytes 81952 | tf_op jit(solution)/shard_map/ppermute | solution.py:205
  19.6 0.1 collective-permute-done.8
  19.8 0.3 shard_map.91
  20.1 0.1 collective-permute-start.9
  20.1 0.3 shard_map.90.near_pooled_ref
  20.4 0.0 collective-permute-done.10.refs_4_
  20.4 0.9 %shard_map.92.far_plain_ref = f32[16,16]{1,0:T(8,128)S(1)} custom-call(bf16[208,128]{1,0:T(8,128)(2,1)S(1)} %get-tuple-element.19.refs_0_, bf16[208,128]{1,0:T(8,128)(2,1)S(1)} %collective-permute-done.refs_1_, bf16[208,128]{1,0:T(8,128)(2,1)S(1)} %collective-permute-done.1.refs_2_, bf16[208,128]{1,0:T(8,128)(2,1)S(1)} %collective-permute-done.2.refs_3_, ...), custom_call_target="tpu_custom_call" | custom-call | tf_op jit(solution)/shard_map/pallas_call | solution.py:179
  21.3 0.1 collective-permute-done.9.far_pooled_ref
  21.4 1.0 %shard_map.93 = (f32[4,64]{1,0:T(4,128)S(1)}, f32[4,64]{1,0:T(4,128)S(1)}, f32[4,64]{1,0:T(4,128)S(1)}, f32[4,64]{1,0:T(4,128)S(1)}) custom-call(f32[160,128]{1,0:T(8,128)S(1)} %shard_map.90.near_pooled_ref, f32[160,128]{1,0:T(8,128)S(1)} %collective-permute-done.9.far_pooled_ref, f32[16,160]{1,0:T(8,128)S(1)} %get-tuple-element.30.spread_ref, ...), custom_call_target="tpu_custom_call" | custom-call | tf_op jit(solution)/shard_map/pallas_call | solution.py:179
  22.4 0.0 copy-start
  22.4 1.5 %collective-permute-start.11 = (f32[4,64]{1,0:T(4,128)S(1)}, f32[4,64]{1,0:T(4,128)S(1)}, u32[]{:S(2)}, u32[]{:S(2)}) collective-permute-start(f32[4,64]{1,0:T(4,128)S(1)} %get-tuple-element.32), channel_id=1, source_target_pairs={{0,8},{1,9},{2,10},{3,11},{4,12},{5,13},{6,14},{7,15},{8,16},{9,17... | collective-permute-start | bytes 3080 | tf_op jit(solution)/shard_map/ppermute | solution.py:202
  23.9 1.4 %collective-permute-start.12 = (f32[4,64]{1,0:T(4,128)S(1)}, f32[4,64]{1,0:T(4,128)S(1)}, u32[]{:S(2)}, u32[]{:S(2)}) collective-permute-start(f32[4,64]{1,0:T(4,128)S(1)} %get-tuple-element.33), channel_id=1, source_target_pairs={{0,16},{1,17},{2,18},{3,19},{4,20},{5,21},{6,22},{7,23},{8,24},{9,... | collective-permute-start | bytes 3080 | tf_op jit(solution)/shard_map/ppermute | solution.py:202
  25.3 2.2 %collective-permute-start.13 = (f32[4,64]{1,0:T(4,128)S(1)}, f32[4,64]{1,0:T(4,128)S(1)}, u32[]{:S(2)}, u32[]{:S(2)}) collective-permute-start(f32[4,64]{1,0:T(4,128)S(1)} %get-tuple-element.34), channel_id=1, source_target_pairs={{0,24},{1,25},{2,26},{3,27},{4,28},{5,29},{6,30},{7,31},{8,0},{9,1... | collective-permute-start | bytes 3080 | tf_op jit(solution)/shard_map/ppermute | solution.py:202
  27.5 0.0 copy-done
  27.5 0.1 shard_map.86.place_ref
  27.6 0.2 collective-permute-done.11.refs_0_
  27.8 0.6 %collective-permute-done.12.refs_1_ = f32[4,64]{1,0:T(4,128)S(1)} collective-permute-done((f32[4,64]{1,0:T(4,128)S(1)}, f32[4,64]{1,0:T(4,128)S(1)}, u32[]{:S(2)}, u32[]{:S(2)}) %collective-permute-start.12) | collective-permute-done | bytes 1056 | tf_op jit(solution)/shard_map/ppermute | solution.py:202
  28.4 0.5 %collective-permute-done.13.refs_2_ = f32[4,64]{1,0:T(4,128)S(1)} collective-permute-done((f32[4,64]{1,0:T(4,128)S(1)}, f32[4,64]{1,0:T(4,128)S(1)}, u32[]{:S(2)}, u32[]{:S(2)}) %collective-permute-start.13) | collective-permute-done | bytes 1056 | tf_op jit(solution)/shard_map/ppermute | solution.py:202
  28.9 0.7 %shard_map.94 = (f32[4,64]{1,0:T(4,128)}, f32[4,64]{1,0:T(4,128)}) custom-call(s32[8,128]{1,0:T(8,128)S(1)} %shard_map.86.place_ref, f32[4,64]{1,0:T(4,128)S(1)} %collective-permute-done.11.refs_0_, f32[4,64]{1,0:T(4,128)S(1)} %collective-permute-done.12.refs_1_, f32[4,64]{1,0:T(4,128)S(1)} %collective-permute-done.13.refs_2_, ...), custom_call_target="tpu_custom_call" | custom-call | tf_op jit(solution)/shard_map/pallas_call | solution.py:179
  (3 shorter events, 0.1 us)
Async XLA Ops:
  0.6 10.8 %copy-start.1 = (s32[128,10]{0,1:T(8,128)S(1)}, s32[128,10]{0,1:T(8,128)}, u32[]{:S(2)}) copy-start(s32[128,10]{0,1:T(8,128)} %param.13) | copy-start | bytes 15364
  1.8 9.1 %collective-permute-start = (bf16[208,128]{1,0:T(8,128)(2,1)S(1)}, bf16[208,128]{1,0:T(8,128)(2,1)S(1)}, u32[]{:S(2)}, u32[]{:S(2)}) collective-permute-start(bf16[208,128]{1,0:T(8,128)(2,1)S(1)} %get-tuple-element.19.refs_0_), channel_id=1, source_target_pairs={{0,8},{1,9},{2,10},{3,11},{4,12},{5,13},{6,14},{7,15},{8,16},{9,17... | collective-permute-start | bytes 159752 | tf_op jit(solution)/shard_map/ppermute | solution.py:202
  4.9 6.8 %collective-permute-start.1 = (bf16[208,128]{1,0:T(8,128)(2,1)S(1)}, bf16[208,128]{1,0:T(8,128)(2,1)S(1)}, u32[]{:S(2)}, u32[]{:S(2)}) collective-permute-start(bf16[208,128]{1,0:T(8,128)(2,1)S(1)} %get-tuple-element.19.refs_0_), channel_id=1, source_target_pairs={{0,24},{1,25},{2,26},{3,27},{4,28},{5,29},{6,30},{7,31},{8,0},{9,1... | collective-permute-start | bytes 159752 | tf_op jit(solution)/shard_map/ppermute | solution.py:202
  7.0 5.3 %collective-permute-start.2 = (bf16[208,128]{1,0:T(8,128)(2,1)S(1)}, bf16[208,128]{1,0:T(8,128)(2,1)S(1)}, u32[]{:S(2)}, u32[]{:S(2)}) collective-permute-start(bf16[208,128]{1,0:T(8,128)(2,1)S(1)} %get-tuple-element.19.refs_0_), channel_id=1, source_target_pairs={{0,16},{1,17},{2,18},{3,19},{4,20},{5,21},{6,22},{7,23},{8,24},{9,... | collective-permute-start | bytes 159752 | tf_op jit(solution)/shard_map/ppermute | solution.py:202
  7.9 3.6 %copy-start.2 = (s32[128,3]{0,1:T(4,128)S(1)}, s32[128,3]{0,1:T(4,128)}, u32[]{:S(2)}) copy-start(s32[128,3]{0,1:T(4,128)} %param.12) | copy-start | bytes 4612
  7.9 7.4 %collective-permute-start.3 = (bf16[512,128]{1,0:T(8,128)(2,1)S(1)}, bf16[512,128]{1,0:T(8,128)(2,1)S(1)}, u32[]{:S(2)}, u32[]{:S(2)}) collective-permute-start(bf16[512,128]{1,0:T(8,128)(2,1)S(1)} %get-tuple-element.20.refs_4_.refs_0_), channel_id=1, source_target_pairs={{0,6},{1,7},{2,4},{3,5},{4,2},{5,3},{6,0},{7,1},{8,14},{9,15},{10,... | collective-permute-start | bytes 393224 | tf_op jit(solution)/shard_map/ppermute | solution.py:205
  10.4 6.9 %collective-permute-start.4 = (bf16[512,128]{1,0:T(8,128)(2,1)S(1)}, bf16[512,128]{1,0:T(8,128)(2,1)S(1)}, u32[]{:S(2)}, u32[]{:S(2)}) collective-permute-start(bf16[512,128]{1,0:T(8,128)(2,1)S(1)} %get-tuple-element.20.refs_4_.refs_0_), channel_id=1, source_target_pairs={{0,4},{1,5},{2,6},{3,7},{4,0},{5,1},{6,2},{7,3},{8,12},{9,13},{10,... | collective-permute-start | bytes 393224 | tf_op jit(solution)/shard_map/ppermute | solution.py:205
  10.9 6.3 %collective-permute-start.5 = (bf16[512,128]{1,0:T(8,128)(2,1)S(1)}, bf16[512,128]{1,0:T(8,128)(2,1)S(1)}, u32[]{:S(2)}, u32[]{:S(2)}) collective-permute-start(bf16[512,128]{1,0:T(8,128)(2,1)S(1)} %get-tuple-element.20.refs_4_.refs_0_), channel_id=1, source_target_pairs={{0,2},{1,3},{2,0},{3,1},{4,6},{5,7},{6,4},{7,5},{8,10},{9,11},{10,... | collective-permute-start | bytes 393224 | tf_op jit(solution)/shard_map/ppermute | solution.py:205
  12.3 6.8 %collective-permute-start.6 = (bf16[320,128]{1,0:T(8,128)(2,1)S(1)}, bf16[320,128]{1,0:T(8,128)(2,1)S(1)}, u32[]{:S(2)}, u32[]{:S(2)}) collective-permute-start(bf16[320,128]{1,0:T(8,128)(2,1)S(1)} %shard_map.89), channel_id=1, source_target_pairs={{0,6},{1,7},{2,4},{3,5},{4,2},{5,3},{6,0},{7,1},{8,14},{9,15},{10,... | collective-permute-start | bytes 245768 | tf_op jit(solution)/shard_map/ppermute | solution.py:205
  14.8 4.8 %collective-permute-start.7 = (bf16[320,128]{1,0:T(8,128)(2,1)S(1)}, bf16[320,128]{1,0:T(8,128)(2,1)S(1)}, u32[]{:S(2)}, u32[]{:S(2)}) collective-permute-start(bf16[320,128]{1,0:T(8,128)(2,1)S(1)} %shard_map.89), channel_id=1, source_target_pairs={{0,4},{1,5},{2,6},{3,7},{4,0},{5,1},{6,2},{7,3},{8,12},{9,13},{10,... | collective-permute-start | bytes 245768 | tf_op jit(solution)/shard_map/ppermute | solution.py:205
  15.3 4.4 %collective-permute-start.8 = (bf16[320,128]{1,0:T(8,128)(2,1)S(1)}, bf16[320,128]{1,0:T(8,128)(2,1)S(1)}, u32[]{:S(2)}, u32[]{:S(2)}) collective-permute-start(bf16[320,128]{1,0:T(8,128)(2,1)S(1)} %shard_map.89), channel_id=1, source_target_pairs={{0,2},{1,3},{2,0},{3,1},{4,6},{5,7},{6,4},{7,5},{8,10},{9,11},{10,... | collective-permute-start | bytes 245768 | tf_op jit(solution)/shard_map/ppermute | solution.py:205
  17.3 3.1 %collective-permute-start.10 = (bf16[2048,128]{1,0:T(8,128)(2,1)S(1)}, bf16[2048,128]{1,0:T(8,128)(2,1)S(1)}, u32[]{:S(2)}, u32[]{:S(2)}) collective-permute-start(bf16[2048,128]{1,0:T(8,128)(2,1)S(1)} %pad_maximum_fusion), channel_id=1, source_target_pairs={{0,1},{1,0},{2,3},{3,2},{4,5},{5,4},{6,7},{7,6},{8,9},{9,8},{10,11... | collective-permute-start | bytes 1572872 | tf_op jit(solution)/shard_map/ppermute | solution.py:205
  20.1 1.3 %collective-permute-start.9 = (f32[160,128]{1,0:T(8,128)S(1)}, f32[160,128]{1,0:T(8,128)S(1)}, u32[]{:S(2)}, u32[]{:S(2)}) collective-permute-start(f32[160,128]{1,0:T(8,128)S(1)} %shard_map.91), channel_id=1, source_target_pairs={{0,1},{1,0},{2,3},{3,2},{4,5},{5,4},{6,7},{7,6},{8,9},{9,8},{10,11... | collective-permute-start | bytes 245768 | tf_op jit(solution)/shard_map/ppermute | solution.py:205
  22.4 5.1 %copy-start = (s32[4,64]{1,0:T(4,128)S(1)}, s32[4,64]{1,0:T(4,128)}, u32[]{:S(2)}) copy-start(s32[4,64]{1,0:T(4,128)} %candidates_ref.1) | copy-start | bytes 3076
  22.4 5.4 %collective-permute-start.11 = (f32[4,64]{1,0:T(4,128)S(1)}, f32[4,64]{1,0:T(4,128)S(1)}, u32[]{:S(2)}, u32[]{:S(2)}) collective-permute-start(f32[4,64]{1,0:T(4,128)S(1)} %get-tuple-element.32), channel_id=1, source_target_pairs={{0,8},{1,9},{2,10},{3,11},{4,12},{5,13},{6,14},{7,15},{8,16},{9,17... | collective-permute-start | bytes 3080 | tf_op jit(solution)/shard_map/ppermute | solution.py:202
  23.9 4.5 %collective-permute-start.12 = (f32[4,64]{1,0:T(4,128)S(1)}, f32[4,64]{1,0:T(4,128)S(1)}, u32[]{:S(2)}, u32[]{:S(2)}) collective-permute-start(f32[4,64]{1,0:T(4,128)S(1)} %get-tuple-element.33), channel_id=1, source_target_pairs={{0,16},{1,17},{2,18},{3,19},{4,20},{5,21},{6,22},{7,23},{8,24},{9,... | collective-permute-start | bytes 3080 | tf_op jit(solution)/shard_map/ppermute | solution.py:202
  25.3 3.6 %collective-permute-start.13 = (f32[4,64]{1,0:T(4,128)S(1)}, f32[4,64]{1,0:T(4,128)S(1)}, u32[]{:S(2)}, u32[]{:S(2)}) collective-permute-start(f32[4,64]{1,0:T(4,128)S(1)} %get-tuple-element.34), channel_id=1, source_target_pairs={{0,24},{1,25},{2,26},{3,27},{4,28},{5,29},{6,30},{7,31},{8,0},{9,1... | collective-permute-start | bytes 3080 | tf_op jit(solution)/shard_map/ppermute | solution.py:202
